TPU v7x, 32 devices: a whole 2x2x4 slice. The times are simulated.
32 devices in a mesh: seq: 8 (over z, x), head: 4 (over y, core).
Axes of the slice: x: 2, y: 2, z: 4, core: 2. Of those that a mesh axis runs over, the one named last changes fastest.
Arguments:
- hidden_in: bfloat16 [4, 2048, 1024], P(None, 'seq'), may hold values from -8 to 8
- lengths: int32 [4], replicated, may hold values from 1024 to 2048, as said below
- input_gain: float32 [1024], replicated, may hold values from 0.1 to 1.9
- query_weight: bfloat16 [1024, 1024], P(None, 'head'), may hold values from -0.1875 to 0.1875
- key_weight: bfloat16 [1024, 1024], P(None, 'head'), may hold values from -0.1875 to 0.1875
- value_weight: bfloat16 [1024, 2048], P(None, 'head'), may hold values from -0.1875 to 0.1875
- alpha_weight: bfloat16 [1024, 8], P(None, 'head'), may hold values from -0.1875 to 0.1875
- beta_weight: bfloat16 [1024, 8], P(None, 'head'), may hold values from -1 to 1
- decay_log: float32 [8], P('head'), may hold values from -12 to -3
- decay_bias: float32 [8], P('head'), may hold values from -2 to 1
- query_kernel: bfloat16 [4, 1024], P(None, 'head'), may hold values from -3 to 3
- key_kernel: bfloat16 [4, 1024], P(None, 'head'), may hold values from -3 to 3
- value_kernel: bfloat16 [4, 2048], P(None, 'head'), may hold values from -3 to 3
- gate_weight: bfloat16 [1024, 2048], P(None, 'head'), may hold values from -0.1875 to 0.1875
- output_gain: float32 [256], replicated, may hold values from 0.1 to 1.9
- output_weight: bfloat16 [2048, 1024], P('head'), may hold values from -0.25 to 0.25
- mixed_gain: float32 [1024], P('head'), may hold values from 0.1 to 1.9
- swiglu_gate: bfloat16 [1024, 2816], P(None, 'head'), may hold values from -0.1875 to 0.1875
- swiglu_up: bfloat16 [1024, 2816], P(None, 'head'), may hold values from -0.1875 to 0.1875
- swiglu_down: bfloat16 [2816, 1024], P('head'), may hold values from -0.21875 to 0.21875
- cotangent: bfloat16 [4, 2048, 1024], P(None, 'seq'), may hold values from -6 to 6
Outputs:
- block_out: bfloat16 [4, 2048, 1024], P(None, 'seq', 'head')
- input_grad: float32 [4, 2048, 1024], P(None, 'seq', 'head')
- input_gain_grad: float32 [1024], P('head')
- query_weight_grad: float32 [1024, 1024], P(None, 'head')
- key_weight_grad: float32 [1024, 1024], P(None, 'head')
- value_weight_grad: float32 [1024, 2048], P(None, 'head')
- alpha_weight_grad: float32 [1024, 8], P(None, 'head')
- beta_weight_grad: float32 [1024, 8], P(None, 'head')
- decay_log_grad: float32 [8], P('head')
- decay_bias_grad: float32 [8], P('head')
- query_kernel_grad: float32 [4, 1024], P(None, 'head')
- key_kernel_grad: float32 [4, 1024], P(None, 'head')
- value_kernel_grad: float32 [4, 2048], P(None, 'head')
- gate_weight_grad: float32 [1024, 2048], P(None, 'head')
- output_gain_grad: float32 [256], P('head')
- output_weight_grad: float32 [2048, 1024], P('head')
- mixed_gain_grad: float32 [1024], P('head')
- swiglu_gate_grad: float32 [1024, 2816], P(None, 'head')
- swiglu_up_grad: float32 [1024, 2816], P(None, 'head')
- swiglu_down_grad: float32 [2816, 1024], P('head')
Inputs may be any that keep to these rules, and one draw needn't show every extreme that they name: Each slot's valid positions are its first lengths entries; one slot, drawn from the seed, is full at 2048.
All inputs are finite; a program needn't handle non-finite values.
Results may differ from a plain program's by a relative error of at most 0.015.
The roundings to bfloat16 on the way count: a program that leaves them out, or rounds other values in their place, can miss the bound.
Values may be sent and summed in bfloat16 or wider, within the bound.
A program may use at most 256 MiB of HBM per device.

v0:
```python
import jax
import jax.numpy as jnp
from jax import lax
from jax.sharding import PartitionSpec as P

BLOCK = 64


HIGHEST_PRECISION = lax.Precision.HIGHEST
NORM_EPSILON = 1e-05
UNIT_EPSILON = 1e-06


def shifted(block, axis, distance):
    devices = range(lax.axis_size(axis))
    route = [(i - distance, i) for i in devices if i - distance in devices]
    return lax.ppermute(block, axis, route)


def carried_in(part, axis, combine, identity, reverse):
    count = lax.axis_size(axis)
    place = lax.axis_index(axis)
    ahead = count - 1 - place if reverse else place
    gathered = jax.tree.map(lambda a: lax.all_gather(a, axis), part)
    state = jax.tree.map(lambda a, e: jnp.zeros_like(a) + jnp.asarray(e, a.dtype), part, identity)

    def one(hop, state):
        source = count - 1 - hop if reverse else hop
        return combine(
            state, jax.tree.map(lambda a: lax.dynamic_index_in_dim(a, source, 0, False), gathered)
        )

    return lax.fori_loop(0, ahead, one, state)


def block_terms(queries, key_rows, value_rows, strength, log_decay):
    length_block = queries.shape[-2]
    position = jnp.arange(length_block)
    inclusive = position[:, None] >= position[None, :]
    strictly = position[:, None] > position[None, :]
    cumulated = jnp.cumsum(log_decay, axis=-1)
    difference = cumulated[..., :, None] - cumulated[..., None, :]
    decayed = jnp.where(inclusive, jnp.exp(jnp.where(inclusive, difference, 0.0)), 0.0)
    key_products = jnp.einsum("...td,...jd->...tj", key_rows, key_rows, precision=HIGHEST_PRECISION)
    triangle = jnp.where(strictly, strength[..., :, None] * decayed * key_products, 0.0)
    right_side = jnp.concatenate(
        [strength[..., None] * value_rows, (strength * jnp.exp(cumulated))[..., None] * key_rows],
        axis=-1,
    )
    solved = lax.linalg.triangular_solve(
        triangle, right_side, left_side=True, lower=True, unit_diagonal=True
    )
    channels = value_rows.shape[-1]
    delta_value = solved[..., :channels]
    key_mix = solved[..., channels:]
    scores = decayed * jnp.einsum(
        "...td,...jd->...tj", queries, key_rows, precision=HIGHEST_PRECISION
    )
    query_eff = jnp.exp(cumulated)[..., None] * queries - jnp.einsum(
        "...tj,...jd->...td", scores, key_mix, precision=HIGHEST_PRECISION
    )
    end_weight = jnp.exp(cumulated[..., -1:] - cumulated)[..., None]
    identity = jnp.eye(key_rows.shape[-1], dtype=key_rows.dtype)
    transition = jnp.exp(cumulated[..., -1])[..., None, None] * identity - jnp.einsum(
        "...jd,...je->...de", key_mix * end_weight, key_rows, precision=HIGHEST_PRECISION
    )
    state_bias = jnp.einsum(
        "...jv,...jd->...vd", delta_value * end_weight, key_rows, precision=HIGHEST_PRECISION
    )
    intra_out = jnp.einsum("...tj,...jv->...tv", scores, delta_value, precision=HIGHEST_PRECISION)
    return (intra_out, query_eff, transition, state_bias)


def combine_maps(earlier, later):
    joined_map = jnp.einsum("...de,...ef->...df", earlier[0], later[0], precision=HIGHEST_PRECISION)
    joined_shift = (
        jnp.einsum("...vd,...df->...vf", earlier[1], later[0], precision=HIGHEST_PRECISION)
        + later[1]
    )
    return (joined_map, joined_shift)


def block_pieces(queries, key_rows, value_rows, strength, log_decay):
    intra_out, query_eff, transition, state_bias = block_terms(
        queries, key_rows, value_rows, strength, log_decay
    )
    moved_map = jnp.moveaxis(transition, 1, 0)
    moved_shift = jnp.moveaxis(state_bias, 1, 0)
    identity = jnp.broadcast_to(
        jnp.eye(moved_map.shape[-1], dtype=moved_map.dtype), moved_map.shape[1:]
    )
    zero_shift = jnp.zeros(moved_shift.shape[1:], moved_shift.dtype)

    def compose(carried, element):
        return (combine_maps(carried, element), carried)

    segment_map, starts = lax.scan(compose, (identity, zero_shift), (moved_map, moved_shift))
    return (
        intra_out,
        query_eff,
        jnp.moveaxis(starts[0], 0, 1),
        jnp.moveaxis(starts[1], 0, 1),
        segment_map[0],
        segment_map[1],
    )


def emit(state_in, intra_out, query_eff, start_maps, start_shifts):
    block_state = (
        jnp.einsum("shvd,schdf->schvf", state_in, start_maps, precision=HIGHEST_PRECISION)
        + start_shifts
    )
    return intra_out + jnp.einsum(
        "schtd,schvd->schtv", query_eff, block_state, precision=HIGHEST_PRECISION
    )


def to_blocks(tensor, block_count):
    leading = tensor.shape[:2]
    shaped = tensor.reshape((leading[0], block_count, leading[1] // block_count) + tensor.shape[2:])
    return jnp.swapaxes(shaped, 2, 3)


def from_blocks(tensor):
    swapped = jnp.swapaxes(tensor, 2, 3)
    return swapped.reshape(
        (swapped.shape[0], swapped.shape[1] * swapped.shape[2]) + swapped.shape[3:]
    )


def per_device(
    hidden_in,
    lengths,
    input_gain,
    query_weight,
    key_weight,
    value_weight,
    alpha_weight,
    beta_weight,
    decay_log,
    decay_bias,
    query_kernel,
    key_kernel,
    value_kernel,
    gate_weight,
    output_gain,
    output_weight,
    mixed_gain,
    swiglu_gate,
    swiglu_up,
    swiglu_down,
    cotangent,
):
    slot_count, segment, width = hidden_in.shape
    total_rows = slot_count * segment
    head_count = decay_log.shape[0]
    key_dim = query_kernel.shape[1] // head_count
    value_dim = value_kernel.shape[1] // head_count
    taps = query_kernel.shape[0]
    block_count = segment // BLOCK
    split_key = head_count * key_dim
    head_parts = lax.axis_size("head")
    shard_width = width // head_parts
    head_start = lax.axis_index("head") * shard_width
    position = lax.axis_index("seq") * segment + jnp.arange(segment)
    mask = (position[None, :] < lengths[:, None]).astype(jnp.float32)[:, :, None]
    x_full = hidden_in.astype(jnp.float32)
    inv_first = lax.rsqrt(jnp.mean(x_full * x_full, axis=-1, keepdims=True) + NORM_EPSILON)
    normed_first = (x_full * inv_first * input_gain).astype(jnp.bfloat16).reshape(total_rows, width)
    x_shard = lax.dynamic_slice_in_dim(x_full, head_start, shard_width, 2)

    def project(weight):
        return jnp.dot(normed_first, weight, preferred_element_type=jnp.float32)

    pre_all = jnp.concatenate(
        [project(query_weight), project(key_weight), project(value_weight)], axis=1
    )
    pre_all = pre_all.astype(jnp.bfloat16).reshape(slot_count, segment, -1)
    gate_pre = project(gate_weight)
    alpha_pre = project(alpha_weight).reshape(slot_count, segment, head_count)
    beta_pre = project(beta_weight).reshape(slot_count, segment, head_count)
    rim = shifted(pre_all[:, segment - taps + 1 :, :], "seq", 1)
    extended = jnp.concatenate([rim, pre_all], axis=1).astype(jnp.float32)
    kernel = jnp.concatenate([query_kernel, key_kernel, value_kernel], axis=1).astype(jnp.float32)

    def prepare(extended_in, kernel_in, alpha_in, beta_in, decay_rate, decay_shift):
        length_out = extended_in.shape[1] - taps + 1
        convolved = kernel_in[0] * extended_in[:, 0:length_out]
        for offset in range(1, taps):
            convolved = convolved + kernel_in[offset] * extended_in[:, offset : offset + length_out]
        active = convolved * jax.nn.sigmoid(convolved)
        query_part = active[..., :split_key].reshape(slot_count, segment, head_count, key_dim)
        key_part = active[..., split_key : 2 * split_key].reshape(
            slot_count, segment, head_count, key_dim
        )
        value_part = active[..., 2 * split_key :].reshape(
            slot_count, segment, head_count, value_dim
        )
        query_unit = (
            query_part
            * lax.rsqrt(jnp.sum(query_part * query_part, axis=-1, keepdims=True) + UNIT_EPSILON)
            * key_dim ** (-0.5)
        )
        key_unit = key_part * lax.rsqrt(
            jnp.sum(key_part * key_part, axis=-1, keepdims=True) + UNIT_EPSILON
        )
        strength = jax.nn.sigmoid(beta_in)
        log_decay = -jnp.exp(decay_rate) * jax.nn.softplus(alpha_in + decay_shift)
        return (query_unit, key_unit, value_part, strength, log_decay)

    prepared, prepare_back = jax.vjp(
        prepare, extended, kernel, alpha_pre, beta_pre, decay_log, decay_bias
    )
    rounded = lax.optimization_barrier(
        (
            prepared[0].astype(jnp.bfloat16),
            prepared[1].astype(jnp.bfloat16),
            prepared[2].astype(jnp.bfloat16),
        )
    )
    blocked = (
        to_blocks(rounded[0].astype(jnp.float32), block_count),
        to_blocks(rounded[1].astype(jnp.float32), block_count),
        to_blocks(rounded[2].astype(jnp.float32), block_count),
        to_blocks(prepared[3], block_count),
        to_blocks(prepared[4], block_count),
    )
    pieces, pieces_back = jax.vjp(block_pieces, *blocked)
    identity_maps = jnp.broadcast_to(jnp.eye(key_dim, dtype=jnp.float32), pieces[4].shape)
    zero_shifts = jnp.zeros(pieces[5].shape, jnp.float32)
    prior = carried_in(
        (pieces[4], pieces[5]), "seq", combine_maps, (identity_maps, zero_shifts), False
    )
    state_in = prior[1]
    mixer_blocks, emit_back = jax.vjp(emit, state_in, pieces[0], pieces[1], pieces[2], pieces[3])
    mixer_out = from_blocks(mixer_blocks)

    def gate_output(mixer_in, gate_in, gain_in):
        scaled = (
            mixer_in
            * lax.rsqrt(jnp.mean(mixer_in * mixer_in, axis=-1, keepdims=True) + NORM_EPSILON)
            * gain_in
        )
        gate_heads = gate_in.reshape(mixer_in.shape)
        return (scaled * gate_heads * jax.nn.sigmoid(gate_heads)).reshape(total_rows, -1)

    gated, gated_back = jax.vjp(gate_output, mixer_out, gate_pre, output_gain)
    gated_low = gated.astype(jnp.bfloat16)
    mixer_part = jnp.dot(gated_low, output_weight, preferred_element_type=jnp.float32).reshape(
        slot_count, segment, width
    )
    attention_shard = lax.psum_scatter(mixer_part, "head", scatter_dimension=2, tiled=True)
    residual = x_shard + mask * attention_shard
    square_sum = lax.psum(jnp.sum(residual * residual, axis=-1, keepdims=True), "head")
    inv_second = lax.rsqrt(square_sum / width + NORM_EPSILON)
    normed_shard = (residual * inv_second * mixed_gain).astype(jnp.bfloat16)
    normed_second = lax.all_gather(normed_shard, "head", axis=2, tiled=True).reshape(
        total_rows, width
    )
    gate_values = jnp.dot(normed_second, swiglu_gate, preferred_element_type=jnp.float32)
    upward_values = jnp.dot(normed_second, swiglu_up, preferred_element_type=jnp.float32)
    sigmoid_gate = jax.nn.sigmoid(gate_values)
    silu_gate = gate_values * sigmoid_gate
    activation = (silu_gate * upward_values).astype(jnp.bfloat16)
    swiglu_part = jnp.dot(activation, swiglu_down, preferred_element_type=jnp.float32).reshape(
        slot_count, segment, width
    )
    swiglu_shard = lax.psum_scatter(swiglu_part, "head", scatter_dimension=2, tiled=True)
    block_out = (residual + mask * swiglu_shard).astype(jnp.bfloat16)
    out_grad = jnp.where(mask > 0, cotangent, jnp.zeros_like(cotangent)).reshape(total_rows, width)
    swiglu_down_grad = jnp.dot(activation.T, out_grad, preferred_element_type=jnp.float32)
    activation_grad = jnp.dot(out_grad, swiglu_down.T, preferred_element_type=jnp.float32)
    upward_grad = (activation_grad * silu_gate).astype(jnp.bfloat16)
    gate_grad = (
        activation_grad * upward_values * sigmoid_gate * (1.0 + gate_values * (1.0 - sigmoid_gate))
    ).astype(jnp.bfloat16)
    swiglu_up_grad = jnp.dot(normed_second.T, upward_grad, preferred_element_type=jnp.float32)
    swiglu_gate_grad = jnp.dot(normed_second.T, gate_grad, preferred_element_type=jnp.float32)
    normed_part = (
        jnp.dot(upward_grad, swiglu_up.T, preferred_element_type=jnp.float32)
        + jnp.dot(gate_grad, swiglu_gate.T, preferred_element_type=jnp.float32)
    ).reshape(slot_count, segment, width)
    normed_grad = lax.psum_scatter(normed_part, "head", scatter_dimension=2, tiled=True)
    mixed_gain_grad = jnp.sum(normed_grad * residual * inv_second, axis=(0, 1))
    weighted_second = normed_grad * mixed_gain
    second_stat = lax.psum(jnp.sum(weighted_second * residual, axis=-1, keepdims=True), "head")
    out_shard = lax.dynamic_slice_in_dim(cotangent, head_start, shard_width, 2).astype(jnp.float32)
    residual_grad = out_shard + inv_second * (
        weighted_second - residual * inv_second * inv_second * second_stat / width
    )
    mixer_grad_low = (mask * residual_grad).astype(jnp.bfloat16)
    mixer_grad = lax.all_gather(mixer_grad_low, "head", axis=2, tiled=True).reshape(
        total_rows, width
    )
    output_weight_grad = jnp.dot(gated_low.T, mixer_grad, preferred_element_type=jnp.float32)
    gated_grad = jnp.dot(mixer_grad, output_weight.T, preferred_element_type=jnp.float32)
    mixer_out_grad, gate_pre_grad, output_gain_part = gated_back(gated_grad)
    emit_grads = emit_back(to_blocks(mixer_out_grad, block_count))
    flipped = jnp.swapaxes(pieces[4], -1, -2)
    later = carried_in(
        (flipped, emit_grads[0]), "seq", combine_maps, (identity_maps, zero_shifts), True
    )
    state_out_grad = later[1]
    map_grad = jnp.einsum("shvd,shvf->shdf", state_in, state_out_grad, precision=HIGHEST_PRECISION)
    piece_grads = pieces_back(
        (emit_grads[1], emit_grads[2], emit_grads[3], emit_grads[4], map_grad, state_out_grad)
    )
    prep_grads = prepare_back(
        (
            from_blocks(piece_grads[0]),
            from_blocks(piece_grads[1]),
            from_blocks(piece_grads[2]),
            from_blocks(piece_grads[3]),
            from_blocks(piece_grads[4]),
        )
    )
    extended_grad = prep_grads[0]
    rim_back = shifted(extended_grad[:, : taps - 1, :], "seq", -1)
    pre_grad = extended_grad[:, taps - 1 :, :]
    pre_grad = jnp.concatenate(
        [pre_grad[:, : segment - taps + 1, :], pre_grad[:, segment - taps + 1 :, :] + rim_back],
        axis=1,
    )
    pre_low = pre_grad.reshape(total_rows, -1).astype(jnp.bfloat16)
    query_pre_grad = pre_low[:, :split_key]
    key_pre_grad = pre_low[:, split_key : 2 * split_key]
    value_pre_grad = pre_low[:, 2 * split_key :]
    gate_low = gate_pre_grad.astype(jnp.bfloat16)
    alpha_low = prep_grads[2].reshape(total_rows, head_count).astype(jnp.bfloat16)
    beta_low = prep_grads[3].reshape(total_rows, head_count).astype(jnp.bfloat16)
    kernel_grad = prep_grads[1]

    def weight_grad(grad_low):
        return jnp.dot(normed_first.T, grad_low, preferred_element_type=jnp.float32)

    def input_part(grad_low, weight):
        return jnp.dot(grad_low, weight.T, preferred_element_type=jnp.float32)

    first_part = (
        input_part(query_pre_grad, query_weight)
        + input_part(key_pre_grad, key_weight)
        + input_part(value_pre_grad, value_weight)
        + input_part(gate_low, gate_weight)
        + input_part(alpha_low, alpha_weight)
        + input_part(beta_low, beta_weight)
    )
    first_part = first_part.reshape(slot_count, segment, width)
    first_sum, gain_sum = lax.psum((first_part, output_gain_part), "head")
    weighted_first = first_sum * input_gain
    first_stat = jnp.sum(weighted_first * x_full, axis=-1, keepdims=True)
    full_input = inv_first * (weighted_first - x_full * inv_first * inv_first * first_stat / width)
    input_grad = residual_grad + lax.dynamic_slice_in_dim(full_input, head_start, shard_width, 2)
    gain_full = jnp.sum(first_sum * x_full * inv_first, axis=(0, 1))
    input_gain_grad = lax.dynamic_slice_in_dim(gain_full, head_start, shard_width, 0)
    value_share = value_dim // head_parts
    output_gain_grad = lax.dynamic_slice_in_dim(
        gain_sum, lax.axis_index("head") * value_share, value_share, 0
    )
    summed = lax.psum(
        (
            input_gain_grad,
            weight_grad(query_pre_grad),
            weight_grad(key_pre_grad),
            weight_grad(value_pre_grad),
            weight_grad(alpha_low),
            weight_grad(beta_low),
            prep_grads[4],
            prep_grads[5],
            kernel_grad[:, :split_key],
            kernel_grad[:, split_key : 2 * split_key],
            kernel_grad[:, 2 * split_key :],
            weight_grad(gate_low),
            output_gain_grad,
            output_weight_grad,
            mixed_gain_grad,
            swiglu_gate_grad,
            swiglu_up_grad,
            swiglu_down_grad,
        ),
        "seq",
    )
    return (block_out, input_grad) + tuple(summed)


def solution(mesh):
    placed = (
        P(None, "seq", None),
        P(),
        P(),
        P(None, "head"),
        P(None, "head"),
        P(None, "head"),
        P(None, "head"),
        P(None, "head"),
        P("head"),
        P("head"),
        P(None, "head"),
        P(None, "head"),
        P(None, "head"),
        P(None, "head"),
        P(),
        P("head", None),
        P("head"),
        P(None, "head"),
        P(None, "head"),
        P("head", None),
        P(None, "seq", None),
    )
    return jax.shard_map(
        per_device,
        mesh=mesh,
        in_specs=placed,
        out_specs=(
            P(None, "seq", "head"),
            P(None, "seq", "head"),
            P("head"),
            P(None, "head"),
            P(None, "head"),
            P(None, "head"),
            P(None, "head"),
            P(None, "head"),
            P("head"),
            P("head"),
            P(None, "head"),
            P(None, "head"),
            P(None, "head"),
            P(None, "head"),
            P("head"),
            P("head", None),
            P("head"),
            P(None, "head"),
            P(None, "head"),
            P("head", None),
        ),
        check_vma=False,
    )
```

profile of v0, /device:TPU:0, one launch (start us, length us, event | category | flops | bytes accessed | tf_op | source)
XLA Modules:
  0.0 1842.5 jit_solution(3707015381279737560)
XLA Ops:
  24.0 5.7 collective-permute-start
  34.8 7.5 reduce_window_sum.22
  68.5 3.9 fusion.38
  103.3 159.2 %custom-call.7 = f32[4,4,2,1,64,64]{4,5,3,2,1,0:T(8,128)} custom-call(f32[4,4,2,1,64,64]{5,4,3,2,1,0:T(8,128)} %add_bitcast_fusion.1), custom_call_target="InvertDiagBlocksLowerTriangular" | custom-call | tf_op jit(solution)/shard_map/jvp()/triangular_solve | solution.py:50
  262.5 5.4 fusion.51
  267.9 5.6 convolution_bitcast_fusion.6
  280.5 44.1 %while.66 = (s32[]{:T(128)}, f32[4,2,128,128]{2,3,1,0:T(8,128)}, f32[4,2,256,128]{2,3,1,0:T(8,128)S(1)}, f32[4,4,2,128,128]{3,4,2,1,0:T(8,128)}, f32[4,4,2,256,1...) while((s32[]{:T(128)}, f32[4,2,128,128]{2,3,1,0:T(8,128)}, ...), condition=%wide.region_5.6_spmd.clone, body=%wide.region_4.5_spmd.clone.sunk | while | flops 604766208 | bytes 15728772 | solution.py:97
  332.2 4.2 convolution_subtract_fusion
  339.8 60.2 %all-gather.15.cloned.1.call-done = f32[32,2,128,128]{3,2,1,0:T(8,128)} async-done(((f32[4,2,128,128]{3,2,1,0:T(8,128)}), f32[32,2,128,128]{3,2,1,0:T(8,128)}) %all-gather.15.cloned.1.call-update) | async-done | bytes 4194320 | tf_op jit(solution)/shard_map/all_gather | solution.py:24
  400.0 125.9 %all-gather.17.cloned.1.call-done = f32[32,2,256,128]{3,2,1,0:T(8,128)} async-done(((f32[4,2,256,128]{3,2,1,0:T(8,128)}), f32[32,2,256,128]{3,2,1,0:T(8,128)}) %all-gather.17.cloned.1.call-update) | async-done | bytes 8388624 | tf_op jit(solution)/shard_map/all_gather | solution.py:24
  526.1 6.7 bitcast_add_fusion
  537.8 5.4 multiply_convert_fusion.4
  544.5 4.8 fusion.137
  549.5 4.1 convert_element_type.106
  554.2 74.0 %reduce-scatter.4.cloned.1.call-done = f32[4,256,256]{2,1,0:T(8,128)} async-done(((f32[4,256,1024]{2,1,0:T(8,128)}), f32[4,256,256]{2,1,0:T(8,128)}) %reduce-scatter.4.cloned.1.call-update) | async-done | bytes 1048592 | tf_op jit(solution)/shard_map/reduce_scatter | solution.py:252
  630.7 6.4 psum.154
  647.2 17.1 all-gather.11.cloned.1.call-done
  668.2 4.0 multiply_convert_fusion.1
  674.0 3.9 convolution_add_fusion.1
  679.3 5.3 fusion.268
  684.7 38.0 %reduce-scatter.8.cloned.1.call-done = f32[4,256,256]{2,1,0:T(8,128)} async-done(((f32[4,256,1024]{2,1,0:T(8,128)}), f32[4,256,256]{2,1,0:T(8,128)}) %reduce-scatter.8.cloned.1.call-update) | async-done | bytes 1048592 | tf_op jit(solution)/shard_map/reduce_scatter | solution.py:283
  724.9 5.7 psum.155
  730.7 38.9 %reduce-scatter.6.cloned.1.call-done = f32[4,256,256]{2,1,0:T(8,128)} async-done(((f32[4,256,1024]{2,1,0:T(8,128)}), f32[4,256,256]{2,1,0:T(8,128)}) %reduce-scatter.6.cloned.1.call-update) | async-done | bytes 1048592 | tf_op jit(solution)/shard_map/reduce_scatter | solution.py:268
  773.3 22.2 %all-gather.13.cloned.1.call-done = bf16[4,256,1024]{2,1,0:T(8,128)(2,1)} async-done(((bf16[4,256,256]{2,1,0:T(8,128)(2,1)}), bf16[4,256,1024]{2,1,0:T(8,128)(2,1)}) %all-gather.13.cloned.1.call-update) | async-done | bytes 2097168 | tf_op jit(solution)/shard_map/all_gather | solution.py:292
  795.5 7.4 multiply_reduce_fusion.7
  805.6 7.4 fusion.70
  814.9 4.8 fusion.111
  836.2 4.5 fusion.125
  864.2 5.0 fusion.272
  869.3 8.1 fusion.89
  877.3 119.5 %all-gather.21.cloned.1.call-done = f32[32,2,256,128]{3,2,1,0:T(8,128)} async-done(((f32[4,2,256,128]{3,2,1,0:T(8,128)}), f32[32,2,256,128]{3,2,1,0:T(8,128)}) %all-gather.21.cloned.1.call-update) | async-done | bytes 8388624 | tf_op jit(solution)/shard_map/all_gather | solution.py:24
  996.9 27.1 %while.64 = (s32[]{:T(128)}, f32[4,2,256,128]{2,3,1,0:T(8,128)S(1)}, s32[]{:T(128)}, f32[8,4,2,128,128]{4,3,2,1,0:T(8,128)}, f32[8,4,2,256,128]{4,3,2,1,0:T(8,12...) while((s32[]{:T(128)}, f32[4,2,256,128]{2,3,1,0:T(8,128)S(1)}, s32[]{:T(128)}, ...), condition=%wide.region_18.19_spmd, body=%wide.region_17.18_spmd.sunk | while | flops 402915328 | bytes 9961627 | solution.py:33
  1031.2 56.5 %while.65 = (s32[]{:T(128)}, f32[4,2,128,128]{2,3,1,0:T(8,128)}, f32[4,2,256,128]{2,3,1,0:T(8,128)S(1)}, f32[4,4,2,128,128]{4,3,2,1,0:T(8,128)}, f32[4,4,2,256,1...) while((s32[]{:T(128)}, f32[4,2,128,128]{2,3,1,0:T(8,128)}, ...), condition=%wide.region_20.21_spmd, body=%wide.region_19.20_spmd.sunk | while | flops 1208483840 | bytes 19925144 | solution.py:97
  1087.8 5.1 multiply_reduce_fusion.8
  1100.2 4.0 fusion.56
  1112.5 4.8 fusion.101
  1126.4 7.1 reduce_window_sum.23
  1150.1 4.0 reshape_reshape.3
  1154.1 3.8 add_add_fusion.3
  1160.3 4.7 multiply_reduce_fusion.3
  1165.0 6.4 broadcast_multiply_fusion
  1178.7 8.3 pad_add_fusion
  1200.1 5.4 fusion.276
  1217.6 7.0 psum.169
  1225.6 59.3 %all-reduce.20.cloned.1.call-done = f32[4,256,1024]{2,1,0:T(8,128)} async-done(((f32[4,256,1024]{2,1,0:T(8,128)}), f32[4,256,1024]{2,1,0:T(8,128)}) %all-reduce.20.cloned.1.call-update) | async-done | bytes 4194320 | tf_op jit(solution)/shard_map/psum | solution.py:348
  1284.9 6.5 multiply_reduce_fusion.4
  1291.4 40.1 %all-reduce.15 = (f32[256]{0:T(256)}, f32[1024,2]{0,1:T(2,128)}, f32[1024,2]{0,1:T(2,128)}, f32[2]{0:T(128)}, f32[2]{0:T(128)}, /*index=5*/f32[4,256]{1,0:T(4,12...) all-reduce(f32[256]{0:T(256)S(1)} %dynamic_slice.97, ...), channel_id=1, replica_groups=mesh['seq'=8,'head'=4] {'seq'}, use_global_device_ids=true, to_apply=%region_37.38 | all-reduce | flops 8772 | bytes 70176 | tf_op jit(solution)/shard_map/psum | solution.py:359
  1334.4 483.4 %all-reduce.22.cloned.1.call-done = (f32[1024,256]{1,0:T(8,128)}, f32[1024,256]{1,0:T(8,128)}, f32[1024,512]{1,0:T(8,128)}, f32[1024,512]{1,0:T(8,128)}, f32[512...) async-done(((f32[1024,256]{1,0:T(8,128)}, f32[1024,256]{1,0:T(8,128)}, f32[1024,512]{1,0:T(8,128)}, f32[1024,512]{1,0:T(8,128)}, ...) | async-done | bytes 17039376 | tf_op jit(solution)/shard_map/psum | solution.py:359
  (659 shorter events, 404.8 us)
Async XLA Ops:
  7.2 660.9 %copy-start = (bf16[1024,704]{0,1:T(8,128)(2,1)S(1)}, bf16[1024,704]{0,1:T(8,128)(2,1)}, u32[]{:S(2)}) copy-start(bf16[1024,704]{0,1:T(8,128)(2,1)} %param.46) | copy-start | bytes 4325380
  7.2 392.8 %all-gather.15.cloned.1.call-start = ((), (), s32[]{:S(2)}) async-start(), calls=%async_computation.9 | async-start | bytes 4718592 | tf_op jit(solution)/shard_map/all_gather | solution.py:24
  12.1 33.6 %copy-start.24 = (bf16[4,256,1024]{2,1,0:T(8,128)(2,1)}, bf16[4,256,1024]{2,1,0:T(8,128)(2,1)S(1)}, u32[]{:S(2)}) copy-start(bf16[4,256,1024]{2,1,0:T(8,128)(2,1)S(1)} %get-tuple-element.717) | copy-start | bytes 6291460
  20.5 10.4 copy-start.164
  20.5 10.4 copy-start.145
  20.5 10.4 copy-start.156
  24.0 42.5 %collective-permute-start = (bf16[4,3,1024]{2,1,0:T(4,128)(2,1)}, bf16[4,3,1024]{2,1,0:T(4,128)(2,1)}, u32[]{:S(2)}, u32[]{:S(2)}) collective-permute-start(bf16[4,3,1024]{2,1,0:T(4,128)(2,1)} %pad_maximum_fusion.1), channel_id=1, source_target_pairs={{0,4},{4,8},{8,12},{12,16},{16,20},{20,24},{24,28},{1,5},{5,9},{9,... | collective-permute-start | bytes 73736 | tf_op jit(solution)/shard_map/ppermute | solution.py:17
  47.7 18.9 %copy-start.62 = (bf16[4,256,256]{2,1,0:T(8,128)(2,1)S(1)}, bf16[4,256,256]{2,1,0:T(8,128)(2,1)}, u32[]{:S(2)}) copy-start(bf16[4,256,256]{2,1,0:T(8,128)(2,1)} %copy.588) | copy-start | bytes 1572868
  47.7 18.9 %copy-start.63 = (bf16[4,256,256]{2,1,0:T(8,128)(2,1)S(1)}, bf16[4,256,256]{2,1,0:T(8,128)(2,1)}, u32[]{:S(2)}) copy-start(bf16[4,256,256]{2,1,0:T(8,128)(2,1)} %copy.587) | copy-start | bytes 1572868
  98.3 175.3 %copy-start.10 = (bf16[4,256,2,128]{3,1,2,0:T(8,128)(2,1)}, bf16[4,256,2,128]{3,1,2,0:T(8,128)(2,1)S(1)}, u32[]{:S(2)}) copy-start(bf16[4,256,2,128]{3,1,2,0:T(8,128)(2,1)S(1)} %get-tuple-element.391) | copy-start | bytes 1572868
  326.7 199.2 %all-gather.17.cloned.1.call-start = ((), (), s32[]{:S(2)}) async-start(), calls=%async_computation.10 | async-start | bytes 9437184 | tf_op jit(solution)/shard_map/all_gather | solution.py:24
  328.1 300.1 %reduce-scatter.4.cloned.1.call-start = ((), (), s32[]{:S(2)}) async-start(), calls=%async_computation.3 | async-start | bytes 5242880 | tf_op jit(solution)/shard_map/reduce_scatter | solution.py:252
  526.0 343.2 %copy-start.7 = (f32[4,2,256,128]{2,3,1,0:T(8,128)}, f32[4,2,256,128]{2,3,1,0:T(8,128)S(1)}, u32[]{:S(2)}) copy-start(f32[4,2,256,128]{2,3,1,0:T(8,128)S(1)} %get-tuple-element.396) | copy-start | bytes 3145732
  549.4 114.9 %all-gather.11.cloned.1.call-start = ((), (), s32[]{:S(2)}) async-start(), calls=%async_computation.4 | async-start | bytes 2621440 | tf_op jit(solution)/shard_map/all_gather | solution.py:257
  630.7 138.8 %copy-start.31 = (f32[4,256,256]{2,1,0:T(8,128)}, f32[4,256,256]{2,1,0:T(8,128)S(1)}, u32[]{:S(2)}) copy-start(f32[4,256,256]{2,1,0:T(8,128)S(1)} %get-tuple-element.695) | copy-start | bytes 3145732
  640.2 82.5 %reduce-scatter.8.cloned.1.call-start = ((), (), s32[]{:S(2)}) async-start(), calls=%async_computation.6 | async-start | bytes 5242880 | tf_op jit(solution)/shard_map/reduce_scatter | solution.py:283
  678.0 91.6 %reduce-scatter.6.cloned.1.call-start = ((), (), s32[]{:S(2)}) async-start(), calls=%async_computation.5 | async-start | bytes 5242880 | tf_op jit(solution)/shard_map/reduce_scatter | solution.py:268
  684.6 38.0 %copy-start.109 = (f32[4,256]{1,0:T(4,128)S(1)}, f32[4,256]{1,0:T(4,128)}, u32[]{:S(2)}) copy-start(f32[4,256]{1,0:T(4,128)} %copy-done.108) | copy-start | bytes 12292
  684.6 38.0 %copy-start.142 = (f32[256]{0:T(256)S(1)}, f32[256]{0:T(256)}, u32[]{:S(2)}) copy-start(f32[256]{0:T(256)} %param.45) | copy-start | bytes 3076
  684.6 84.9 %copy-start.128 = (f32[4,256]{1,0:T(4,128)S(1)}, f32[4,256]{1,0:T(4,128)}, u32[]{:S(2)}) copy-start(f32[4,256]{1,0:T(4,128)} %get-tuple-element.733) | copy-start | bytes 12292
  684.7 110.8 %all-gather.13.cloned.1.call-start = ((), (), s32[]{:S(2)}) async-start(), calls=%async_computation.7 | async-start | bytes 2621440 | tf_op jit(solution)/shard_map/all_gather | solution.py:292
  722.7 46.9 %copy-start.46 = (f32[4,256,256]{2,1,0:T(8,128)S(1)}, f32[4,256,256]{2,1,0:T(8,128)}, u32[]{:S(2)}) copy-start(f32[4,256,256]{2,1,0:T(8,128)} %reduce-scatter.8.cloned.1.call-done) | copy-start | bytes 3145732
  730.7 41.8 %copy-start.126 = (f32[4,256]{1,0:T(4,128)}, f32[4,256]{1,0:T(4,128)S(1)}, u32[]{:S(2)}) copy-start(f32[4,256]{1,0:T(4,128)S(1)} %psum.155) | copy-start | bytes 12292
  730.7 64.8 %copy-start.139 = (f32[4,256,2]{1,2,0:T(2,128)S(1)}, f32[4,256,2]{1,2,0:T(2,128)}, u32[]{:S(2)}) copy-start(f32[4,256,2]{1,2,0:T(2,128)} %copy-done.138) | copy-start | bytes 24580
  730.7 64.8 %copy-start.153 = (f32[256]{0:T(256)S(1)}, f32[256]{0:T(256)}, u32[]{:S(2)}) copy-start(f32[256]{0:T(256)} %param.43) | copy-start | bytes 3076
  772.5 104.8 %all-gather.19.cloned.1.call-start = ((), (), s32[]{:S(2)}) async-start(), calls=%async_computation.11 | async-start | bytes 4718592 | tf_op jit(solution)/shard_map/all_gather | solution.py:24
  773.3 223.6 %all-gather.21.cloned.1.call-start = ((), (), s32[]{:S(2)}) async-start(), calls=%async_computation.12 | async-start | bytes 9437184 | tf_op jit(solution)/shard_map/all_gather | solution.py:24
  805.6 9.3 copy-start.35
  819.7 465.2 %all-reduce.20.cloned.1.call-start = ((), (), s32[]{:S(2)}) async-start(), calls=%async_computation.8 | async-start | bytes 8388608 | tf_op jit(solution)/shard_map/psum | solution.py:348
  840.7 8.9 copy-start.39
  1107.1 10.2 copy-start.37
  1124.5 9.1 copy-start.113
  1124.5 9.1 copy-start.148
  1124.5 9.1 copy-start.150
  1124.5 9.1 copy-start.152
  1124.5 9.3 copy-start.146
  1176.0 11.6 collective-permute-start.1
  1178.6 8.9 copy-start.17
  1178.6 8.9 copy-start.19
  1199.9 618.0 %all-reduce.22.cloned.1.call-start = ((), (), s32[]{:S(2)}) async-start(), calls=%async_computation.13 | async-start | bytes 34078720 | tf_op jit(solution)/shard_map/psum | solution.py:359
  1224.7 60.1 %copy-start.125 = (f32[4,256]{1,0:T(4,128)S(1)}, f32[4,256]{1,0:T(4,128)}, u32[]{:S(2)}) copy-start(f32[4,256]{1,0:T(4,128)} %copy-done.124) | copy-start | bytes 12292
  1224.7 60.1 %copy-start.141 = (f32[1024]{0:T(1024)S(1)}, f32[1024]{0:T(1024)}, u32[]{:S(2)}) copy-start(f32[1024]{0:T(1024)} %param.31) | copy-start | bytes 12292
  1225.5 65.9 %copy-start.149 = (f32[256]{0:T(256)S(1)}, f32[256]{0:T(256)}, u32[]{:S(2)}) copy-start(f32[256]{0:T(256)} %get-tuple-element.610) | copy-start | bytes 3076
  1225.5 106.0 %copy-start.32 = (f32[4,256,256]{2,1,0:T(8,128)S(1)}, f32[4,256,256]{2,1,0:T(8,128)}, u32[]{:S(2)}) copy-start(f32[4,256,256]{2,1,0:T(8,128)} %copy-done.31) | copy-start | bytes 3145732
  1225.6 106.0 %copy-start.47 = (f32[4,256,256]{2,1,0:T(8,128)S(1)}, f32[4,256,256]{2,1,0:T(8,128)}, u32[]{:S(2)}) copy-start(f32[4,256,256]{2,1,0:T(8,128)} %reduce-scatter.8.cloned.1.call-done) | copy-start | bytes 3145732
  1225.6 106.0 %copy-start.110 = (f32[4,256]{1,0:T(4,128)S(1)}, f32[4,256]{1,0:T(4,128)}, u32[]{:S(2)}) copy-start(f32[4,256]{1,0:T(4,128)} %copy-done.108) | copy-start | bytes 12292
  1225.6 106.0 %copy-start.127 = (f32[4,256]{1,0:T(4,128)S(1)}, f32[4,256]{1,0:T(4,128)}, u32[]{:S(2)}) copy-start(f32[4,256]{1,0:T(4,128)} %copy-done.126) | copy-start | bytes 12292
  1225.6 106.0 %copy-start.143 = (f32[256]{0:T(256)S(1)}, f32[256]{0:T(256)}, u32[]{:S(2)}) copy-start(f32[256]{0:T(256)} %param.45) | copy-start | bytes 3076
  (138 other events, 453.5 us)
Sparse Core Ops, SparseCore 0:
  326.8 73.1 all-gather.14
  402.7 123.1 all-gather.16
  549.5 78.6 reduce-scatter.3
  640.3 23.9 all-gather.10
  678.1 44.4 reduce-scatter.7
  725.0 44.4 reduce-scatter.5
  772.6 22.8 all-gather.12
  797.8 73.3 all-gather.18
  873.6 123.1 all-gather.20
  1200.0 84.7 all-reduce.19
  1292.4 525.3 all-reduce.21
where the time goes:
time: 1850 us; the launch traced here: 1840 us
  waiting for transfers between devices  1040 us (56%)
  other arithmetic  273 us (15%)
  matrix products  262 us (14%)
  local copies, waits for them, and re-layouts  183 us (10%)
  blocking collectives  59.3 us (3%)
    psum x1, waiting for transfers between devices, per_device(): lax.psum((input_gain_grad, weight_grad(query_pre_grad), weight_grad(key_p...  483 us
    all_gather x4, waiting for transfers between devices, carried_in(): gathered = jax.tree.map(lambda a: lax.all_gather(a, axis), part)  306 us
    another operation x3, other arithmetic, block_terms(): lax.linalg.triangular_solve(triangle, right_side, left_side=True, lower=T...  161 us
    reduce_scatter x1, waiting for transfers between devices, per_device(): lax.psum_scatter(mixer_part, 'head', scatter_dimension=2, tiled=True)  74 us
    psum x1, waiting for transfers between devices, per_device(): first_sum, gain_sum = lax.psum((first_part, output_gain_part), 'head')  59.3 us
    unnamed x358, local copies, waits for them, and re-layouts  45.7 us
    dot_general x19, matrix products, combine_maps(): jnp.einsum('...vd,...df->...vf', earlier[1], later[0], precision=HIGHEST_...  42.1 us
    psum x1, blocking collectives, per_device(): lax.psum((input_gain_grad, weight_grad(query_pre_grad), weight_grad(key_p...  40.1 us
  transfers between devices with their start and end apart: 13, of which 10 were waited for; matrix products, arithmetic and copies ran while one was open for 10% of the time, Pallas kernels for 0%

commit v1 on v0

v1 whole, which is shorter than its diff:
```python
import functools

import jax
import jax.numpy as jnp
from jax import lax
from jax.experimental import pallas as pl
from jax.experimental.pallas import tpu as pltpu
from jax.sharding import PartitionSpec as P

NORM_EPSILON = 1e-05
UNIT_EPSILON = 1e-06
RIM = 8
LANES = 128
F32 = jnp.float32
BF16 = jnp.bfloat16
VMEM_LIMIT = 56 * 1024 * 1024

NN = (((1,), (0,)), ((), ()))
NT = (((1,), (1,)), ((), ()))
TN = (((0,), (0,)), ((), ()))


def split(x):
    high = x.astype(BF16)
    return high, (x - high.astype(F32)).astype(BF16)


def raw(a, b, dims):
    return lax.dot_general(a, b, dims, preferred_element_type=F32)


def mm(a, b, dims=NN):
    a_high, a_low = a if isinstance(a, tuple) else (a, None)
    b_high, b_low = b if isinstance(b, tuple) else (b, None)
    total = raw(a_high, b_high, dims)
    if a_low is not None:
        total = total + raw(a_low, b_high, dims)
    if b_low is not None:
        total = total + raw(a_high, b_low, dims)
    return total


def sigmoid(x):
    return 1.0 / (1.0 + jnp.exp(-x))


def softplus(x):
    return jnp.maximum(x, 0.0) + jnp.log1p(jnp.exp(-jnp.abs(x)))


def grid_masks(size):
    row = lax.broadcasted_iota(jnp.int32, (size, size), 0)
    col = lax.broadcasted_iota(jnp.int32, (size, size), 1)
    return row, col


def unit_inverse(lower, row, col):
    size = lower.shape[0]
    base = 8
    same = (row // base) == (col // base)
    block = jnp.where(same, lower, 0.0)
    one = split(block)
    square = mm(one, one)
    square_parts = split(square)
    fourth = mm(square_parts, square_parts)
    inverse = jnp.where(row == col, 1.0, 0.0) - block + square - mm(one, square_parts)
    inverse = inverse + mm(split(inverse), split(fourth))
    while base < size:
        inside = (row // (2 * base)) == (col // (2 * base))
        apart = (row // base) != (col // base)
        off = split(jnp.where(inside & apart, lower, 0.0))
        parts = split(inverse)
        inverse = inverse - mm(split(mm(parts, off)), parts)
        base *= 2
    return inverse


def gates_of(ab, rate, bias):
    return -rate * softplus(ab + bias), sigmoid(ab)


def decay_of(log_col, log_row, row, col):
    seen = row >= col
    cum_col = jnp.sum(jnp.where(seen, log_row, 0.0), axis=1, keepdims=True)
    cum_row = jnp.sum(jnp.where(row <= col, log_col, 0.0), axis=0, keepdims=True)
    end = jnp.sum(log_row, axis=1, keepdims=True)
    decayed = jnp.where(seen, jnp.exp(jnp.where(seen, cum_col - cum_row, 0.0)), 0.0)
    return cum_col, cum_row, end, decayed


def convolve(ext, taps_ref, length):
    taps = 4
    total = taps_ref[0:1, :] * ext[pl.ds(RIM - taps + 1, length), :]
    for tap in range(1, taps):
        total = total + taps_ref[tap : tap + 1, :] * ext[pl.ds(RIM - taps + 1 + tap, length), :]
    return total


def delta_forward(
    heads, key_dim, value_dim, pre_ref, rim_ref, ab_ref, abt_ref, taps_ref, lane_ref, col_ref,
    query_out, key_out, value_out, inverse_out, delta_out, mix_out, eff_out, map_out, shift_out, ext,
):
    length = pre_ref.shape[1]
    ext[0:RIM, :] = rim_ref[0]
    ext[RIM : RIM + length, :] = pre_ref[0].astype(F32)
    conv = convolve(ext, taps_ref, length)
    active = conv * sigmoid(conv)
    row, col = grid_masks(length)
    log_cols, strength_cols = gates_of(ab_ref[0], lane_ref[0:1, :], lane_ref[1:2, :])
    log_rows, strength_rows = gates_of(abt_ref[0], col_ref[0:8, 0:1], col_ref[8:16, 0:1])
    key_start = heads * key_dim
    value_start = 2 * heads * key_dim
    for h in range(heads):
        query_act = active[:, h * key_dim : (h + 1) * key_dim]
        key_act = active[:, key_start + h * key_dim : key_start + (h + 1) * key_dim]
        value_act = active[:, value_start + h * value_dim : value_start + (h + 1) * value_dim]
        query_scale = lax.rsqrt(jnp.sum(query_act * query_act, axis=1, keepdims=True) + UNIT_EPSILON)
        key_scale = lax.rsqrt(jnp.sum(key_act * key_act, axis=1, keepdims=True) + UNIT_EPSILON)
        query = (query_act * query_scale * key_dim ** (-0.5)).astype(BF16)
        key = (key_act * key_scale).astype(BF16)
        value = value_act.astype(BF16)
        query_out[0, h] = query
        key_out[0, h] = key
        value_out[0, h] = value
        strength = strength_cols[:, heads + h : heads + h + 1]
        strength_row = strength_rows[heads + h : heads + h + 1, :]
        cum_col, cum_row, end, decayed = decay_of(
            log_cols[:, h : h + 1], log_rows[h : h + 1, :], row, col
        )
        products = mm(key, key, NT)
        triangle = jnp.where(row > col, strength * decayed * products, 0.0)
        inverse = unit_inverse(triangle, row, col)
        inverse_out[0, h] = inverse
        scaled = inverse * strength_row
        delta = mm(split(scaled), value)
        mix = mm(split(scaled * jnp.exp(cum_row)), key)
        delta_out[0, h] = delta
        mix_out[0, h] = mix
        scores = split(decayed * mm(query, key, NT))
        eff_out[0, h] = jnp.exp(cum_col) * query.astype(F32) - mm(scores, split(mix))
        end_weight = jnp.exp(end - cum_col)
        small_row = lax.broadcasted_iota(jnp.int32, (key_dim, key_dim), 0)
        small_col = lax.broadcasted_iota(jnp.int32, (key_dim, key_dim), 1)
        moved = jnp.where(small_row == small_col, jnp.exp(end), 0.0)
        map_out[0, h] = moved - mm(split(mix * end_weight), key, TN)
        shift_out[0, h] = mm(split(delta * end_weight), key, TN)


def emit_forward(
    heads, query_ref, key_ref, ab_ref, abt_ref, lane_ref, col_ref, delta_ref, mix_ref, state_ref,
    gate_ref, gain_ref, rows_out, mixer_out, gated_out,
):
    length = query_ref.shape[2]
    value_dim = delta_ref.shape[3]
    row, col = grid_masks(length)
    log_cols, _ = gates_of(ab_ref[0], lane_ref[0:1, :], lane_ref[1:2, :])
    log_rows, _ = gates_of(abt_ref[0], col_ref[0:8, 0:1], col_ref[8:16, 0:1])
    for h in range(heads):
        query, key = query_ref[0, h], key_ref[0, h]
        cum_col, _, _, decayed = decay_of(log_cols[:, h : h + 1], log_rows[h : h + 1, :], row, col)
        scores = split(decayed * mm(query, key, NT))
        state = split(state_ref[0, h])
        rows = delta_ref[0, h] - mm(split(mix_ref[0, h]), state, NT)
        rows_out[0, h] = rows
        mixer = mm(scores, split(rows)) + jnp.exp(cum_col) * mm(query, state, NT)
        mixer_out[0, h] = mixer
        scale = lax.rsqrt(jnp.sum(mixer * mixer, axis=1, keepdims=True) / value_dim + NORM_EPSILON)
        gate = gate_ref[0, :, h * value_dim : (h + 1) * value_dim]
        gated = mixer * scale * gain_ref[0:1, :] * (gate * sigmoid(gate))
        gated_out[0, :, h * value_dim : (h + 1) * value_dim] = gated.astype(BF16)


def gate_backward(
    heads, gated_grad_ref, mixer_ref, gate_ref, gain_ref, eff_ref,
    mixer_grad_out, gate_grad_out, gain_grad_out, shift_grad_out,
):
    value_dim = mixer_ref.shape[3]

    @pl.when(pl.program_id(0) == 0)
    def _():
        gain_grad_out[...] = jnp.zeros_like(gain_grad_out)

    gain = gain_ref[0:1, :]
    for h in range(heads):
        here = slice(h * value_dim, (h + 1) * value_dim)
        grad = gated_grad_ref[0, :, here]
        mixer = mixer_ref[0, h]
        gate = gate_ref[0, :, here]
        scale = lax.rsqrt(jnp.sum(mixer * mixer, axis=1, keepdims=True) / value_dim + NORM_EPSILON)
        sig = sigmoid(gate)
        unit = mixer * scale
        gate_grad_out[0, :, here] = (
            grad * unit * gain * (sig * (1.0 + gate * (1.0 - sig)))
        ).astype(BF16)
        scaled_grad = grad * (gate * sig)
        gain_grad_out[0:1, :] += jnp.sum(scaled_grad * unit, axis=0, keepdims=True)
        unit_grad = scaled_grad * gain
        stat = jnp.sum(unit_grad * mixer, axis=1, keepdims=True) / value_dim
        mixer_grad = scale * (unit_grad - mixer * (scale * scale * stat))
        mixer_grad_out[0, h] = mixer_grad
        shift_grad_out[0, h] = mm(split(mixer_grad), split(eff_ref[0, h]), TN)


def delta_backward(
    heads, key_dim, value_dim, pre_ref, rim_ref, ab_ref, abt_ref, taps_ref, lane_ref, col_ref,
    query_ref, key_ref, value_ref, inverse_ref, rows_ref, state_ref, state_grad_ref, mixer_grad_ref,
    pre_grad_out, tail_out, rim_grad_out, ab_grad_out, taps_grad_out, lane_grad_out,
    ext, conv_grad,
):
    length = pre_ref.shape[1]
    taps = 4

    @pl.when(pl.program_id(0) == 0)
    def _():
        taps_grad_out[...] = jnp.zeros_like(taps_grad_out)
        lane_grad_out[...] = jnp.zeros_like(lane_grad_out)

    ext[0:RIM, :] = rim_ref[0]
    ext[RIM : RIM + length, :] = pre_ref[0].astype(F32)
    row, col = grid_masks(length)
    lane = lax.broadcasted_iota(jnp.int32, (length, LANES), 1)
    log_cols, strength_cols = gates_of(ab_ref[0], lane_ref[0:1, :], lane_ref[1:2, :])
    log_rows, strength_rows = gates_of(abt_ref[0], col_ref[0:8, 0:1], col_ref[8:16, 0:1])
    key_start = heads * key_dim
    value_start = 2 * heads * key_dim
    strict = row > col
    grads = jnp.zeros((length, LANES), F32)
    conv_grad[0:RIM, :] = jnp.zeros((RIM, conv_grad.shape[1]), F32)
    conv_grad[RIM + length : 2 * RIM + length, :] = jnp.zeros((RIM, conv_grad.shape[1]), F32)

    def activation(start, width):
        total = taps_ref[0:1, start : start + width] * ext[pl.ds(RIM - taps + 1, length), start : start + width]
        for tap in range(1, taps):
            total = total + (
                taps_ref[tap : tap + 1, start : start + width]
                * ext[pl.ds(RIM - taps + 1 + tap, length), start : start + width]
            )
        sig = sigmoid(total)
        return total * sig, sig * (1.0 + total * (1.0 - sig))

    def unit_back(grad, start, scale_by):
        act, slope = activation(start, key_dim)
        scale = lax.rsqrt(jnp.sum(act * act, axis=1, keepdims=True) + UNIT_EPSILON)
        inner = jnp.sum(act * grad, axis=1, keepdims=True)
        back = scale_by * scale * (grad - act * (scale * scale * inner))
        conv_grad[RIM : RIM + length, start : start + key_dim] = back * slope

    for h in range(heads):
        query, key, value = query_ref[0, h], key_ref[0, h], value_ref[0, h]
        query_f, key_f = query.astype(F32), key.astype(F32)
        strength = strength_cols[:, heads + h : heads + h + 1]
        cum_col, cum_row, end, decayed = decay_of(
            log_cols[:, h : h + 1], log_rows[h : h + 1, :], row, col
        )
        rise = jnp.exp(cum_col)
        end_weight = jnp.exp(end - cum_col)
        state_f, leaving_f = state_ref[0, h], state_grad_ref[0, h]
        state, leaving = split(state_f), split(leaving_f)
        rows = split(rows_ref[0, h])
        out_grad = split(mixer_grad_ref[0, h])
        products = mm(key, key, NT)
        scores = decayed * mm(query, key, NT)
        rows_grad = mm(split(scores), out_grad, TN) + end_weight * mm(key, leaving, NT)
        scores_grad = mm(out_grad, rows, NT)
        query_grad = rise * mm(out_grad, state)
        right_grad = mm(split(inverse_ref[0, h]), split(rows_grad), TN)
        key_state = mm(key, state, NT)
        triangle_grad = -jnp.where(strict, mm(split(right_grad), rows, NT), 0.0)
        value_grad = strength * right_grad
        strength_grad = jnp.sum(right_grad * (value.astype(F32) - rise * key_state), axis=1, keepdims=True)
        read_grad = -rise * value_grad
        cum_grad = jnp.sum(read_grad * key_state, axis=1, keepdims=True)
        key_grad = mm(split(read_grad), state)
        decayed_grad = triangle_grad * decayed
        strength_grad = strength_grad + jnp.sum(decayed_grad * products, axis=1, keepdims=True)
        weighted = strength * decayed_grad
        both = weighted * products + scores_grad * scores
        products_grad = split(weighted)
        overlap_grad = split(scores_grad * decayed)
        cum_grad = cum_grad + jnp.sum(both, axis=1, keepdims=True) + jnp.sum(query_f * query_grad, axis=1, keepdims=True)
        query_grad = query_grad + mm(overlap_grad, key)
        key_grad = (
            key_grad + mm(overlap_grad, query, TN) + mm(products_grad, key) + mm(products_grad, key, TN)
        )
        moved = mm(rows, leaving)
        key_grad = key_grad + end_weight * moved
        end_part = jnp.sum(moved * key_f, axis=1, keepdims=True) * end_weight
        cum_grad = cum_grad - end_part
        last = jnp.sum(end_part, axis=0, keepdims=True) + jnp.exp(end) * jnp.sum(
            jnp.sum(leaving_f * state_f, axis=1, keepdims=True), axis=0, keepdims=True
        )
        turned = jnp.sum(jnp.where(row == col, cum_grad, 0.0), axis=0, keepdims=True)
        turned = turned - jnp.sum(both, axis=0, keepdims=True)
        log_grad = jnp.sum(jnp.where(row <= col, turned, 0.0), axis=1, keepdims=True) + last
        grads = jnp.where(lane == h, log_grad, grads)
        grads = jnp.where(lane == heads + h, strength_grad, grads)
        unit_back(query_grad, h * key_dim, key_dim ** (-0.5))
        unit_back(key_grad, key_start + h * key_dim, 1.0)
        _, slope = activation(value_start + h * value_dim, value_dim)
        conv_grad[RIM : RIM + length, value_start + h * value_dim : value_start + (h + 1) * value_dim] = (
            value_grad * slope
        )

    softened = -lane_ref[0:1, :] * sigmoid(ab_ref[0] + lane_ref[1:2, :])
    decay_part = grads * softened
    is_log = lane < heads
    ab_grad_out[0] = jnp.where(is_log, decay_part, grads * strength_cols * (1.0 - strength_cols))
    lane_grad_out[0:1, :] += jnp.sum(jnp.where(is_log, grads * log_cols, 0.0), axis=0, keepdims=True)
    lane_grad_out[1:2, :] += jnp.sum(jnp.where(is_log, decay_part, 0.0), axis=0, keepdims=True)
    main = conv_grad[RIM : RIM + length, :]
    pre_grad = jnp.zeros_like(main)
    rim_grad = jnp.zeros((RIM, conv_grad.shape[1]), F32)
    for tap in range(taps):
        weight = taps_ref[tap : tap + 1, :]
        taps_grad_out[tap : tap + 1, :] += jnp.sum(
            main * ext[pl.ds(RIM - taps + 1 + tap, length), :], axis=0, keepdims=True
        )
        pre_grad = pre_grad + weight * conv_grad[pl.ds(RIM + taps - 1 - tap, length), :]
        rim_grad = rim_grad + weight * conv_grad[pl.ds(taps - 1 - tap, RIM), :]
    pre_grad_out[0] = pre_grad.astype(BF16)
    tail_out[0] = pre_grad[length - RIM : length, :]
    rim_grad_out[0] = rim_grad


def by_slot(shape):
    rest = len(shape) - 1
    return pl.BlockSpec((1,) + tuple(shape[1:]), lambda s: (s,) + (0,) * rest)


def whole(shape):
    return pl.BlockSpec(tuple(shape), lambda s: (0,) * len(shape))


def run_slots(body, slots, sliced, shared, sliced_out, shared_out=(), scratch=(), order=None):
    operands = list(sliced) + list(shared)
    specs = [by_slot(a.shape) for a in sliced] + [whole(a.shape) for a in shared]
    if order is not None:
        operands = [operands[i] for i in order]
        specs = [specs[i] for i in order]
    return pl.pallas_call(
        body,
        grid=(slots,),
        in_specs=specs,
        out_specs=[by_slot(o.shape) for o in sliced_out] + [whole(o.shape) for o in shared_out],
        out_shape=list(sliced_out) + list(shared_out),
        scratch_shapes=list(scratch),
        compiler_params=pltpu.CompilerParams(vmem_limit_bytes=VMEM_LIMIT),
    )(*operands)


def shifted(block, axis, distance):
    devices = range(lax.axis_size(axis))
    route = [(i - distance, i) for i in devices if i - distance in devices]
    return lax.ppermute(block, axis, route)


def to_units(parts, units):
    pairs, value_dim, key_dim = parts.shape
    share = units // pairs
    return parts.reshape(units, value_dim // share, key_dim)


def exchange(parts, axis):
    return lax.all_to_all(parts, axis, 0, 0, tiled=True)


def per_device(
    hidden_in, lengths, input_gain, query_weight, key_weight, value_weight, alpha_weight, beta_weight,
    decay_log, decay_bias, query_kernel, key_kernel, value_kernel, gate_weight, output_gain,
    output_weight, mixed_gain, swiglu_gate, swiglu_up, swiglu_down, cotangent,
):
    slots, segment, width = hidden_in.shape
    rows = slots * segment
    heads = decay_log.shape[0]
    key_dim = query_kernel.shape[1] // heads
    value_dim = value_kernel.shape[1] // heads
    taps = query_kernel.shape[0]
    split_key = heads * key_dim
    channels = 2 * split_key + heads * value_dim
    head_parts = lax.axis_size("head")
    seq_parts = lax.axis_size("seq")
    shard = width // head_parts
    head_start = lax.axis_index("head") * shard
    pairs = slots * heads
    sds = jax.ShapeDtypeStruct

    position = lax.axis_index("seq") * segment + jnp.arange(segment)
    mask = (position[None, :] < lengths[:, None]).astype(F32)[:, :, None]

    def norm_rows(x):
        inv = lax.rsqrt(jnp.mean(x * x, axis=-1, keepdims=True) + NORM_EPSILON)
        return inv, (x * inv * input_gain).astype(BF16)

    rim_in = shifted(hidden_in[:, segment - taps + 1 :, :], "seq", 1)
    x_full = hidden_in.astype(F32)
    inv_first, normed_first = norm_rows(x_full)
    normed_first = normed_first.reshape(rows, width)
    x_shard = lax.dynamic_slice_in_dim(x_full, head_start, shard, 2)
    qkv_weight = jnp.concatenate([query_weight, key_weight, value_weight], axis=1)
    ab_weight = jnp.concatenate(
        [alpha_weight, beta_weight, jnp.zeros((width, LANES - 2 * heads), BF16)], axis=1
    )

    def project(x, weight):
        return jnp.dot(x, weight, preferred_element_type=F32)

    pre_all = project(normed_first, qkv_weight).astype(BF16).reshape(slots, segment, channels)
    gate_pre = project(normed_first, gate_weight).reshape(slots, segment, -1)
    ab_pre = project(normed_first, ab_weight).reshape(slots, segment, LANES)
    ab_rows = jnp.swapaxes(ab_pre[:, :, :8], 1, 2)
    _, rim_normed = norm_rows(rim_in.astype(F32))
    rim_pre = project(rim_normed.reshape(slots * (taps - 1), width), qkv_weight).astype(BF16).astype(F32)
    rim_pre = jnp.pad(rim_pre.reshape(slots, taps - 1, channels), ((0, 0), (RIM - taps + 1, 0), (0, 0)))
    kernel = jnp.concatenate([query_kernel, key_kernel, value_kernel], axis=1).astype(F32)
    kernel = jnp.pad(kernel, ((0, 8 - taps), (0, 0)))
    rate = jnp.exp(decay_log)
    pad_heads = lambda v: jnp.pad(v, (0, LANES - heads))
    lane_gates = jnp.pad(jnp.stack([pad_heads(rate), pad_heads(decay_bias)]), ((0, 6), (0, 0)))
    pad_rows = lambda v: jnp.broadcast_to(jnp.pad(v, (0, 8 - heads))[:, None], (8, LANES))
    col_gates = jnp.concatenate([pad_rows(rate), pad_rows(decay_bias)], axis=0)
    gain_row = jnp.broadcast_to(output_gain[None, :], (8, value_dim))

    per_pair = lambda *tail: sds((slots, heads) + tail, F32)
    low_pair = lambda *tail: sds((slots, heads) + tail, BF16)
    query, key, value, inverse, delta, mix, eff, maps, shifts = run_slots(
        functools.partial(delta_forward, heads, key_dim, value_dim),
        slots,
        (pre_all, rim_pre, ab_pre, ab_rows),
        (kernel, lane_gates, col_gates),
        (
            low_pair(segment, key_dim), low_pair(segment, key_dim), low_pair(segment, value_dim),
            per_pair(segment, segment), per_pair(segment, value_dim), per_pair(segment, key_dim),
            per_pair(segment, key_dim), per_pair(key_dim, key_dim), per_pair(value_dim, key_dim),
        ),
        scratch=[pltpu.VMEM((segment + RIM, channels), F32)],
    )

    units = seq_parts
    share = units // pairs
    own_maps = jnp.repeat(maps.astype(BF16).reshape(pairs, key_dim, key_dim), share, axis=0)
    own_shifts = to_units(shifts.astype(BF16).reshape(pairs, value_dim, key_dim), units)
    all_maps = exchange(own_maps, "seq").astype(F32)
    all_shifts = exchange(own_shifts, "seq").astype(F32)
    high = functools.partial(jnp.dot, precision=lax.Precision.HIGHEST, preferred_element_type=F32)
    state = jnp.zeros_like(all_shifts[0])
    states = []
    for p in range(seq_parts):
        states.append(state)
        state = high(state, all_maps[p]) + all_shifts[p]
    state_in = exchange(jnp.stack(states).astype(BF16), "seq").astype(F32)
    state_in = state_in.reshape(slots, heads, value_dim, key_dim)

    value_rows, mixer, gated = run_slots(
        functools.partial(emit_forward, heads),
        slots,
        (query, key, ab_pre, ab_rows, delta, mix, state_in, gate_pre),
        (lane_gates, col_gates, gain_row),
        (
            per_pair(segment, value_dim), per_pair(segment, value_dim),
            sds((slots, segment, heads * value_dim), BF16),
        ),
        order=(0, 1, 2, 3, 8, 9, 4, 5, 6, 7, 10),
    )
    gated_low = gated.reshape(rows, heads * value_dim)

    def scatter_sum(part):
        low = part.astype(BF16).reshape(slots, segment, width)
        return lax.psum_scatter(low, "head", scatter_dimension=2, tiled=True).astype(F32)

    attention_shard = scatter_sum(project(gated_low, output_weight))
    residual = x_shard + mask * attention_shard
    square_sum = lax.psum(jnp.sum(residual * residual, axis=-1, keepdims=True), "head")
    inv_second = lax.rsqrt(square_sum / width + NORM_EPSILON)
    normed_shard = (residual * inv_second * mixed_gain).astype(BF16)
    normed_second = lax.all_gather(normed_shard, "head", axis=2, tiled=True).reshape(rows, width)
    gate_values = project(normed_second, swiglu_gate)
    upward_values = project(normed_second, swiglu_up)
    sigmoid_gate = jax.nn.sigmoid(gate_values)
    silu_gate = gate_values * sigmoid_gate
    activation = (silu_gate * upward_values).astype(BF16)
    out_grad = jnp.where(mask > 0, cotangent, jnp.zeros_like(cotangent)).reshape(rows, width)
    activation_grad = jnp.dot(out_grad, swiglu_down.T, preferred_element_type=F32)
    upward_grad = (activation_grad * silu_gate).astype(BF16)
    gate_grad = (
        activation_grad * upward_values * sigmoid_gate * (1.0 + gate_values * (1.0 - sigmoid_gate))
    ).astype(BF16)
    normed_part = jnp.dot(upward_grad, swiglu_up.T, preferred_element_type=F32) + jnp.dot(
        gate_grad, swiglu_gate.T, preferred_element_type=F32
    )
    normed_grad = scatter_sum(normed_part)
    swiglu_shard = scatter_sum(project(activation, swiglu_down))
    block_out = (residual + mask * swiglu_shard).astype(BF16)
    swiglu_down_grad = project(activation.T, out_grad)
    swiglu_up_grad = project(normed_second.T, upward_grad)
    swiglu_gate_grad = project(normed_second.T, gate_grad)

    def sum_low(parts):
        flat = jnp.concatenate([p.astype(BF16).reshape(-1, LANES) for p in parts], axis=0)
        total = lax.psum(flat, "seq")
        out, at = [], 0
        for p in parts:
            size = p.size // LANES
            out.append(total[at : at + size].reshape(p.shape).astype(F32))
            at += size
        return out

    swiglu_sums = sum_low((swiglu_down_grad, swiglu_up_grad, swiglu_gate_grad))
    mixed_gain_grad = jnp.sum(normed_grad * residual * inv_second, axis=(0, 1))
    weighted_second = normed_grad * mixed_gain
    second_stat = lax.psum(jnp.sum(weighted_second * residual, axis=-1, keepdims=True), "head")
    out_shard = lax.dynamic_slice_in_dim(cotangent, head_start, shard, 2).astype(F32)
    residual_grad = out_shard + inv_second * (
        weighted_second - residual * inv_second * inv_second * second_stat / width
    )
    mixer_grad_low = (mask * residual_grad).astype(BF16)
    mixer_grad = lax.all_gather(mixer_grad_low, "head", axis=2, tiled=True).reshape(rows, width)
    gated_grad = jnp.dot(mixer_grad, output_weight.T, preferred_element_type=F32)
    output_weight_grad = project(gated_low.T, mixer_grad)

    mixer_out_grad, gate_low, gain_part, shift_grads = gate_backward_call(
        heads, slots, segment, value_dim, key_dim, gated_grad, mixer, gate_pre, eff, gain_row
    )
    gate_low = gate_low.reshape(rows, heads * value_dim)
    gate_weight_grad = project(normed_first.T, gate_low)
    middle_sums = sum_low((output_weight_grad, gate_weight_grad))

    all_grads = exchange(
        to_units(shift_grads.astype(BF16).reshape(pairs, value_dim, key_dim), units), "seq"
    ).astype(F32)
    leaving = jnp.zeros_like(all_grads[0])
    leavings = [None] * seq_parts
    for p in reversed(range(seq_parts)):
        leavings[p] = leaving
        leaving = high(leaving, all_maps[p].T) + all_grads[p]
    state_grad = exchange(jnp.stack(leavings).astype(BF16), "seq").astype(F32)
    state_grad = state_grad.reshape(slots, heads, value_dim, key_dim)

    pre_low, tail, rim_grad, ab_grad, taps_grad, lane_grad = run_slots(
        functools.partial(delta_backward, heads, key_dim, value_dim),
        slots,
        (pre_all, rim_pre, ab_pre, ab_rows, query, key, value, inverse, value_rows, state_in, state_grad, mixer_out_grad),
        (kernel, lane_gates, col_gates),
        (
            sds((slots, segment, channels), BF16), sds((slots, RIM, channels), F32),
            sds((slots, RIM, channels), F32), sds((slots, segment, LANES), F32),
        ),
        (sds((8, channels), F32), sds((8, LANES), F32)),
        scratch=[
            pltpu.VMEM((segment + RIM, channels), F32),
            pltpu.VMEM((segment + 2 * RIM, channels), F32),
        ],
        order=(0, 1, 2, 3, 12, 13, 14, 4, 5, 6, 7, 8, 9, 10, 11),
    )
    rim_back = shifted(rim_grad[:, RIM - taps + 1 :, :], "seq", -1)
    last_rows = (tail[:, RIM - taps + 1 :, :] + rim_back).astype(BF16)
    pre_low = lax.dynamic_update_slice_in_dim(pre_low, last_rows, segment - taps + 1, 1)
    pre_low = pre_low.reshape(rows, channels)
    ab_low = ab_grad.reshape(rows, LANES).astype(BF16)

    first_part = (
        jnp.dot(pre_low, qkv_weight.T, preferred_element_type=F32)
        + jnp.dot(gate_low, gate_weight.T, preferred_element_type=F32)
        + jnp.dot(ab_low, ab_weight.T, preferred_element_type=F32)
    )
    first_sum = scatter_sum(first_part)
    pre_weight_grad = project(normed_first.T, pre_low)
    ab_weight_grad = project(normed_first.T, ab_low)[:, : 2 * heads]
    (pre_sums,) = sum_low((pre_weight_grad,))
    weighted_first = first_sum * lax.dynamic_slice_in_dim(input_gain, head_start, shard, 0)
    first_stat = lax.psum(jnp.sum(weighted_first * x_shard, axis=-1, keepdims=True), "head")
    input_grad = (
        residual_grad
        + inv_first * (weighted_first - x_shard * inv_first * inv_first * first_stat / width)
    )
    input_gain_grad = jnp.sum(first_sum * x_shard * inv_first, axis=(0, 1))
    gain_sum = lax.psum(gain_part[0], ("head", "seq"))
    value_share = value_dim // head_parts
    output_gain_grad = lax.dynamic_slice_in_dim(
        gain_sum, lax.axis_index("head") * value_share, value_share, 0
    )
    small = lax.psum(
        (input_gain_grad, ab_weight_grad, lane_grad[0, :heads], lane_grad[1, :heads], taps_grad[:taps], mixed_gain_grad),
        "seq",
    )
    taps_sum = small[4]
    return (
        block_out,
        input_grad,
        small[0],
        pre_sums[:, :split_key],
        pre_sums[:, split_key : 2 * split_key],
        pre_sums[:, 2 * split_key :],
        small[1][:, :heads],
        small[1][:, heads:],
        small[2],
        small[3],
        taps_sum[:, :split_key],
        taps_sum[:, split_key : 2 * split_key],
        taps_sum[:, 2 * split_key :],
        middle_sums[1],
        output_gain_grad,
        middle_sums[0],
        small[5],
        swiglu_sums[2],
        swiglu_sums[1],
        swiglu_sums[0],
    )


def gate_backward_call(heads, slots, segment, value_dim, key_dim, gated_grad, mixer, gate_pre, eff, gain_row):
    sds = jax.ShapeDtypeStruct
    gated_grad = gated_grad.reshape(slots, segment, -1)
    outs = [
        sds((slots, heads, segment, value_dim), F32),
        sds((slots, segment, heads * value_dim), BF16),
        sds((8, value_dim), F32),
        sds((slots, heads, value_dim, key_dim), F32),
    ]
    return pl.pallas_call(
        functools.partial(gate_backward, heads),
        grid=(slots,),
        in_specs=[
            by_slot(gated_grad.shape), by_slot(mixer.shape), by_slot(gate_pre.shape),
            whole(gain_row.shape), by_slot(eff.shape),
        ],
        out_specs=[by_slot(outs[0].shape), by_slot(outs[1].shape), whole(outs[2].shape), by_slot(outs[3].shape)],
        out_shape=outs,
        compiler_params=pltpu.CompilerParams(vmem_limit_bytes=VMEM_LIMIT),
    )(gated_grad, mixer, gate_pre, gain_row, eff)


def solution(mesh):
    seq, cols, lines = P(None, "seq", None), P(None, "head"), P("head", None)
    one = P("head")
    placed = (
        seq, P(), P(), cols, cols, cols, cols, cols, one, one, cols, cols, cols, cols, P(), lines, one,
        cols, cols, lines, seq,
    )
    both = P(None, "seq", "head")
    return jax.shard_map(
        per_device,
        mesh=mesh,
        in_specs=placed,
        out_specs=(
            both, both, one, cols, cols, cols, cols, cols, one, one, cols, cols, cols, cols, one, lines,
            one, cols, cols, lines,
        ),
        check_vma=False,
    )
```

time: 1850 us -> 813 us (0.44)
  waiting for transfers between devices: 1040 us -> 345 us
  other arithmetic: 273 us -> 62.9 us
  matrix products: 262 us -> 102 us
  local copies, waits for them, and re-layouts: 183 us -> 62.9 us
  Pallas kernels: 0 us -> 82.5 us
  blocking collectives: 59.3 us -> 102 us
  starting transfers between devices: 8.61 us -> 29 us
    psum x2 -> x1, waiting for transfers between devices: 543 us -> 187 us  [sum_low(): total = lax.psum(flat, 'seq')]
    all_gather x4 -> x0, waiting for transfers between devices: 306 us -> none  [carried_in(): gathered = jax.tree.map(lambda a: lax.all_gather(a, axis), part)]
    another operation x7 -> x1, other arithmetic: 177 us -> 0.6 us  [per_device(): jnp.stack([pad_heads(rate), pad_heads(decay_bias)])]
    dot_general x87 -> x36, matrix products: 252 us -> 102 us  [the longest x15 53.4 us: project(): return jnp.dot(x, weight, preferred_element_type=F32)]
    pallas_call x0 -> x4, Pallas kernels: none -> 82.5 us  [the longest x3 75.7 us: run_slots(): pl.pallas_call(body, grid=(slots,), in_specs=specs, out_specs=[by_slot(o....]
    reduce_scatter x3 -> x4, waiting for transfers between devices: 151 us -> 79.4 us  [scatter_sum(): lax.psum_scatter(low, 'head', scatter_dimension=2, tiled=True).astype(F32)]
    psum x2 -> x3, blocking collectives: 47.1 us -> 89.9 us  [the longest x1 44.8 us: per_device(): gain_sum = lax.psum(gain_part[0], ('head', 'seq'))]
    all_to_all x0 -> x5, waiting for transfers between devices: none -> 37.7 us  [exchange(): return lax.all_to_all(parts, axis, 0, 0, tiled=True)]
  transfers between devices with their start and end apart: 13 -> 14, of which waited for: 10 -> 11; matrix products, arithmetic and copies ran while one was open for 10% -> 14% of each run, Pallas kernels for 0% -> 0%
where the time goes in v1:
time: 813 us; the launch traced here: 801 us
  waiting for transfers between devices  345 us (42%)
  matrix products  102 us (13%)
  blocking collectives  102 us (13%)
  Pallas kernels  82.5 us (10%)
  local copies, waits for them, and re-layouts  62.9 us (8%)
  other arithmetic  62.9 us (8%)
  starting transfers between devices  29 us (4%)
  between operations  15.3 us (2%)
    psum x1, waiting for transfers between devices, sum_low(): total = lax.psum(flat, 'seq')  187 us
    reduce_scatter x4, waiting for transfers between devices, scatter_sum(): lax.psum_scatter(low, 'head', scatter_dimension=2, tiled=True).astype(F32)  79.4 us
    pallas_call x3, Pallas kernels, run_slots(): pl.pallas_call(body, grid=(slots,), in_specs=specs, out_specs=[by_slot(o....  75.7 us
    dot_general x15, matrix products, project(): return jnp.dot(x, weight, preferred_element_type=F32)  53.4 us
    psum x1, blocking collectives, per_device(): gain_sum = lax.psum(gain_part[0], ('head', 'seq'))  44.8 us
    psum x1, blocking collectives, per_device(): lax.psum((input_gain_grad, ab_weight_grad, lane_grad[0, :heads], lane_gra...  39.1 us
    all_to_all x5, waiting for transfers between devices, exchange(): return lax.all_to_all(parts, axis, 0, 0, tiled=True)  37.7 us
    all_gather x1, waiting for transfers between devices, per_device(): lax.all_gather(mixer_grad_low, 'head', axis=2, tiled=True)  23 us
  transfers between devices with their start and end apart: 14, of which 11 were waited for; matrix products, arithmetic and copies ran while one was open for 14% of the time, Pallas kernels for 0%

profile of v1, /device:TPU:0, one launch (start us, length us, event | category | flops | bytes accessed | tf_op | source)
XLA Modules:
  0.0 801.3 jit_solution(16796390849264600778)
XLA Ops:
  8.9 5.4 collective-permute-start
  19.7 3.7 convolution_convert_fusion.1
  37.1 40.2 %shard_map.356 = (bf16[4,2,256,128]{3,2,1,0:T(8,128)(2,1)}, bf16[4,2,256,128]{3,2,1,0:T(8,128)(2,1)}, bf16[4,2,256,256]{3,2,1,0:T(8,128)(2,1)}, f32[4,2,256,256]...) custom-call(bf16[4,256,1024]{2,1,0:T(8,128)(2,1)} %bitcast.233, ...), custom_call_target="tpu_custom_call" | custom-call | tf_op jit(solution)/shard_map/pallas_call | solution.py:340
  79.5 4.3 all-to-all-start.1
  85.5 12.6 %all-to-all-done.1 = bf16[8,256,128]{2,1,0:T(8,128)(2,1)} async-done(((bf16[8,256,128]{2,1,0:T(8,128)(2,1)}), bf16[8,256,128]{2,1,0:T(8,128)(2,1)}, u32[]{:S(2)}, u32[]{:S(2)}) %all-to-all-start.1) | async-done | bytes 524320 | tf_op jit(solution)/shard_map/all_to_all | solution.py:364
  98.1 4.3 all-to-all-start
  105.1 5.9 all-to-all-done
  123.3 4.1 all-to-all-start.2
  127.5 4.4 fusion.23.gate_ref
  131.9 9.1 %all-to-all-done.2 = bf16[8,256,128]{2,1,0:T(8,128)(2,1)} async-done(((bf16[8,256,128]{2,1,0:T(8,128)(2,1)}), bf16[8,256,128]{2,1,0:T(8,128)(2,1)}, u32[]{:S(2)}, u32[]{:S(2)}) %all-to-all-start.2) | async-done | bytes 524320 | tf_op jit(solution)/shard_map/all_to_all | solution.py:364
  143.7 8.6 %shard_map.357 = (f32[4,2,256,256]{3,2,1,0:T(8,128)}, f32[4,2,256,256]{3,2,1,0:T(8,128)}, bf16[4,256,512]{2,1,0:T(8,128)(2,1)}) custom-call(bf16[4,2,256,128]{3,2,1,0:T(8,128)(2,1)} %get-tuple-element.42.query_ref, bf16[4,2,256,128]{3,2,1,0:T(8,128)(2,1)} %get-tuple-element.43.key_ref, f32[4,256,128]{2,1,0:T(8,128)} %copy.48.ab_ref, ...), custom_call_target="tpu_custom_call" | custom-call | tf_op jit(solution)/shard_map/pallas_call | solution.py:340
  152.4 3.8 convolution_convert_fusion
  158.9 28.0 %reduce-scatter.5.cloned.1.call-done = bf16[4,256,256]{2,1,0:T(8,128)(2,1)} async-done(((bf16[4,256,1024]{2,1,0:T(8,128)(2,1)}), bf16[4,256,256]{2,1,0:T(8,128)(2,1)}) %reduce-scatter.5.cloned.1.call-update) | async-done | bytes 524304 | tf_op jit(solution)/shard_map/reduce_scatter | solution.py:468
  188.7 5.8 psum.91
  198.9 3.3 fusion.51
  202.1 17.4 %all-gather.3.cloned.1.call-done = bf16[4,256,1024]{2,1,0:T(8,128)(2,1)} async-done(((bf16[4,256,256]{2,1,0:T(8,128)(2,1)}), bf16[4,256,1024]{2,1,0:T(8,128)(2,1)}) %all-gather.3.cloned.1.call-update) | async-done | bytes 2097168 | tf_op jit(solution)/shard_map/all_gather | solution.py:475
  219.6 3.8 fusion.50
  223.5 4.0 multiply_convert_fusion.1
  229.3 3.3 add_convert_fusion.1
  234.0 4.5 convolution_convert_fusion.2
  238.5 25.7 %reduce-scatter.9.cloned.1.call-done = bf16[4,256,256]{2,1,0:T(8,128)(2,1)} async-done(((bf16[4,256,1024]{2,1,0:T(8,128)(2,1)}), bf16[4,256,256]{2,1,0:T(8,128)(2,1)}) %reduce-scatter.9.cloned.1.call-update) | async-done | bytes 524304 | tf_op jit(solution)/shard_map/reduce_scatter | solution.py:468
  266.2 6.1 psum.92
  272.4 25.7 %reduce-scatter.7.cloned.1.call-done = bf16[4,256,256]{2,1,0:T(8,128)(2,1)} async-done(((bf16[4,256,1024]{2,1,0:T(8,128)(2,1)}), bf16[4,256,256]{2,1,0:T(8,128)(2,1)}) %reduce-scatter.7.cloned.1.call-update) | async-done | bytes 524304 | tf_op jit(solution)/shard_map/reduce_scatter | solution.py:468
  301.0 23.0 %all-gather.5.cloned.1.call-done = bf16[4,256,1024]{2,1,0:T(8,128)(2,1)} async-done(((bf16[4,256,256]{2,1,0:T(8,128)(2,1)}), bf16[4,256,1024]{2,1,0:T(8,128)(2,1)}) %all-gather.5.cloned.1.call-update) | async-done | bytes 2097168 | tf_op jit(solution)/shard_map/all_gather | solution.py:516
  324.0 4.2 fusion.21.gated_grad_ref
  328.2 6.8 shard_map.358
  337.1 5.5 all-to-all-start.3
  342.6 4.8 convolution_convert_fusion.4
  347.4 10.1 %all-to-all-done.3 = bf16[8,256,128]{2,1,0:T(8,128)(2,1)S(1)} async-done(((bf16[8,256,128]{2,1,0:T(8,128)(2,1)}), bf16[8,256,128]{2,1,0:T(8,128)(2,1)S(1)}, u32[]{:S(2)}, u32[]{:S(2)}) %all-to-all-start.3) | async-done | bytes 524320 | tf_op jit(solution)/shard_map/all_to_all | solution.py:364
  369.7 3.6 all-to-all-start.4
  373.5 4.9 convolution_convert_fusion.3
  380.0 3.4 reshape.250
  386.0 4.3 reshape.251
  390.3 4.8 convolution_convert_fusion.5
  395.1 3.5 reshape.249
  398.6 4.8 fusion.53
  404.4 26.8 %shard_map.359 = (bf16[4,256,1024]{2,1,0:T(8,128)(2,1)}, f32[4,8,1024]{2,1,0:T(8,128)}, f32[4,8,1024]{2,1,0:T(8,128)}, f32[4,256,128]{2,1,0:T(8,128)}, f32[8,1024]{1,0:T(8,128)}, /*index=5*/f32[8,128]{1,0:T(8,128)}) custom-call(bf16[4,256,1024]{2,1,0:T(8,128)(2,1)} %bitcast.234, f32[4,8,1024]{2,1,0:T(8,128)} %pad_convert_fusion.rim_ref, ...), custom_call_target="tpu_custom_call" | custom-call | tf_op jit(solution)/shard_map/pallas_call | solution.py:340
  439.9 8.3 %add_convert_fusion = bf16[1024,1024]{1,0:T(8,128)(2,1)} fusion(f32[1024,1024]{1,0:T(8,128)} %fusion.25, f32[1024,1024]{1,0:T(8,128)} %fusion.53, bf16[1024,1024]{1,0:T(8,128)(2,1)} %bitcast.252, bf16[1024,1024]{1,0:T(8,128)(2,1)} %copy-done.8), kind=kOutput, calls=%fused_computation.2 | convolution fusion | flops 2150629376 | bytes 14680064 | tf_op jit(solution)/shard_map/dot_general | solution.py:561
  448.3 13.0 %pad_maximum_fusion = bf16[16896,128]{1,0:T(8,128)(2,1)} fusion(bf16[5632,128]{1,0:T(8,128)(2,1)} %reshape.251, bf16[5632,128]{1,0:T(8,128)(2,1)S(1)} %reshape.250, bf16[5632,128]{1,0:T(8,128)(2,1)} %reshape.249), kind=kLoop, calls=%fused_computation | loop fusion | flops 12976128 | bytes 8650752 | tf_op jit(solution)/shard_map/concatenate | solution.py:498
  463.1 4.1 bitcast_convert_fusion.1
  471.9 3.8 bitcast_convert_fusion
  476.5 44.8 %psum.101 = f32[256]{0:T(256)S(1)} all-reduce(f32[256]{0:T(256)S(1)} %bitcast.247), channel_id=1, replica_groups=mesh['seq'=8,'head'=4] {'head','seq'}, use_global_device_ids=true, to_apply=%region_20.21 | all-reduce | flops 256 | bytes 2048 | tf_op jit(solution)/shard_map/psum | solution.py:576
  526.6 39.1 %all-reduce.7 = (f32[256]{0:T(256)}, f32[1024,4]{0,1:T(4,128)S(1)}, f32[2]{0:T(128)}, f32[2]{0:T(128)}, f32[4,1024]{1,0:T(4,128)S(1)}, /*index=5*/f32[256]{0:T(256)}) all-reduce(f32[256]{0:T(256)S(1)} %get-tuple-element.84, f32[1024,4]{0,1:T(4,128)S(1)} %slice.208, ...), channel_id=1, replica_groups=mesh['seq'=8,'head'=4] {'seq'}, use_global_device_ids=true, to_apply=%region_13.14 | all-reduce | flops 8708 | bytes 69664 | tf_op jit(solution)/shard_map/psum | solution.py:581
  566.3 6.0 psum.93
  576.7 186.6 %all-reduce.11.cloned.1.call-done = (bf16[1024,1024]{1,0:T(8,128)(2,1)}, bf16[8192,128]{1,0:T(8,128)(2,1)}, bf16[16896,128]{1,0:T(8,128)(2,1)}) async-done(((bf16[1024,1024]{1,0:T(8,128)(2,1)}, bf16[8192,128]{1,0:T(8,128)(2,1)}, bf16[16896,128]{1,0:T(8,128)(2,1)}), (bf16[1024,1024]{1,0:T(8,128)(2,1)}, bf16[8192,128]{1,0:T(8,128)(2,1)}, bf16[16896,128]{1,0:T(8,128)(2,1)})) %all-reduce.11.cloned.1.call-update) | async-done | bytes 8519696 | tf_op jit(solution)/shard_map/psum | solution.py:499
  767.6 3.7 slice_convert_fusion
  781.9 4.2 reshape.263
  786.1 3.1 slice_convert_fusion.3
  (213 shorter events, 124.7 us)
Async XLA Ops:
  7.2 216.2 %copy-start = (bf16[1024,704]{0,1:T(8,128)(2,1)S(1)}, bf16[1024,704]{0,1:T(8,128)(2,1)}, u32[]{:S(2)}) copy-start(bf16[1024,704]{0,1:T(8,128)(2,1)} %param.38) | copy-start | bytes 4325380
  7.2 9.2 %copy-start.2 = (bf16[4,256,1024]{2,1,0:T(8,128)(2,1)S(1)}, bf16[4,256,1024]{2,1,0:T(8,128)(2,1)}, u32[]{:S(2)}) copy-start(bf16[4,256,1024]{2,1,0:T(8,128)(2,1)} %param.21) | copy-start | bytes 6291460
  7.2 9.2 %copy-start.20 = (f32[1024]{0:T(1024)S(1)}, f32[1024]{0:T(1024)}, u32[]{:S(2)}) copy-start(f32[1024]{0:T(1024)} %param.23) | copy-start | bytes 12292
  8.9 18.4 %collective-permute-start = (bf16[4,3,1024]{2,1,0:T(4,128)(2,1)}, bf16[4,3,1024]{2,1,0:T(4,128)(2,1)}, u32[]{:S(2)}, u32[]{:S(2)}) collective-permute-start(bf16[4,3,1024]{2,1,0:T(4,128)(2,1)} %slice.138), channel_id=1, source_target_pairs={{0,4},{4,8},{8,12},{12,16},{16,20},{20,24},{24,28},{1,5},{5,9},{9,... | collective-permute-start | bytes 73736 | tf_op jit(solution)/shard_map/ppermute | solution.py:354
  17.0 6.4 copy-start.3
  19.6 3.7 copy-start.8
  19.6 3.7 copy-start.36
  19.7 4.3 copy-start.29
  19.7 4.3 copy-start.30
  19.7 4.3 copy-start.31
  28.1 8.3 %copy-start.35 = (f32[16]{0:T(128)S(1)}, f32[16]{0:T(128)}, u32[]{:S(2)}) copy-start(f32[16]{0:T(128)} %fusion.42) | copy-start | bytes 196
  79.5 18.7 %all-to-all-start.1 = ((bf16[8,256,128]{2,1,0:T(8,128)(2,1)}), bf16[8,256,128]{2,1,0:T(8,128)(2,1)}, u32[]{:S(2)}, u32[]{:S(2)}) async-start(bf16[8,256,128]{2,1,0:T(8,128)(2,1)} %bitcast.239), calls=%async_computation.1 | async-start | bytes 1048576 | tf_op jit(solution)/shard_map/all_to_all | solution.py:364
  98.1 12.8 %all-to-all-start = ((bf16[8,128,128]{2,1,0:T(8,128)(2,1)}), bf16[8,128,128]{2,1,0:T(8,128)(2,1)}, u32[]{:S(2)}, u32[]{:S(2)}) async-start(bf16[8,128,128]{2,1,0:T(8,128)(2,1)} %bitcast.244), calls=%async_computation | async-start | bytes 524288 | tf_op jit(solution)/shard_map/all_to_all | solution.py:364
  123.3 17.7 %all-to-all-start.2 = ((bf16[8,256,128]{2,1,0:T(8,128)(2,1)}), bf16[8,256,128]{2,1,0:T(8,128)(2,1)}, u32[]{:S(2)}, u32[]{:S(2)}) async-start(bf16[8,256,128]{2,1,0:T(8,128)(2,1)} %fusion.10), calls=%async_computation.2 | async-start | bytes 1048576 | tf_op jit(solution)/shard_map/all_to_all | solution.py:364
  127.4 15.7 %copy-start.32 = (f32[256]{0:T(256)S(1)}, f32[256]{0:T(256)}, u32[]{:S(2)}) copy-start(f32[256]{0:T(256)} %param.35) | copy-start | bytes 3076
  127.5 59.4 %reduce-scatter.5.cloned.1.call-start = ((), (), s32[]{:S(2)}) async-start(), calls=%async_computation.9 | async-start | bytes 2621440 | tf_op jit(solution)/shard_map/reduce_scatter | solution.py:468
  143.7 8.7 %copy-start.43 = (bf16[512,1024]{1,0:T(8,128)(2,1)S(1)}, bf16[512,1024]{1,0:T(8,128)(2,1)}, u32[]{:S(2)}) copy-start(bf16[512,1024]{1,0:T(8,128)(2,1)} %param.36) | copy-start | bytes 3145732
  156.2 63.4 %all-gather.3.cloned.1.call-start = ((), (), s32[]{:S(2)}) async-start(), calls=%async_computation.10 | async-start | bytes 2621440 | tf_op jit(solution)/shard_map/all_gather | solution.py:475
  156.2 2.6 copy-start.37
  158.8 35.7 %copy-start.21 = (f32[256]{0:T(256)S(1)}, f32[256]{0:T(256)}, u32[]{:S(2)}) copy-start(f32[256]{0:T(256)} %param.37) | copy-start | bytes 3076
  195.5 68.7 %reduce-scatter.9.cloned.1.call-start = ((), (), s32[]{:S(2)}) async-start(), calls=%async_computation.12 | async-start | bytes 2621440 | tf_op jit(solution)/shard_map/reduce_scatter | solution.py:468
  195.6 3.3 copy-start.41
  219.6 3.9 copy-start.38
  219.6 3.9 copy-start.46
  223.5 4.0 copy-start.40
  232.6 65.5 %reduce-scatter.7.cloned.1.call-start = ((), (), s32[]{:S(2)}) async-start(), calls=%async_computation.11 | async-start | bytes 2621440 | tf_op jit(solution)/shard_map/reduce_scatter | solution.py:468
  238.5 85.5 %all-gather.5.cloned.1.call-start = ((), (), s32[]{:S(2)}) async-start(), calls=%async_computation.13 | async-start | bytes 2621440 | tf_op jit(solution)/shard_map/all_gather | solution.py:516
  272.3 51.7 %copy-start.44 = (bf16[512,1024]{1,0:T(8,128)(2,1)S(1)}, bf16[512,1024]{1,0:T(8,128)(2,1)}, u32[]{:S(2)}) copy-start(bf16[512,1024]{1,0:T(8,128)(2,1)} %param.36) | copy-start | bytes 3145732
  337.1 20.4 %all-to-all-start.3 = ((bf16[8,256,128]{2,1,0:T(8,128)(2,1)}), bf16[8,256,128]{2,1,0:T(8,128)(2,1)S(1)}, u32[]{:S(2)}, u32[]{:S(2)}) async-start(bf16[8,256,128]{2,1,0:T(8,128)(2,1)} %bitcast.42), calls=%async_computation.6 | async-start | bytes 1048576 | tf_op jit(solution)/shard_map/all_to_all | solution.py:364
  369.7 33.7 %all-to-all-start.4 = ((bf16[8,256,128]{2,1,0:T(8,128)(2,1)}), bf16[8,256,128]{2,1,0:T(8,128)(2,1)S(1)}, u32[]{:S(2)}, u32[]{:S(2)}) async-start(bf16[8,256,128]{2,1,0:T(8,128)(2,1)} %constant_dynamic-update-slice_fusion.4), calls=%async_computation.7 | async-start | bytes 1048576 | tf_op jit(solution)/shard_map/all_to_all | solution.py:364
  373.3 5.1 copy-start.13
  373.3 151.5 %reduce-scatter.11.cloned.1.call-start = ((), (), s32[]{:S(2)}) async-start(), calls=%async_computation.14 | async-start | bytes 2621440 | tf_op jit(solution)/shard_map/reduce_scatter | solution.py:468
  404.4 30.2 %copy-start.25 = (bf16[1024,2]{0,1:T(2,128)(2,1)S(1)}, bf16[1024,2]{0,1:T(2,128)(2,1)}, u32[]{:S(2)}) copy-start(bf16[1024,2]{0,1:T(2,128)(2,1)} %param.28) | copy-start | bytes 12292
  404.4 30.2 %copy-start.27 = (bf16[1024,2]{0,1:T(2,128)(2,1)S(1)}, bf16[1024,2]{0,1:T(2,128)(2,1)}, u32[]{:S(2)}) copy-start(bf16[1024,2]{0,1:T(2,128)(2,1)} %param.27) | copy-start | bytes 12292
  404.4 30.2 %copy-start.34 = (bf16[128]{0:T(256)(128)(2,1)S(1)}, bf16[128]{0:T(256)(128)(2,1)}, u32[]{:S(2)}) copy-start(bf16[128]{0:T(256)(128)(2,1)} %copy-done.33) | copy-start | bytes 772
  432.2 6.2 collective-permute-start.1
  434.6 2.8 copy-start.9
  434.6 3.7 copy-start.19
  448.3 315.0 %all-reduce.11.cloned.1.call-start = ((), (), s32[]{:S(2)}) async-start(), calls=%async_computation.15 | async-start | bytes 17039360 | tf_op jit(solution)/shard_map/psum | solution.py:499
  448.3 13.0 %copy-start.12 = (bf16[4,256,1024]{2,1,0:T(8,128)(2,1)S(1)}, bf16[4,256,1024]{2,1,0:T(8,128)(2,1)}, u32[]{:S(2)}) copy-start(bf16[4,256,1024]{2,1,0:T(8,128)(2,1)} %all-gather.5.cloned.1.call-done) | copy-start | bytes 6291460
  448.3 13.0 %copy-start.15 = (bf16[4,256,512]{2,1,0:T(8,128)(2,1)S(1)}, bf16[4,256,512]{2,1,0:T(8,128)(2,1)}, u32[]{:S(2)}) copy-start(bf16[4,256,512]{2,1,0:T(8,128)(2,1)} %get-tuple-element.48) | copy-start | bytes 3145732
  468.9 3.0 copy-start.39
  475.7 46.2 %copy-start.10 = (bf16[4,256,128]{2,1,0:T(8,128)(2,1)S(1)}, bf16[4,256,128]{2,1,0:T(8,128)(2,1)}, u32[]{:S(2)}) copy-start(bf16[4,256,128]{2,1,0:T(8,128)(2,1)} %copy-done.9) | copy-start | bytes 786436
  521.8 4.8 copy-start.28
  521.8 51.7 %copy-start.6 = (bf16[4,256,256]{2,1,0:T(8,128)(2,1)S(1)}, bf16[4,256,256]{2,1,0:T(8,128)(2,1)}, u32[]{:S(2)}) copy-start(bf16[4,256,256]{2,1,0:T(8,128)(2,1)} %reduce-scatter.9.cloned.1.call-done) | copy-start | bytes 1572868
  521.9 51.7 %copy-start.22 = (f32[256]{0:T(256)S(1)}, f32[256]{0:T(256)}, u32[]{:S(2)}) copy-start(f32[256]{0:T(256)} %param.37) | copy-start | bytes 3076
  763.3 2.8 copy-start.5
  763.3 4.4 copy-start.7
  (15 other events, 24.4 us)
Sparse Core Ops, SparseCore 0:
  156.3 30.5 reduce-scatter.4
  195.6 23.9 all-gather.2
  232.7 31.4 reduce-scatter.8
  266.6 31.4 reduce-scatter.6
  301.2 22.8 all-gather.4
  448.4 32.0 reduce-scatter.10
  486.2 277.0 all-reduce.10

commit v2 on v1

--- a/solution.py
+++ b/solution.py
@@ -348,6 +348,410 @@
     )(*operands)
 
 
+MESH = pl.DeviceIdType.MESH
+
+
+def remote(src, dst, send_sem, recv_sem, device):
+    return pltpu.make_async_remote_copy(
+        src_ref=src, dst_ref=dst, send_sem=send_sem, recv_sem=recv_sem, device_id=device, device_id_type=MESH
+    )
+
+
+def turn_to_row(column, row, col):
+    return jnp.sum(jnp.where(row == col, column, 0.0), axis=0, keepdims=True)
+
+
+def turn_to_column(line, row, col):
+    return jnp.sum(jnp.where(row == col, line, 0.0), axis=1, keepdims=True)
+
+
+def middle_kernel(
+    slots, head_parts, gated, x_shard, out_grad, cot_shard, mask, out_weight, gate_weight, up_weight,
+    down_weight, gain,
+    block_out, normed_out, act_out, up_grad_out, gate_grad_out, mixer_grad_out, residual_grad_out,
+    gated_grad_out, gain_grad_out,
+    whole_part, part, low, from_core, to_line, from_line, residual, inverse, stat_own, stat_in, spread, grad_shard,
+    core_send, core_recv, line_send, line_recv, stat_send, stat_recv,
+    spread_line_send, spread_line_recv, spread_core_send, spread_core_recv,
+):
+    me = lax.axis_index("head")
+    place = lax.axis_index("seq")
+    lines = head_parts // 2
+    core = lax.rem(me, 2)
+    line = me // 2
+    sibling = 2 * line + (1 - core)
+    length, shard = x_shard.shape[1], x_shard.shape[2]
+    width = shard * head_parts
+    row, col = grid_masks(length)
+
+    barrier = pltpu.get_barrier_semaphore()
+    for away in range(1, head_parts):
+        pl.semaphore_signal(
+            barrier, inc=1, device_id=(place, lax.rem(me + away, head_parts)), device_id_type=MESH
+        )
+    pl.semaphore_wait(barrier, head_parts - 1)
+    gain_grad_out[...] = jnp.zeros_like(gain_grad_out)
+
+    def core_copy(kind, s, y):
+        return remote(
+            low.at[kind, s, y], from_core.at[kind, s, y],
+            core_send.at[kind, s, y], core_recv.at[kind, s, y], (place, sibling),
+        )
+
+    def line_copy(kind, s, away):
+        return remote(
+            to_line.at[kind, s, away - 1], from_line.at[kind, s, away - 1],
+            line_send.at[kind, s, away - 1], line_recv.at[kind, s, away - 1],
+            (place, 2 * lax.rem(line + away, lines) + core),
+        )
+
+    def stat_copy(kind, s, away):
+        return remote(
+            stat_own.at[kind, s], stat_in.at[kind, s, away - 1],
+            stat_send.at[kind, s, away - 1], stat_recv.at[kind, s, away - 1],
+            (place, lax.rem(me + away, head_parts)),
+        )
+
+    def spread_line_copy(kind, s, away):
+        return remote(
+            spread.at[kind, s, me], spread.at[kind, s, me],
+            spread_line_send.at[kind, s, away - 1], spread_line_recv.at[kind, s, away - 1],
+            (place, 2 * lax.rem(line + away, lines) + core),
+        )
+
+    def spread_core_copy(kind, s, away):
+        y = lax.rem(line + away, lines)
+        return remote(
+            spread.at[kind, s, 2 * y + core], spread.at[kind, s, 2 * y + core],
+            spread_core_send.at[kind, s, away], spread_core_recv.at[kind, s, away], (place, sibling),
+        )
+
+    def spread_core_arrival(kind, s, away):
+        y = lax.rem(line + away, lines)
+        return remote(
+            spread.at[kind, s, 2 * y + (1 - core)], spread.at[kind, s, 2 * y + (1 - core)],
+            spread_core_send.at[kind, s, away], spread_core_recv.at[kind, s, away], (place, sibling),
+        )
+
+    def spread_line_arrival(kind, s, away):
+        y = lax.rem(line + lines - away, lines)
+        return remote(
+            spread.at[kind, s, 2 * y + core], spread.at[kind, s, 2 * y + core],
+            spread_line_send.at[kind, s, away - 1], spread_line_recv.at[kind, s, away - 1],
+            (place, 2 * y + core),
+        )
+
+    def send_part(kind, s, value):
+        for j in range(head_parts):
+            whole_part[j] = value[:, j * shard : (j + 1) * shard]
+        for y in range(lines):
+            low[kind, s, y] = whole_part[2 * y + (1 - core)].astype(BF16)
+            core_copy(kind, s, y).start()
+            part[kind, s, y] = whole_part[2 * y + core]
+
+    def join_core(kind, s):
+        for y in range(lines):
+            core_copy(kind, s, y).wait_recv()
+        for away in range(1, lines):
+            y = lax.rem(line + away, lines)
+            joined = part[kind, s, y] + from_core[kind, s, y].astype(F32)
+            to_line[kind, s, away - 1] = joined.astype(BF16)
+            line_copy(kind, s, away).start()
+        part[kind, s, line] = part[kind, s, line] + from_core[kind, s, line].astype(F32)
+
+    def join_line(kind, s):
+        total = part[kind, s, line]
+        for away in range(1, lines):
+            line_copy(kind, s, away).wait_recv()
+            total = total + from_line[kind, s, away - 1].astype(F32)
+        return total
+
+    def send_stat(kind, s, column):
+        stat_own[kind, s] = jnp.broadcast_to(turn_to_row(column, row, col), (8, length))
+        for away in range(1, head_parts):
+            stat_copy(kind, s, away).start()
+
+    def join_stat(kind, s):
+        total = stat_own[kind, s]
+        for away in range(1, head_parts):
+            stat_copy(kind, s, away).wait_recv()
+            total = total + stat_in[kind, s, away - 1]
+        return turn_to_column(total[0:1, :], row, col)
+
+    def send_spread(kind, s, value):
+        spread[kind, s, me] = value
+        for away in range(1, lines):
+            spread_line_copy(kind, s, away).start()
+        spread_core_copy(kind, s, 0).start()
+
+    def pass_spread(kind, s):
+        for away in range(1, lines):
+            spread_line_arrival(kind, s, lines - away).wait_recv()
+            spread_core_copy(kind, s, away).start()
+
+    def take_spread(kind, s):
+        for away in range(lines):
+            spread_core_arrival(kind, s, away).wait_recv()
+        return jnp.concatenate([spread[kind, s, j] for j in range(head_parts)], axis=1)
+
+    def attention(s):
+        send_part(0, s, raw(gated[s], out_weight[...], NN))
+
+    def rows_in(s):
+        total = x_shard[s].astype(F32) + mask[s][:, 0:1] * join_line(0, s)
+        residual[s] = total
+        send_stat(0, s, jnp.sum(total * total, axis=1, keepdims=True))
+
+    def norm_second(s):
+        inv = lax.rsqrt(join_stat(0, s) / width + NORM_EPSILON)
+        inverse[s] = jnp.broadcast_to(inv, (length, LANES))
+        send_spread(0, s, (residual[s] * inv * gain[0:1, :]).astype(BF16))
+
+    def swiglu(s):
+        normed = take_spread(0, s)
+        normed_out[s] = normed
+        gate_values = raw(normed, gate_weight[...], NN)
+        up_values = raw(normed, up_weight[...], NN)
+        act_grad = raw(out_grad[s], down_weight[...], NT)
+        sig = sigmoid(gate_values)
+        silu = gate_values * sig
+        act_out[s] = (silu * up_values).astype(BF16)
+        up_grad = (act_grad * silu).astype(BF16)
+        gate_grad = (act_grad * up_values * sig * (1.0 + gate_values * (1.0 - sig))).astype(BF16)
+        up_grad_out[s] = up_grad
+        gate_grad_out[s] = gate_grad
+        send_part(1, s, raw(up_grad, up_weight[...], NT) + raw(gate_grad, gate_weight[...], NT))
+
+    def swiglu_out(s):
+        send_part(2, s, raw(act_out[s], down_weight[...], NN))
+
+    def block_rows(s):
+        block_out[s] = (residual[s] + mask[s][:, 0:1] * join_line(2, s)).astype(BF16)
+
+    def norm_back(s):
+        grad = join_line(1, s)
+        inv = inverse[s][:, 0:1]
+        gain_grad_out[0:1, :] += jnp.sum(grad * residual[s] * inv, axis=0, keepdims=True)
+        weighted = grad * gain[0:1, :]
+        grad_shard[s] = weighted
+        send_stat(1, s, jnp.sum(weighted * residual[s], axis=1, keepdims=True))
+
+    def residual_back(s):
+        stat = join_stat(1, s) / width
+        inv = inverse[s][:, 0:1]
+        grad = cot_shard[s].astype(F32) + inv * (grad_shard[s] - residual[s] * (inv * inv * stat))
+        residual_grad_out[s] = grad
+        send_spread(1, s, (mask[s][:, 0:1] * grad).astype(BF16))
+
+    def mixer_rows(s):
+        grad = take_spread(1, s)
+        mixer_grad_out[s] = grad
+        gated_grad_out[s] = raw(grad, out_weight[...], NT)
+
+    stages = (
+        (10, mixer_rows),
+        (9, functools.partial(pass_spread, 1)),
+        (8, residual_back),
+        (7, norm_back),
+        (6, functools.partial(join_core, 1)),
+        (8, block_rows),
+        (7, functools.partial(join_core, 2)),
+        (4, functools.partial(pass_spread, 0)),
+        (3, norm_second),
+        (2, rows_in),
+        (1, functools.partial(join_core, 0)),
+        (0, attention),
+        (5, swiglu),
+        (6, swiglu_out),
+    )
+
+    def step(t, carry):
+        for offset, stage in stages:
+            s = t - offset
+
+            @pl.when((s >= 0) & (s < slots))
+            def _(stage=stage, s=s):
+                stage(s)
+
+        return carry
+
+    lax.fori_loop(0, slots + 10, step, 0)
+
+    def drain(s, carry):
+        for kind in range(3):
+            for y in range(lines):
+                core_copy(kind, s, y).wait_send()
+            for away in range(1, lines):
+                line_copy(kind, s, away).wait_send()
+        for kind in range(2):
+            for away in range(1, head_parts):
+                stat_copy(kind, s, away).wait_send()
+            for away in range(1, lines):
+                spread_line_copy(kind, s, away).wait_send()
+            for away in range(lines):
+                spread_core_copy(kind, s, away).wait_send()
+        return carry
+
+    lax.fori_loop(0, slots, drain, 0)
+
+
+def middle_call(
+    head_parts, gated, x_shard, out_grad, cot_shard, mask, out_weight, gate_weight, up_weight, down_weight, gain
+):
+    slots, length, shard = x_shard.shape
+    width = shard * head_parts
+    hidden = gate_weight.shape[1]
+    lines = head_parts // 2
+    sds = jax.ShapeDtypeStruct
+    vmem = pl.BlockSpec(memory_space=pltpu.VMEM)
+    dma = pltpu.SemaphoreType.DMA
+    outs = (
+        sds((slots, length, shard), BF16), sds((slots, length, width), BF16),
+        sds((slots, length, hidden), BF16), sds((slots, length, hidden), BF16),
+        sds((slots, length, hidden), BF16), sds((slots, length, width), BF16),
+        sds((slots, length, shard), F32), sds((slots, length, gated.shape[2]), F32), sds((8, shard), F32),
+    )
+    return pl.pallas_call(
+        functools.partial(middle_kernel, slots, head_parts),
+        in_specs=[vmem] * 10,
+        out_specs=[vmem] * len(outs),
+        out_shape=outs,
+        scratch_shapes=[
+            pltpu.VMEM((head_parts, length, shard), F32),
+            pltpu.VMEM((3, slots, lines, length, shard), F32),
+            pltpu.VMEM((3, slots, lines, length, shard), BF16),
+            pltpu.VMEM((3, slots, lines, length, shard), BF16),
+            pltpu.VMEM((3, slots, lines - 1, length, shard), BF16),
+            pltpu.VMEM((3, slots, lines - 1, length, shard), BF16),
+            pltpu.VMEM((slots, length, shard), F32),
+            pltpu.VMEM((slots, length, LANES), F32),
+            pltpu.VMEM((2, slots, 8, length), F32),
+            pltpu.VMEM((2, slots, head_parts - 1, 8, length), F32),
+            pltpu.VMEM((2, slots, head_parts, length, shard), BF16),
+            pltpu.VMEM((slots, length, shard), F32),
+            dma((3, slots, lines)), dma((3, slots, lines)),
+            dma((3, slots, lines - 1)), dma((3, slots, lines - 1)),
+            dma((2, slots, head_parts - 1)), dma((2, slots, head_parts - 1)),
+            dma((2, slots, lines - 1)), dma((2, slots, lines - 1)),
+            dma((2, slots, lines)), dma((2, slots, lines)),
+        ],
+        compiler_params=pltpu.CompilerParams(
+            collective_id=0, has_side_effects=True, vmem_limit_bytes=VMEM_LIMIT
+        ),
+        cost_estimate=pl.CostEstimate(flops=12 * 10**9, bytes_accessed=30 * 10**6, transcendentals=0),
+    )(gated, x_shard, out_grad, cot_shard, mask, out_weight, gate_weight, up_weight, down_weight, gain)
+
+
+def ring_kernel(parts, count, *refs):
+    ins, outs, held = refs[:count], refs[count : 2 * count], refs[2 * count : 3 * count]
+    send, recv, spread_send, spread_recv = refs[3 * count :]
+    index = lax.axis_index("seq")
+    other = lax.axis_index("head")
+    side = lax.rem(index, 2)
+    level = index // 2
+    levels = parts // 2
+    position = jnp.where(side == 1, level, parts - 1 - level)
+    up = jnp.where(side == 1, jnp.where(level == levels - 1, index - 1, index + 2),
+                   jnp.where(level == 0, index + 1, index - 2))
+    down = jnp.where(side == 1, jnp.where(level == 0, index - 1, index - 2),
+                     jnp.where(level == levels - 1, index + 1, index + 2))
+    targets = (up, down)
+    barrier = pltpu.get_barrier_semaphore()
+    for target in targets:
+        pl.semaphore_signal(barrier, inc=1, device_id=(target, other), device_id_type=MESH)
+
+    def rows_of(a, way, chunk):
+        size = ins[a].shape[0] // (2 * parts)
+        return pl.ds(pl.multiple_of((chunk * 2 + way) * size, size), size)
+
+    def chunk_at(way, step):
+        if way == 0:
+            return lax.rem(position - step + 2 * parts, parts)
+        return lax.rem(position + step + 2 * parts, parts)
+
+    def sum_copy(a, way, step):
+        return remote(
+            held[a].at[way, step], held[a].at[way, step + 1], send.at[a, way], recv.at[a, way, step],
+            (targets[way], other),
+        )
+
+    def spread_copy(a, way, step):
+        block = rows_of(a, way, chunk_at(way, step - 1))
+        return remote(
+            outs[a].at[block, :], outs[a].at[block, :], spread_send.at[a, way], spread_recv.at[a, way, step],
+            (targets[way], other),
+        )
+
+    def spread_arrival(a, way, step):
+        block = rows_of(a, way, chunk_at(way, step))
+        return remote(
+            outs[a].at[block, :], outs[a].at[block, :], spread_send.at[a, way], spread_recv.at[a, way, step],
+            (targets[way], other),
+        )
+
+    lanes = [(a, way) for a in range(count) for way in range(2)]
+    for a, way in lanes:
+        held[a][way, 0] = ins[a][rows_of(a, way, chunk_at(way, 0)), :]
+    pl.semaphore_wait(barrier, 2)
+    for a, way in lanes:
+        sum_copy(a, way, 0).start()
+
+    def add(step, a, way):
+        sum_copy(a, way, step).wait_recv()
+        mine = ins[a][rows_of(a, way, chunk_at(way, step + 1)), :].astype(F32)
+        return (held[a][way, step + 1].astype(F32) + mine).astype(BF16)
+
+    def one(step, carry):
+        for a, way in lanes:
+            held[a][way, step + 1] = add(step, a, way)
+            sum_copy(a, way, step).wait_send()
+            sum_copy(a, way, step + 1).start()
+        return carry
+
+    lax.fori_loop(0, parts - 2, one, 0)
+    last = parts - 2
+    for a, way in lanes:
+        outs[a][rows_of(a, way, chunk_at(way, parts - 1)), :] = add(last, a, way)
+        sum_copy(a, way, last).wait_send()
+        spread_copy(a, way, 0).start()
+
+    def pass_on(step, carry):
+        for a, way in lanes:
+            spread_arrival(a, way, step).wait_recv()
+            spread_copy(a, way, step).wait_send()
+            spread_copy(a, way, step + 1).start()
+        return carry
+
+    lax.fori_loop(0, parts - 2, pass_on, 0)
+    for a, way in lanes:
+        spread_arrival(a, way, last).wait_recv()
+        spread_copy(a, way, last).wait_send()
+
+
+def ring_sum(parts, arrays):
+    count = len(arrays)
+    unit = 32 * parts
+    padded = [jnp.pad(a, ((0, -a.shape[0] % unit), (0, 0))) for a in arrays]
+    vmem = pl.BlockSpec(memory_space=pltpu.VMEM)
+    dma = pltpu.SemaphoreType.DMA
+    sds = jax.ShapeDtypeStruct
+    sums = pl.pallas_call(
+        functools.partial(ring_kernel, parts, count),
+        in_specs=[vmem] * count,
+        out_specs=[vmem] * count,
+        out_shape=[sds(a.shape, BF16) for a in padded],
+        scratch_shapes=[
+            pltpu.VMEM((2, parts, a.shape[0] // (2 * parts), a.shape[1]), BF16) for a in padded
+        ]
+        + [dma((count, 2)), dma((count, 2, parts - 1)), dma((count, 2)), dma((count, 2, parts - 1))],
+        compiler_params=pltpu.CompilerParams(
+            collective_id=1, has_side_effects=True, vmem_limit_bytes=VMEM_LIMIT
+        ),
+        cost_estimate=pl.CostEstimate(flops=10**8, bytes_accessed=500 * 10**6, transcendentals=0),
+    )(*padded)
+    return [t[: a.shape[0]] for t, a in zip(sums, arrays)]
+
+
 def shifted(block, axis, distance):
     devices = range(lax.axis_size(axis))
     route = [(i - distance, i) for i in devices if i - distance in devices]
@@ -467,62 +871,35 @@
         low = part.astype(BF16).reshape(slots, segment, width)
         return lax.psum_scatter(low, "head", scatter_dimension=2, tiled=True).astype(F32)
 
-    attention_shard = scatter_sum(project(gated_low, output_weight))
-    residual = x_shard + mask * attention_shard
-    square_sum = lax.psum(jnp.sum(residual * residual, axis=-1, keepdims=True), "head")
-    inv_second = lax.rsqrt(square_sum / width + NORM_EPSILON)
-    normed_shard = (residual * inv_second * mixed_gain).astype(BF16)
-    normed_second = lax.all_gather(normed_shard, "head", axis=2, tiled=True).reshape(rows, width)
-    gate_values = project(normed_second, swiglu_gate)
-    upward_values = project(normed_second, swiglu_up)
-    sigmoid_gate = jax.nn.sigmoid(gate_values)
-    silu_gate = gate_values * sigmoid_gate
-    activation = (silu_gate * upward_values).astype(BF16)
-    out_grad = jnp.where(mask > 0, cotangent, jnp.zeros_like(cotangent)).reshape(rows, width)
-    activation_grad = jnp.dot(out_grad, swiglu_down.T, preferred_element_type=F32)
-    upward_grad = (activation_grad * silu_gate).astype(BF16)
-    gate_grad = (
-        activation_grad * upward_values * sigmoid_gate * (1.0 + gate_values * (1.0 - sigmoid_gate))
-    ).astype(BF16)
-    normed_part = jnp.dot(upward_grad, swiglu_up.T, preferred_element_type=F32) + jnp.dot(
-        gate_grad, swiglu_gate.T, preferred_element_type=F32
-    )
-    normed_grad = scatter_sum(normed_part)
-    swiglu_shard = scatter_sum(project(activation, swiglu_down))
-    block_out = (residual + mask * swiglu_shard).astype(BF16)
-    swiglu_down_grad = project(activation.T, out_grad)
-    swiglu_up_grad = project(normed_second.T, upward_grad)
-    swiglu_gate_grad = project(normed_second.T, gate_grad)
-
-    def sum_low(parts):
-        flat = jnp.concatenate([p.astype(BF16).reshape(-1, LANES) for p in parts], axis=0)
-        total = lax.psum(flat, "seq")
-        out, at = [], 0
-        for p in parts:
-            size = p.size // LANES
-            out.append(total[at : at + size].reshape(p.shape).astype(F32))
-            at += size
-        return out
-
-    swiglu_sums = sum_low((swiglu_down_grad, swiglu_up_grad, swiglu_gate_grad))
-    mixed_gain_grad = jnp.sum(normed_grad * residual * inv_second, axis=(0, 1))
-    weighted_second = normed_grad * mixed_gain
-    second_stat = lax.psum(jnp.sum(weighted_second * residual, axis=-1, keepdims=True), "head")
-    out_shard = lax.dynamic_slice_in_dim(cotangent, head_start, shard, 2).astype(F32)
-    residual_grad = out_shard + inv_second * (
-        weighted_second - residual * inv_second * inv_second * second_stat / width
-    )
-    mixer_grad_low = (mask * residual_grad).astype(BF16)
-    mixer_grad = lax.all_gather(mixer_grad_low, "head", axis=2, tiled=True).reshape(rows, width)
-    gated_grad = jnp.dot(mixer_grad, output_weight.T, preferred_element_type=F32)
-    output_weight_grad = project(gated_low.T, mixer_grad)
+    out_grad = jnp.where(mask > 0, cotangent, jnp.zeros_like(cotangent))
+    cot_shard = lax.dynamic_slice_in_dim(cotangent, head_start, shard, 2)
+    (
+        block_out, normed_second, activation, upward_grad, gate_grad, mixer_grad, residual_grad, gated_grad,
+        mixed_gain_part,
+    ) = middle_call(
+        head_parts, gated, lax.dynamic_slice_in_dim(hidden_in, head_start, shard, 2), out_grad, cot_shard,
+        jnp.broadcast_to(mask, (slots, segment, LANES)), output_weight, swiglu_gate, swiglu_up, swiglu_down,
+        jnp.broadcast_to(mixed_gain[None, :], (8, shard)),
+    )
+    gated_grad = gated_grad.reshape(rows, heads * value_dim)
+
+    def flat(a):
+        return a.reshape(rows, a.shape[2])
+
+    def weight_grad(left, right):
+        return lax.dot_general(left, right, TN, preferred_element_type=F32).astype(BF16)
+
+    normed_second = flat(normed_second)
+    swiglu_down_grad = weight_grad(flat(activation), flat(out_grad))
+    swiglu_grads = jnp.concatenate(
+        [weight_grad(normed_second, flat(upward_grad)), weight_grad(normed_second, flat(gate_grad))], axis=1
+    )
+    output_weight_grad = weight_grad(gated_low, flat(mixer_grad))
 
     mixer_out_grad, gate_low, gain_part, shift_grads = gate_backward_call(
         heads, slots, segment, value_dim, key_dim, gated_grad, mixer, gate_pre, eff, gain_row
     )
     gate_low = gate_low.reshape(rows, heads * value_dim)
-    gate_weight_grad = project(normed_first.T, gate_low)
-    middle_sums = sum_low((output_weight_grad, gate_weight_grad))
 
     all_grads = exchange(
         to_units(shift_grads.astype(BF16).reshape(pairs, value_dim, key_dim), units), "seq"
@@ -563,9 +940,6 @@
         + jnp.dot(ab_low, ab_weight.T, preferred_element_type=F32)
     )
     first_sum = scatter_sum(first_part)
-    pre_weight_grad = project(normed_first.T, pre_low)
-    ab_weight_grad = project(normed_first.T, ab_low)[:, : 2 * heads]
-    (pre_sums,) = sum_low((pre_weight_grad,))
     weighted_first = first_sum * lax.dynamic_slice_in_dim(input_gain, head_start, shard, 0)
     first_stat = lax.psum(jnp.sum(weighted_first * x_shard, axis=-1, keepdims=True), "head")
     input_grad = (
@@ -573,37 +947,58 @@
         + inv_first * (weighted_first - x_shard * inv_first * inv_first * first_stat / width)
     )
     input_gain_grad = jnp.sum(first_sum * x_shard * inv_first, axis=(0, 1))
-    gain_sum = lax.psum(gain_part[0], ("head", "seq"))
+    small_rows = jnp.concatenate(
+        [
+            taps_grad[:taps].reshape(-1), gain_part[0], lane_grad[:2].reshape(-1), mixed_gain_part[0],
+            lax.dot_general(ab_low, normed_first, TN, preferred_element_type=F32)[: 2 * heads].reshape(-1),
+        ]
+    )
+    sizes = (taps * channels, value_dim, 2 * LANES, shard, 2 * heads * width)
+    small_rows = jnp.pad(small_rows, (0, -small_rows.shape[0] % width)).reshape(-1, width)
+    first_grads = jnp.concatenate(
+        [weight_grad(normed_first, pre_low), weight_grad(normed_first, gate_low)], axis=1
+    )
+    line_grads = jnp.concatenate([swiglu_down_grad, output_weight_grad, small_rows.astype(BF16)], axis=0)
+    swiglu_sum, first_grad_sum, line_sum = ring_sum(seq_parts, (swiglu_grads, first_grads, line_grads))
+    hidden = swiglu_gate.shape[1]
+    small_sum = line_sum[hidden + heads * value_dim :].reshape(-1).astype(F32)
+    pieces, at = [], 0
+    for size in sizes:
+        pieces.append(small_sum[at : at + size])
+        at += size
+    taps_sum = pieces[0].reshape(taps, channels)
+    lane_sum = pieces[2].reshape(2, LANES)
+    ab_sum = pieces[4].reshape(2 * heads, width).T
+    input_gain_sum = lax.psum(input_gain_grad, "seq")
+    gain_sum = lax.psum(pieces[1], "head")
     value_share = value_dim // head_parts
     output_gain_grad = lax.dynamic_slice_in_dim(
         gain_sum, lax.axis_index("head") * value_share, value_share, 0
     )
-    small = lax.psum(
-        (input_gain_grad, ab_weight_grad, lane_grad[0, :heads], lane_grad[1, :heads], taps_grad[:taps], mixed_gain_grad),
-        "seq",
-    )
-    taps_sum = small[4]
+    wide = first_grad_sum.astype(F32)
+    lines = line_sum.astype(F32)
+    both = swiglu_sum.astype(F32)
     return (
         block_out,
         input_grad,
-        small[0],
-        pre_sums[:, :split_key],
-        pre_sums[:, split_key : 2 * split_key],
-        pre_sums[:, 2 * split_key :],
-        small[1][:, :heads],
-        small[1][:, heads:],
-        small[2],
-        small[3],
+        input_gain_sum,
+        wide[:, :split_key],
+        wide[:, split_key : 2 * split_key],
+        wide[:, 2 * split_key : channels],
+        ab_sum[:, :heads],
+        ab_sum[:, heads:],
+        lane_sum[0, :heads],
+        lane_sum[1, :heads],
         taps_sum[:, :split_key],
         taps_sum[:, split_key : 2 * split_key],
         taps_sum[:, 2 * split_key :],
-        middle_sums[1],
+        wide[:, channels:],
         output_gain_grad,
-        middle_sums[0],
-        small[5],
-        swiglu_sums[2],
-        swiglu_sums[1],
-        swiglu_sums[0],
+        lines[hidden : hidden + heads * value_dim],
+        pieces[3],
+        both[:, hidden:],
+        both[:, :hidden],
+        lines[:hidden],
     )
 
 

time: 813 us -> 591 us (0.73)
  waiting for transfers between devices: 345 us -> 24.5 us
  Pallas kernels: 82.5 us -> 336 us
  blocking collectives: 102 us -> 26.2 us
  matrix products: 102 us -> 52.9 us
  other arithmetic: 62.9 us -> 45.7 us
  local copies, waits for them, and re-layouts: 62.9 us -> 50.4 us
    pallas_call x0 -> x2, Pallas kernels: none -> 254 us  [the longest x1 173 us: ring_sum(): pl.pallas_call(functools.partial(ring_kernel, parts, count), in_specs=[vm...]
    psum x1 -> x0, waiting for transfers between devices: 187 us -> none  [sum_low(): total = lax.psum(flat, 'seq')]
    reduce_scatter x4 -> x1, waiting for transfers between devices: 79.4 us -> 0.01 us  [scatter_sum(): lax.psum_scatter(low, 'head', scatter_dimension=2, tiled=True).astype(F32)]
    psum x4 -> x1, blocking collectives: 95.8 us -> 20.4 us  [per_device(): input_gain_sum = lax.psum(input_gain_grad, 'seq')]
    dot_general x15 -> x4, matrix products: 53.4 us -> 9.03 us  [project(): return jnp.dot(x, weight, preferred_element_type=F32)]
    all_gather x2 -> x0, waiting for transfers between devices: 40.4 us -> none  [the longest x1 23 us: per_device(): lax.all_gather(mixer_grad_low, 'head', axis=2, tiled=True)]
    all_to_all x5, waiting for transfers between devices: 37.7 us -> 23.6 us  [exchange(): return lax.all_to_all(parts, axis, 0, 0, tiled=True)]
    convert_element_type x7 -> x5, local copies, waits for them, and re-layouts: 18.6 us -> 5.17 us  [the longest x2 5.12 us: weight_grad(): lax.dot_general(left, right, TN, preferred_element_type=F32).astype(BF16)]
  transfers between devices with their start and end apart: 14 -> 8, of which waited for: 11 -> 5; matrix products, arithmetic and copies ran while one was open for 14% -> 17% of each run, Pallas kernels for 0% -> 30%
where the time goes in v2:
time: 591 us; the launch traced here: 581 us
  Pallas kernels  336 us (57%)
  matrix products  52.9 us (9%)
  local copies, waits for them, and re-layouts  50.4 us (9%)
  other arithmetic  45.7 us (8%)
  starting transfers between devices  30.1 us (5%)
  blocking collectives  26.2 us (4%)
  waiting for transfers between devices  24.5 us (4%)
  between operations  15.1 us (3%)
    pallas_call x1, Pallas kernels, ring_sum(): pl.pallas_call(functools.partial(ring_kernel, parts, count), in_specs=[vm...  173 us
    pallas_call x1, Pallas kernels, middle_call(): pl.pallas_call(functools.partial(middle_kernel, slots, head_parts), in_sp...  81.3 us
    pallas_call x3, Pallas kernels, run_slots(): pl.pallas_call(body, grid=(slots,), in_specs=specs, out_specs=[by_slot(o....  75.4 us
    all_to_all x5, waiting for transfers between devices, exchange(): return lax.all_to_all(parts, axis, 0, 0, tiled=True)  23.6 us
    all_to_all x5, starting transfers between devices, exchange(): return lax.all_to_all(parts, axis, 0, 0, tiled=True)  23.5 us
    psum x1, blocking collectives, per_device(): input_gain_sum = lax.psum(input_gain_grad, 'seq')  20.4 us
    dot_general x6, matrix products, weight_grad(): lax.dot_general(left, right, TN, preferred_element_type=F32).astype(BF16)  19.4 us
    unnamed x85, local copies, waits for them, and re-layouts  17.3 us
  transfers between devices with their start and end apart: 8, of which 5 were waited for; matrix products, arithmetic and copies ran while one was open for 17% of the time, Pallas kernels for 30%

profile of v2, /device:TPU:0, one launch (start us, length us, event | category | flops | bytes accessed | tf_op | source)
XLA Modules:
  0.0 581.0 jit_solution(8924590522092070629)
XLA Ops:
  8.2 4.8 collective-permute-start
  13.1 2.1 multiply_reduce_fusion
  18.5 3.7 convolution_convert_fusion
  29.1 40.2 %shard_map.356 = (bf16[4,2,256,128]{3,2,1,0:T(8,128)(2,1)}, bf16[4,2,256,128]{3,2,1,0:T(8,128)(2,1)}, bf16[4,2,256,256]{3,2,1,0:T(8,128)(2,1)}, f32[4,2,256,256]...) custom-call(bf16[4,256,1024]{2,1,0:T(8,128)(2,1)} %bitcast.223, ...), custom_call_target="tpu_custom_call" | custom-call | tf_op jit(solution)/shard_map/pallas_call | solution.py:340
  69.4 2.1 convert_element_type.135
  71.5 5.4 all-to-all-start.1
  76.9 2.4 convert_element_type.128
  79.3 2.6 copy.79.gate_weight
  81.9 2.6 copy.80.up_weight
  86.3 4.8 all-to-all-done.1
  91.2 3.6 all-to-all-start
  99.3 4.4 all-to-all-done
  109.6 4.2 all-to-all-start.2
  113.8 3.3 broadcast_select_fusion.out_grad
  117.1 2.6 fusion.18.gate_ref
  119.7 7.8 %all-to-all-done.2 = bf16[8,256,128]{2,1,0:T(8,128)(2,1)} async-done(((bf16[8,256,128]{2,1,0:T(8,128)(2,1)}), bf16[8,256,128]{2,1,0:T(8,128)(2,1)}, u32[]{:S(2)}, u32[]{:S(2)}) %all-to-all-start.2) | async-done | bytes 524320 | tf_op jit(solution)/shard_map/all_to_all | solution.py:768
  127.4 2.1 convert.115.state_ref
  130.2 8.5 %shard_map.357 = (f32[4,2,256,256]{3,2,1,0:T(8,128)}, f32[4,2,256,256]{3,2,1,0:T(8,128)}, bf16[4,256,512]{2,1,0:T(8,128)(2,1)}) custom-call(bf16[4,2,256,128]{3,2,1,0:T(8,128)(2,1)} %get-tuple-element.54.query_ref, bf16[4,2,256,128]{3,2,1,0:T(8,128)(2,1)} %get-tuple-element.55.key_ref, f32[4,256,128]{2,1,0:T(8,128)} %copy.77.ab_ref, ...), custom_call_target="tpu_custom_call" | custom-call | tf_op jit(solution)/shard_map/pallas_call | solution.py:340
  140.3 81.3 %shard_map.358 = (bf16[4,256,256]{2,1,0:T(8,128)(2,1)}, bf16[4,256,1024]{2,1,0:T(8,128)(2,1)}, bf16[4,256,704]{2,1,0:T(8,128)(2,1)}, bf16[4,256,704]{2,1,0:T(8,1...) custom-call(bf16[4,256,512]{2,1,0:T(8,128)(2,1)} %get-tuple-element., ...), custom_call_target="tpu_custom_call" | custom-call | flops 12000000000 | bytes 30000000 | tf_op jit(solution)/shard_map/pallas_call | solution.py:614
  221.6 6.9 %shard_map.359 = (f32[4,2,256,256]{3,2,1,0:T(8,128)}, bf16[4,256,512]{2,1,0:T(8,128)(2,1)}, f32[8,256]{1,0:T(8,128)}, f32[4,2,256,128]{3,2,1,0:T(8,128)}) custom-call(f32[4,256,512]{2,1,0:T(8,128)} %get-tuple-element.66.gated_grad_ref, f32[4,2,256,256]{3,2,1,0:T(8,128)} %get-tuple-element.67.mixer_ref, f32[4,256,512]{2,1,0:T(8,128)} %fusion.18.gate_ref, ...), custom_call_target="tpu_custom_call" | custom-call | tf_op jit(solution)/shard_map/pallas_call | solution.py:1014
  228.5 2.1 convert_element_type.138
  230.6 4.3 all-to-all-start.3
  234.9 4.8 bitcast_convert_fusion.3
  239.8 2.6 copy.84
  242.4 4.8 bitcast_convert_fusion.2
  247.2 2.6 copy.85
  249.8 4.5 pad_maximum_fusion.1.refs_0_
  255.0 2.2 bitcast_convert_fusion.4
  257.2 2.3 bitcast_convert_fusion.5
  267.3 6.0 %all-to-all-start.4 = ((bf16[8,256,128]{2,1,0:T(8,128)(2,1)}), bf16[8,256,128]{2,1,0:T(8,128)(2,1)}, u32[]{:S(2)}, u32[]{:S(2)}) async-start(bf16[8,256,128]{2,1,0:T(8,128)(2,1)} %constant_dynamic-update-slice_fusion.4), calls=%async_computation.4 | async-start | bytes 1048576 | tf_op jit(solution)/shard_map/all_to_all | solution.py:768
  274.3 4.7 fusion.52
  279.0 2.8 bitcast_convert_fusion.1
  281.8 6.6 %all-to-all-done.4 = bf16[8,256,128]{2,1,0:T(8,128)(2,1)} async-done(((bf16[8,256,128]{2,1,0:T(8,128)(2,1)}), bf16[8,256,128]{2,1,0:T(8,128)(2,1)}, u32[]{:S(2)}, u32[]{:S(2)}) %all-to-all-start.4) | async-done | bytes 524320 | tf_op jit(solution)/shard_map/all_to_all | solution.py:768
  288.4 2.1 convert.116.state_grad_ref
  290.5 26.6 %shard_map.360 = (bf16[4,256,1024]{2,1,0:T(8,128)(2,1)}, f32[4,8,1024]{2,1,0:T(8,128)}, f32[4,8,1024]{2,1,0:T(8,128)}, f32[4,256,128]{2,1,0:T(8,128)}, f32[8,1024]{1,0:T(8,128)}, /*index=5*/f32[8,128]{1,0:T(8,128)}) custom-call(bf16[4,256,1024]{2,1,0:T(8,128)(2,1)} %bitcast.224, f32[4,8,1024]{2,1,0:T(8,128)} %pad_convert_fusion.rim_ref, ...), custom_call_target="tpu_custom_call" | custom-call | tf_op jit(solution)/shard_map/pallas_call | solution.py:340
  321.8 2.8 fusion.20
  328.0 8.4 %add_convert_fusion = bf16[1024,1024]{1,0:T(8,128)(2,1)} fusion(f32[1024,1024]{1,0:T(8,128)} %fusion.20, f32[1024,1024]{1,0:T(8,128)} %fusion.52, bf16[1024,1024]{1,0:T(8,128)(2,1)} %bitcast.232, bf16[1024,1024]{1,0:T(8,128)(2,1)} %copy-done.8), kind=kOutput, calls=%fused_computation.5 | convolution fusion | flops 2150629376 | bytes 14680064 | tf_op jit(solution)/shard_map/dot_general | solution.py:938
  337.6 2.9 fusion.4.refs_2_
  340.4 2.4 bitcast_convert_fusion
  344.8 172.6 %shard_map.361 = (bf16[1024,1408]{1,0:T(8,128)(2,1)}, bf16[1024,1536]{1,0:T(8,128)(2,1)}, bf16[1280,1024]{1,0:T(8,128)(2,1)}) custom-call(bf16[1024,1408]{1,0:T(8,128)(2,1)} %pad_maximum_fusion.1.refs_0_, bf16[1024,1536]{1,0:T(8,128)(2,1)} %pad_maximum_fusion.refs_1_, bf16[1280,1024]{1,0:T(8,128)(2,1)} %fusion.4.refs_2_), custom_call_target="tpu_custom_call" | custom-call | flops 100000000 | bytes 500000000 | tf_op jit(solution)/shard_map/pallas_call | solution.py:738
  517.4 2.3 slice_convert_fusion
  524.6 3.4 fusion.48
  528.0 3.4 copy.93
  531.4 3.6 copy.94
  538.8 2.6 fusion.46
  543.3 20.4 %psum.22 = f32[256]{0:T(256)} all-reduce(f32[256]{0:T(256)S(1)} %get-tuple-element.148), channel_id=1, replica_groups=mesh['seq'=8,'head'=4] {'seq'}, use_global_device_ids=true, to_apply=%region_6.7 | all-reduce | flops 256 | bytes 2048 | tf_op jit(solution)/shard_map/psum | solution.py:972
  563.7 5.7 all-reduce.9
  570.1 2.8 fusion.15
  (170 shorter events, 58.2 us)
Async XLA Ops:
  7.2 109.9 %copy-start = (bf16[1024,512]{1,0:T(8,128)(2,1)S(1)}, bf16[1024,512]{1,0:T(8,128)(2,1)}, u32[]{:S(2)}) copy-start(bf16[1024,512]{1,0:T(8,128)(2,1)} %param.34) | copy-start | bytes 3145732
  7.2 8.0 %copy-start.2 = (bf16[4,256,1024]{2,1,0:T(8,128)(2,1)S(1)}, bf16[4,256,1024]{2,1,0:T(8,128)(2,1)}, u32[]{:S(2)}) copy-start(bf16[4,256,1024]{2,1,0:T(8,128)(2,1)} %param.21) | copy-start | bytes 6291460
  7.2 8.0 %copy-start.21 = (f32[1024]{0:T(1024)S(1)}, f32[1024]{0:T(1024)}, u32[]{:S(2)}) copy-start(f32[1024]{0:T(1024)} %param.23) | copy-start | bytes 12292
  8.2 17.3 %collective-permute-start = (bf16[4,3,1024]{2,1,0:T(4,128)(2,1)S(1)}, bf16[4,3,1024]{2,1,0:T(4,128)(2,1)S(1)}, u32[]{:S(2)}, u32[]{:S(2)}) collective-permute-start(bf16[4,3,1024]{2,1,0:T(4,128)(2,1)S(1)} %slice.174), channel_id=1, source_target_pairs={{0,4},{4,8},{8,12},{12,16},{16,20},{20,24},{24,28},{1,5},{5,9},{9,... | collective-permute-start | bytes 73736 | tf_op jit(solution)/shard_map/ppermute | solution.py:758
  15.2 0.7 copy-start.22
  15.2 0.7 copy-start.23
  15.8 2.7 copy-start.5
  15.8 1.6 copy-start.16
  15.8 1.6 copy-start.33
  15.8 2.0 copy-start.17
  15.9 2.4 copy-start.12
  16.7 0.8 copy-start.15
  18.4 3.7 copy-start.8
  18.5 3.7 copy-start.29
  18.5 4.3 copy-start.24
  18.5 4.3 copy-start.25
  18.5 4.3 copy-start.26
  71.5 19.7 %all-to-all-start.1 = ((bf16[8,256,128]{2,1,0:T(8,128)(2,1)}), bf16[8,256,128]{2,1,0:T(8,128)(2,1)}, u32[]{:S(2)}, u32[]{:S(2)}) async-start(bf16[8,256,128]{2,1,0:T(8,128)(2,1)} %bitcast.226), calls=%async_computation.1 | async-start | bytes 1048576 | tf_op jit(solution)/shard_map/all_to_all | solution.py:768
  91.2 12.5 %all-to-all-start = ((bf16[8,128,128]{2,1,0:T(8,128)(2,1)}), bf16[8,128,128]{2,1,0:T(8,128)(2,1)S(1)}, u32[]{:S(2)}, u32[]{:S(2)}) async-start(bf16[8,128,128]{2,1,0:T(8,128)(2,1)} %bitcast.229), calls=%async_computation | async-start | bytes 524288 | tf_op jit(solution)/shard_map/all_to_all | solution.py:768
  99.3 14.4 %copy-start.30 = (s32[4]{0:T(128)S(1)}, s32[4]{0:T(128)}, u32[]{:S(2)}) copy-start(s32[4]{0:T(128)} %param.22) | copy-start | bytes 52
  109.6 17.9 %all-to-all-start.2 = ((bf16[8,256,128]{2,1,0:T(8,128)(2,1)}), bf16[8,256,128]{2,1,0:T(8,128)(2,1)}, u32[]{:S(2)}, u32[]{:S(2)}) async-start(bf16[8,256,128]{2,1,0:T(8,128)(2,1)} %fusion.12), calls=%async_computation.2 | async-start | bytes 1048576 | tf_op jit(solution)/shard_map/all_to_all | solution.py:768
  113.8 3.3 copy-start.6
  117.1 12.5 %copy-start.27 = (f32[256]{0:T(256)S(1)}, f32[256]{0:T(256)}, u32[]{:S(2)}) copy-start(f32[256]{0:T(256)} %param.35) | copy-start | bytes 3076
  130.2 9.5 %copy-start.28 = (f32[256]{0:T(256)S(1)}, f32[256]{0:T(256)}, u32[]{:S(2)}) copy-start(f32[256]{0:T(256)} %param.37) | copy-start | bytes 3076
  230.6 28.9 %all-to-all-start.3 = ((bf16[8,256,128]{2,1,0:T(8,128)(2,1)}), bf16[8,256,128]{2,1,0:T(8,128)(2,1)}, u32[]{:S(2)}, u32[]{:S(2)}) async-start(bf16[8,256,128]{2,1,0:T(8,128)(2,1)} %bitcast.227), calls=%async_computation.3 | async-start | bytes 1048576 | tf_op jit(solution)/shard_map/all_to_all | solution.py:768
  249.7 5.2 copy-start.10
  249.8 5.2 copy-start.14
  254.9 2.3 copy-start.32
  267.3 21.1 %all-to-all-start.4 = ((bf16[8,256,128]{2,1,0:T(8,128)(2,1)}), bf16[8,256,128]{2,1,0:T(8,128)(2,1)}, u32[]{:S(2)}, u32[]{:S(2)}) async-start(bf16[8,256,128]{2,1,0:T(8,128)(2,1)} %constant_dynamic-update-slice_fusion.4), calls=%async_computation.4 | async-start | bytes 1048576 | tf_op jit(solution)/shard_map/all_to_all | solution.py:768
  273.3 268.1 %reduce-scatter.2.cloned.1.call-start = ((), (), s32[]{:S(2)}) async-start(), calls=%async_computation.6 | async-start | bytes 2621440 | tf_op jit(solution)/shard_map/reduce_scatter | solution.py:872
  274.3 4.7 copy-start.9
  274.3 4.7 copy-start.34
  317.1 3.1 copy-start.20
  320.2 6.2 %collective-permute-start.1 = (f32[4,3,1024]{2,1,0:T(4,128)S(1)}, f32[4,3,1024]{2,1,0:T(4,128)S(1)}, u32[]{:S(2)}, u32[]{:S(2)}) collective-permute-start(f32[4,3,1024]{2,1,0:T(4,128)S(1)} %slice.199), channel_id=1, source_target_pairs={{4,0},{8,4},{12,8},{16,12},{20,16},{24,20},{28,24},{5,1},{9,5},{13... | collective-permute-start | bytes 147464 | tf_op jit(solution)/shard_map/ppermute | solution.py:758
  321.8 4.6 copy-start.19
  336.3 1.2 copy-start.7
  337.6 2.9 copy-start.31
  340.4 2.4 copy-start.13
  521.6 3.0 copy-start.3
  531.4 5.9 %copy-start.4 = (bf16[1024,1536]{1,0:T(8,128)(2,1)S(1)}, bf16[1024,1536]{1,0:T(8,128)(2,1)}, u32[]{:S(2)}) copy-start(bf16[1024,1536]{1,0:T(8,128)(2,1)} %get-tuple-element.85) | copy-start | bytes 9437188
  541.4 28.7 %copy-start.11 = (f32[4,256,256]{2,1,0:T(8,128)S(1)}, f32[4,256,256]{2,1,0:T(8,128)}, u32[]{:S(2)}) copy-start(f32[4,256,256]{2,1,0:T(8,128)} %get-tuple-element.62) | copy-start | bytes 3145732
  543.3 29.6 %copy-start.18 = (bf16[4,256,256]{2,1,0:T(8,128)(2,1)S(1)}, bf16[4,256,256]{2,1,0:T(8,128)(2,1)}, u32[]{:S(2)}) copy-start(bf16[4,256,256]{2,1,0:T(8,128)(2,1)} %get-tuple-element.202) | copy-start | bytes 1572868
  570.1 3.6 copy-start.1
Sparse Core Ops, SparseCore 0:
  336.5 30.3 reduce-scatter.1

commit v3 on v2

v3 whole, which is shorter than its diff:
```python
import functools
import types

import jax
import jax.numpy as jnp
from jax import lax
from jax.experimental import pallas as pl
from jax.experimental.pallas import tpu as pltpu
from jax.sharding import PartitionSpec as P

NORM_EPSILON = 1e-05
UNIT_EPSILON = 1e-06
RIM = 8
LANES = 128
F32 = jnp.float32
BF16 = jnp.bfloat16
VMEM_LIMIT = 58 * 1024 * 1024

NN = (((1,), (0,)), ((), ()))
NT = (((1,), (1,)), ((), ()))
TN = (((0,), (0,)), ((), ()))


def split(x):
    high = x.astype(BF16)
    return high, (x - high.astype(F32)).astype(BF16)


def raw(a, b, dims):
    return lax.dot_general(a, b, dims, preferred_element_type=F32)


def mm(a, b, dims=NN):
    a_high, a_low = a if isinstance(a, tuple) else (a, None)
    b_high, b_low = b if isinstance(b, tuple) else (b, None)
    total = raw(a_high, b_high, dims)
    if a_low is not None:
        total = total + raw(a_low, b_high, dims)
    if b_low is not None:
        total = total + raw(a_high, b_low, dims)
    return total


def sigmoid(x):
    return 1.0 / (1.0 + jnp.exp(-x))


def softplus(x):
    return jnp.maximum(x, 0.0) + jnp.log1p(jnp.exp(-jnp.abs(x)))


def grid_masks(size):
    row = lax.broadcasted_iota(jnp.int32, (size, size), 0)
    col = lax.broadcasted_iota(jnp.int32, (size, size), 1)
    return row, col


def join(a, b, dims=NN):
    return raw(
        jnp.concatenate([a[0], a[1], a[0]], axis=1), jnp.concatenate([b[0], b[0], b[1]], axis=0), dims
    )


def unit_inverse(lower):
    size = lower.shape[0]
    if size > LANES:
        half = size // 2
        first = unit_inverse(lower[:half, :half])
        second = unit_inverse(lower[half:, half:])
        corner = -join(split(join(split(second), split(lower[half:, :half]))), split(first))
        top = jnp.concatenate([first, jnp.zeros((half, half), F32)], axis=1)
        return jnp.concatenate([top, jnp.concatenate([corner, second], axis=1)], axis=0)
    row, col = grid_masks(size)
    apart = row ^ col
    base = 8
    block = jnp.where(apart < base, lower, 0.0)
    one = split(block)
    square = join(one, one)
    square_parts = split(square)
    fourth = join(square_parts, square_parts)
    inverse = jnp.where(row == col, 1.0, 0.0) - block + square - join(one, square_parts)
    inverse = inverse + join(split(inverse), split(fourth))
    while base < size:
        off = split(jnp.where((apart >= base) & (apart < 2 * base), lower, 0.0))
        parts = split(inverse)
        inverse = inverse - join(split(join(parts, off)), parts)
        base *= 2
    return inverse


def gates_of(ab, rate, bias):
    return -rate * softplus(ab + bias), sigmoid(ab)


def decay_of(log_col, log_row, row, col):
    seen = row >= col
    cum_col = jnp.sum(jnp.where(seen, log_row, 0.0), axis=1, keepdims=True)
    cum_row = jnp.sum(jnp.where(row <= col, log_col, 0.0), axis=0, keepdims=True)
    end = jnp.sum(log_row, axis=1, keepdims=True)
    decayed = jnp.where(seen, jnp.exp(jnp.where(seen, cum_col - cum_row, 0.0)), 0.0)
    return cum_col, cum_row, end, decayed


def convolve(ext, taps_ref, length):
    taps = 4
    total = taps_ref[0:1, :] * ext[pl.ds(RIM - taps + 1, length), :]
    for tap in range(1, taps):
        total = total + taps_ref[tap : tap + 1, :] * ext[pl.ds(RIM - taps + 1 + tap, length), :]
    return total


MESH = pl.DeviceIdType.MESH


def remote(src, dst, send_sem, recv_sem, device):
    return pltpu.make_async_remote_copy(
        src_ref=src, dst_ref=dst, send_sem=send_sem, recv_sem=recv_sem, device_id=device, device_id_type=MESH
    )


def turn_to_row(column, row, col):
    return jnp.sum(jnp.where(row == col, column, 0.0), axis=0, keepdims=True)


def turn_to_column(line, row, col):
    return jnp.sum(jnp.where(row == col, line, 0.0), axis=1, keepdims=True)


def staged_call(kernel, operands, outs, scratch, collective_id, late=(), leaving=(), kept=(), slots=0, flops=10**10):
    dma = pltpu.SemaphoreType.DMA
    order = [i for group in late for i in group]
    vmem, free = pl.BlockSpec(memory_space=pltpu.VMEM), pl.BlockSpec(memory_space=pl.ANY)
    count, total = len(operands), len(operands) + len(outs)
    stages = [pltpu.VMEM(operands[i].shape, operands[i].dtype) for i in order]
    stages += [pltpu.VMEM(outs[i].shape, outs[i].dtype) for i in leaving]
    sems = [dma((max(1, len(order)),)), dma((max(1, len(leaving)), max(1, slots)))]

    def body(*refs):
        ins, results, rest = list(refs[:count]), list(refs[count:total]), refs[total:]
        held, (in_sem, out_sem), rest = rest[: len(stages)], rest[len(stages) : len(stages) + 2], rest[len(stages) + 2 :]
        copies = {}
        for j, i in enumerate(order):
            copies[i] = pltpu.make_async_copy(ins[i], held[j], in_sem.at[j])
            copies[i].start()
            ins[i] = held[j]
        targets = {}
        for j, i in enumerate(leaving):
            targets[i] = (results[i], held[len(order) + j], j)
            results[i] = held[len(order) + j]
        left = {}

        def arrive(group):
            for i in late[group]:
                copies[i].wait()

        def out_copy(i, slot):
            target, source, j = targets[i]
            if slot is None:
                return pltpu.make_async_copy(source, target, out_sem.at[j, 0])
            return pltpu.make_async_copy(source.at[slot], target.at[slot], out_sem.at[j, slot])

        def leave(slot, *indices):
            for i in indices:
                left[i] = slot is not None
                out_copy(i, slot).start()

        kernel(arrive, leave, *ins, *results, *rest)
        for i in leaving:
            for slot in range(slots) if left[i] else (None,):
                out_copy(i, slot).wait()

    late_set = set(order)
    return pl.pallas_call(
        body,
        in_specs=[free if i in late_set else vmem for i in range(count)],
        out_specs=[free if i in leaving or i in kept else vmem for i in range(len(outs))],
        out_shape=tuple(outs),
        scratch_shapes=stages + sems + list(scratch),
        compiler_params=pltpu.CompilerParams(
            collective_id=collective_id, has_side_effects=True, vmem_limit_bytes=VMEM_LIMIT
        ),
        cost_estimate=pl.CostEstimate(flops=flops, bytes_accessed=60 * 10**6, transcendentals=0),
    )(*operands)


class Units:
    def __init__(self, count, pairs):
        self.count, self.pairs, self.share = count, pairs, count // pairs
        self.me, self.other = lax.axis_index("seq"), lax.axis_index("head")

    def ahead(self, place):
        return lax.rem(place - self.me + self.count, self.count) - 1

    def behind(self, place):
        return lax.rem(self.me - place + self.count, self.count) - 1

    def to_owner(self, src, dst, send, recv, unit):
        return remote(src, dst.at[self.me], send.at[self.ahead(unit)], recv.at[self.ahead(unit)], (unit, self.other))

    def at_owner(self, src, dst, send, recv, place):
        return remote(src, dst.at[place], send.at[self.behind(place)], recv.at[self.behind(place)], (place, self.other))

    def pieces(self, value):
        size = value.shape[0] // self.share
        return [value[i * size : (i + 1) * size] for i in range(self.share)]

    def whole(self, ref, pair):
        return jnp.concatenate([ref[pair * self.share + i] for i in range(self.share)], axis=0)

    def greet(self, barrier):
        def one(away, carry):
            pl.semaphore_signal(
                barrier, inc=1, device_id=(lax.rem(self.me + away, self.count), self.other), device_id_type=MESH
            )
            return carry

        lax.fori_loop(1, self.count, one, 0)


def forward_kernel(
    slots, heads, key_dim, value_dim, parts, arrive, leave,
    hidden, input_gain, query_weight, key_weight, value_weight, gate_weight, ab_weight, taps_ref, lanes, cols, gain,
    query_out, key_out, value_out, inverse_out, eff_out, rows_out, mixer_out, gated_out,
    normed, pre, gate, x_out, inv_out, rim, ab, abt, states, maps_in,
    ext, rim_rows, delta, mix, maps_low, shifts_low, shifts_in, state_send, edge_send, edge_recv,
    map_send, map_recv, shift_send, shift_recv, back_send, back_recv,
):
    length = pre.shape[1]
    units = Units(parts, slots * heads)
    me = units.me
    barrier = pltpu.get_barrier_semaphore()
    units.greet(barrier)
    row, col = grid_masks(length)
    key_start = heads * key_dim
    value_start = 2 * heads * key_dim
    width = hidden.shape[2]
    shard = x_out.shape[2]
    edge = rim_rows.shape[1]
    shard_start = pl.multiple_of(units.other * shard, shard)

    def edge_copy():
        return remote(
            hidden.at[:, length - edge : length, :], rim_rows, edge_send.at[0], edge_recv.at[0],
            (lax.rem(me + 1, parts), units.other),
        )

    def norm_rows(x):
        inv = lax.rsqrt(jnp.sum(x * x, axis=1, keepdims=True) / width + NORM_EPSILON)
        return inv, (x * inv * input_gain[0:1, :]).astype(BF16)

    def project(s, carry):
        inv, low = norm_rows(hidden[s].astype(F32))
        normed[s] = low
        x_out[s] = hidden[s, :, pl.ds(shard_start, shard)]
        inv_out[s] = jnp.broadcast_to(inv, (length, LANES))
        pre[s, :, :key_start] = raw(low, query_weight[...], NN).astype(BF16)
        pre[s, :, key_start:value_start] = raw(low, key_weight[...], NN).astype(BF16)
        pre[s, :, value_start:] = raw(low, value_weight[...], NN).astype(BF16)
        gate[s] = raw(low, gate_weight[...], NN)
        gates = raw(low, ab_weight[...], NN)
        ab[s] = gates
        abt[s] = jnp.transpose(gates)[0:8, :]
        leave(s, 8, 9, 10, 11, 12)

        @pl.when(s == 0)
        def _():
            pl.semaphore_wait(barrier, parts - 1)
            edge_copy().start()

        return carry

    lax.fori_loop(0, slots, project, 0)
    edge_copy().wait_recv()
    _, edge_low = norm_rows(rim_rows[...].reshape(slots * edge, width).astype(F32))
    edge_pre = jnp.concatenate(
        [raw(edge_low, weight[...], NN) for weight in (query_weight, key_weight, value_weight)], axis=1
    ).astype(BF16).astype(F32)
    for s in range(slots):
        rim[s] = jnp.where(me > 0, edge_pre[(s + 1) * edge - RIM : (s + 1) * edge, :], 0.0)

    def map_copy(unit):
        return units.to_owner(maps_low.at[unit // units.share], maps_in, map_send, map_recv, unit)

    def shift_copy(unit):
        return units.to_owner(shifts_low.at[unit], shifts_in, shift_send, shift_recv, unit)

    def back_copy(place):
        ahead = units.ahead(place)
        return remote(
            state_send.at[place], states.at[me], back_send.at[ahead], back_recv.at[ahead], (place, units.other)
        )

    def back_arrival(unit):
        behind = units.behind(unit)
        return remote(
            state_send.at[unit], states.at[unit], back_send.at[behind], back_recv.at[behind], (unit, units.other)
        )

    def slot_terms(s, carry):
        ext[0:RIM, :] = rim[s]
        ext[RIM : RIM + length, :] = pre[s].astype(F32)
        conv = convolve(ext, taps_ref, length)
        active = conv * sigmoid(conv)
        log_cols, strength_cols = gates_of(ab[s], lanes[0:1, :], lanes[1:2, :])
        log_rows, strength_rows = gates_of(abt[s], cols[0:8, 0:1], cols[8:16, 0:1])
        for h in range(heads):
            query_act = active[:, h * key_dim : (h + 1) * key_dim]
            key_act = active[:, key_start + h * key_dim : key_start + (h + 1) * key_dim]
            value_act = active[:, value_start + h * value_dim : value_start + (h + 1) * value_dim]
            query_scale = lax.rsqrt(jnp.sum(query_act * query_act, axis=1, keepdims=True) + UNIT_EPSILON)
            key_scale = lax.rsqrt(jnp.sum(key_act * key_act, axis=1, keepdims=True) + UNIT_EPSILON)
            query = (query_act * query_scale * key_dim ** (-0.5)).astype(BF16)
            key = (key_act * key_scale).astype(BF16)
            value = value_act.astype(BF16)
            query_out[s, h] = query
            key_out[s, h] = key
            value_out[s, h] = value
            strength = strength_cols[:, heads + h : heads + h + 1]
            strength_row = strength_rows[heads + h : heads + h + 1, :]
            cum_col, cum_row, end, decayed = decay_of(
                log_cols[:, h : h + 1], log_rows[h : h + 1, :], row, col
            )
            products = mm(key, key, NT)
            inverse = unit_inverse(jnp.where(row > col, strength * decayed * products, 0.0))
            inverse_out[s, h] = inverse
            scaled = inverse * strength_row
            delta_h = mm(split(scaled), value)
            mix_h = mm(split(scaled * jnp.exp(cum_row)), key)
            delta[s, h] = delta_h
            mix[s, h] = mix_h
            scores = split(decayed * mm(query, key, NT))
            eff_out[s, h] = jnp.exp(cum_col) * query.astype(F32) - mm(scores, split(mix_h))
            end_weight = jnp.exp(end - cum_col)
            small_row = lax.broadcasted_iota(jnp.int32, (key_dim, key_dim), 0)
            small_col = lax.broadcasted_iota(jnp.int32, (key_dim, key_dim), 1)
            moved = jnp.where(small_row == small_col, jnp.exp(end), 0.0)
            pair = s * heads + h
            maps_low[pair] = (moved - mm(split(mix_h * end_weight), key, TN)).astype(BF16)
            for i, piece in enumerate(units.pieces(mm(split(delta_h * end_weight), key, TN).astype(BF16))):
                shifts_low[pair * units.share + i] = piece

        leave(s, 0, 1, 2, 3, 4)
        for i in range(heads * units.share):
            unit = s * heads * units.share + i

            @pl.when(unit != me)
            def _(unit=unit):
                map_copy(unit).start()
                shift_copy(unit).start()

            @pl.when(unit == me)
            def _(unit=unit):
                maps_in[unit] = maps_low[unit // units.share]
                shifts_in[unit] = shifts_low[unit]

        return carry

    lax.fori_loop(0, slots, slot_terms, 0)

    def scan(place, state):
        low = state.astype(BF16)

        @pl.when(place != me)
        def _():
            state_send[place] = low
            back_copy(place).start()
            units.at_owner(maps_low.at[0], maps_in, map_send, map_recv, place).wait_recv()
            units.at_owner(shifts_low.at[0], shifts_in, shift_send, shift_recv, place).wait_recv()

        @pl.when(place == me)
        def _():
            states[place] = low

        return mm(split(state), maps_in[place]) + shifts_in[place].astype(F32)

    lax.fori_loop(0, parts, scan, jnp.zeros((value_dim // units.share, key_dim), F32))

    def emit(s, carry):
        for i in range(heads * units.share):
            unit = s * heads * units.share + i

            @pl.when(unit != me)
            def _(unit=unit):
                back_arrival(unit).wait_recv()

        log_cols, _ = gates_of(ab[s], lanes[0:1, :], lanes[1:2, :])
        log_rows, _ = gates_of(abt[s], cols[0:8, 0:1], cols[8:16, 0:1])
        for h in range(heads):
            query, key = query_out[s, h], key_out[s, h]
            cum_col, _, _, decayed = decay_of(log_cols[:, h : h + 1], log_rows[h : h + 1, :], row, col)
            scores = split(decayed * mm(query, key, NT))
            state = units.whole(states, s * heads + h)
            rows = delta[s, h] - mm(split(mix[s, h]), state, NT)
            rows_out[s, h] = rows
            mixer = mm(scores, split(rows)) + jnp.exp(cum_col) * mm(query, state, NT)
            mixer_out[s, h] = mixer
            scale = lax.rsqrt(jnp.sum(mixer * mixer, axis=1, keepdims=True) / value_dim + NORM_EPSILON)
            here = slice(h * value_dim, (h + 1) * value_dim)
            gate_h = gate[s, :, here]
            gated_out[s, :, here] = (mixer * scale * gain[0:1, :] * (gate_h * sigmoid(gate_h))).astype(BF16)
        leave(s, 5, 6, 7)
        return carry

    lax.fori_loop(0, slots, emit, 0)

    def drain(away, carry):
        unit = lax.rem(me + away, parts)
        map_copy(unit).wait_send()
        shift_copy(unit).wait_send()
        back_copy(unit).wait_send()
        return carry

    lax.fori_loop(1, parts, drain, 0)
    edge_copy().wait_send()


def forward_call(parts, head_parts, heads, *operands):
    hidden, query_weight, value_weight, gate_weight = operands[0], operands[2], operands[4], operands[5]
    slots, length, width = hidden.shape
    key_dim, value_dim = query_weight.shape[1] // heads, value_weight.shape[1] // heads
    channels = heads * (2 * key_dim + value_dim)
    share = parts // (slots * heads)
    sds = jax.ShapeDtypeStruct
    dma = pltpu.SemaphoreType.DMA
    per = lambda kind, *tail: sds((slots, heads) + tail, kind)
    each = lambda kind, *tail: sds((slots,) + tail, kind)
    unit = (parts, value_dim // share, key_dim)
    outs = (
        per(BF16, length, key_dim), per(BF16, length, key_dim), per(BF16, length, value_dim),
        per(F32, length, length), per(F32, length, key_dim), per(F32, length, value_dim),
        per(F32, length, value_dim), each(BF16, length, heads * value_dim),
        each(BF16, length, width), each(BF16, length, channels), each(F32, length, heads * value_dim),
        each(BF16, length, width // head_parts), each(F32, length, LANES), each(F32, RIM, channels),
        each(F32, length, LANES), each(F32, 8, length),
        sds(unit, BF16), sds((parts, key_dim, key_dim), BF16),
    )
    scratch = [
        pltpu.VMEM((length + RIM, channels), F32),
        pltpu.VMEM((slots, 2 * RIM, width), BF16),
        pltpu.VMEM((slots, heads, length, value_dim), F32),
        pltpu.VMEM((slots, heads, length, key_dim), F32),
        pltpu.VMEM((slots * heads, key_dim, key_dim), BF16),
        pltpu.VMEM(unit, BF16), pltpu.VMEM(unit, BF16), pltpu.VMEM(unit, BF16), dma((1,)), dma((1,)),
    ] + [dma((parts - 1,))] * 6
    return staged_call(
        functools.partial(forward_kernel, slots, heads, key_dim, value_dim, parts),
        operands, outs, scratch, 2, leaving=tuple(range(13)), slots=slots,
    )


def head_scratch(kinds, stats, slots, head_parts, length, shard):
    lines = head_parts // 2
    dma = pltpu.SemaphoreType.DMA
    return [
        pltpu.VMEM((head_parts, length, shard), F32),
        pltpu.VMEM((kinds, slots, lines, length, shard), F32),
        pltpu.VMEM((kinds, slots, lines, length, shard), BF16),
        pltpu.VMEM((kinds, slots, lines, length, shard), BF16),
        pltpu.VMEM((kinds, slots, lines - 1, length, shard), BF16),
        pltpu.VMEM((kinds, slots, lines - 1, length, shard), BF16),
        pltpu.VMEM((stats, slots, 8, length), F32),
        pltpu.VMEM((stats, slots, head_parts - 1, 8, length), F32),
        dma((kinds, slots, lines)), dma((kinds, slots, lines)),
        dma((kinds, slots, lines - 1)), dma((kinds, slots, lines - 1)),
        dma((stats, slots, head_parts - 1)), dma((stats, slots, head_parts - 1)),
    ]


def head_tools(head_parts, refs, stats):
    whole_part, part, low, from_core, to_line, from_line, stat_own, stat_in = refs[:8]
    core_send, core_recv, line_send, line_recv, stat_send, stat_recv = refs[8:]
    me = lax.axis_index("head")
    place = lax.axis_index("seq")
    lines = head_parts // 2
    core = lax.rem(me, 2)
    line = me // 2
    sibling = 2 * line + (1 - core)
    length, shard = whole_part.shape[1:]
    row, col = grid_masks(length)

    def greet(barrier):
        for away in range(1, head_parts):
            pl.semaphore_signal(
                barrier, inc=1, device_id=(place, lax.rem(me + away, head_parts)), device_id_type=MESH
            )

    def core_copy(kind, s, y):
        return remote(
            low.at[kind, s, y], from_core.at[kind, s, y],
            core_send.at[kind, s, y], core_recv.at[kind, s, y], (place, sibling),
        )

    def line_copy(kind, s, away):
        return remote(
            to_line.at[kind, s, away - 1], from_line.at[kind, s, away - 1],
            line_send.at[kind, s, away - 1], line_recv.at[kind, s, away - 1],
            (place, 2 * lax.rem(line + away, lines) + core),
        )

    def stat_copy(kind, s, away):
        return remote(
            stat_own.at[kind, s], stat_in.at[kind, s, away - 1],
            stat_send.at[kind, s, away - 1], stat_recv.at[kind, s, away - 1],
            (place, lax.rem(me + away, head_parts)),
        )

    def send_part(kind, s, value):
        for j in range(head_parts):
            whole_part[j] = value[:, j * shard : (j + 1) * shard]
        for y in range(lines):
            low[kind, s, y] = whole_part[2 * y + (1 - core)].astype(BF16)
            core_copy(kind, s, y).start()
            part[kind, s, y] = whole_part[2 * y + core]

    def join_core(kind, s):
        for y in range(lines):
            core_copy(kind, s, y).wait_recv()
        for away in range(1, lines):
            y = lax.rem(line + away, lines)
            joined = part[kind, s, y] + from_core[kind, s, y].astype(F32)
            to_line[kind, s, away - 1] = joined.astype(BF16)
            line_copy(kind, s, away).start()
        part[kind, s, line] = part[kind, s, line] + from_core[kind, s, line].astype(F32)

    def join_line(kind, s):
        total = part[kind, s, line]
        for away in range(1, lines):
            line_copy(kind, s, away).wait_recv()
            total = total + from_line[kind, s, away - 1].astype(F32)
        return total

    def send_stat(kind, s, column):
        stat_own[kind, s] = jnp.broadcast_to(turn_to_row(column, row, col), (8, length))
        for away in range(1, head_parts):
            stat_copy(kind, s, away).start()

    def join_stat(kind, s):
        total = stat_own[kind, s]
        for away in range(1, head_parts):
            stat_copy(kind, s, away).wait_recv()
            total = total + stat_in[kind, s, away - 1]
        return turn_to_column(total[0:1, :], row, col)

    def drain(s):
        for kind in range(part.shape[0]):
            for y in range(lines):
                core_copy(kind, s, y).wait_send()
            for away in range(1, lines):
                line_copy(kind, s, away).wait_send()
        for kind in range(stats):
            for away in range(1, head_parts):
                stat_copy(kind, s, away).wait_send()

    return types.SimpleNamespace(
        me=me, place=place, lines=lines, core=core, line=line, sibling=sibling, greet=greet,
        send_part=send_part, join_core=join_core, join_line=join_line, send_stat=send_stat,
        join_stat=join_stat, drain=drain,
    )


def weight_rows(left, right, store):
    wide = left.shape[2]
    step = min(wide, 256)
    steps = wide // step

    def one(j, carry):
        start = pl.multiple_of(j * step, step)
        block = left[:, :, pl.ds(start, step)]
        store(start, step, raw(block.reshape(-1, step), right, TN).astype(BF16))
        return carry

    lax.fori_loop(0, steps, one, 0)
    if wide % step:
        rest = wide % step
        block = left[:, :, steps * step :]
        store(steps * step, rest, raw(block.reshape(-1, rest), right, TN).astype(BF16))


def middle_kernel(
    slots, head_parts, parts, heads, arrive, leave,
    gated, x_shard, cotangent, mask, out_weight, gate_weight, up_weight,
    down_weight, gain, mixer, gate, gain_row, eff,
    residual, act_all, up_part, gate_part, down_part, residual_grad_out, mixer_rows_grad, mixer_grad, gate_grad_out,
    gain_grad_out, output_gain_grad, shifts_in,
    normed_all, up_grad_all, gate_grad_all, out_grad,
    inverse, spread, grad_shard, shifts_low, shift_send, shift_recv,
    spread_line_send, spread_line_recv, spread_core_send, spread_core_recv,
    *head_refs,
):
    tools = head_tools(head_parts, head_refs, 2)
    me, place, lines, core, line, sibling = (
        tools.me, tools.place, tools.lines, tools.core, tools.line, tools.sibling
    )
    send_part, join_core, join_line = tools.send_part, tools.join_core, tools.join_line
    send_stat, join_stat = tools.send_stat, tools.join_stat
    length, shard = x_shard.shape[1], x_shard.shape[2]
    width = shard * head_parts
    hidden = gate_weight.shape[0]
    value_dim = mixer.shape[3]
    units = Units(parts, slots * heads)

    barrier = pltpu.get_barrier_semaphore()
    tools.greet(barrier)
    units.greet(barrier)
    gain_grad_out[...] = jnp.zeros_like(gain_grad_out)
    output_gain_grad[...] = jnp.zeros_like(output_gain_grad)
    pl.semaphore_wait(barrier, head_parts - 1 + parts - 1)

    def shift_copy(unit):
        return units.to_owner(shifts_low.at[unit], shifts_in, shift_send, shift_recv, unit)

    def spread_line_copy(kind, s, away):
        return remote(
            spread.at[kind, s, me], spread.at[kind, s, me],
            spread_line_send.at[kind, s, away - 1], spread_line_recv.at[kind, s, away - 1],
            (place, 2 * lax.rem(line + away, lines) + core),
        )

    def spread_core_copy(kind, s, away):
        y = lax.rem(line + away, lines)
        return remote(
            spread.at[kind, s, 2 * y + core], spread.at[kind, s, 2 * y + core],
            spread_core_send.at[kind, s, away], spread_core_recv.at[kind, s, away], (place, sibling),
        )

    def spread_core_arrival(kind, s, away):
        y = lax.rem(line + away, lines)
        return remote(
            spread.at[kind, s, 2 * y + (1 - core)], spread.at[kind, s, 2 * y + (1 - core)],
            spread_core_send.at[kind, s, away], spread_core_recv.at[kind, s, away], (place, sibling),
        )

    def spread_line_arrival(kind, s, away):
        y = lax.rem(line + lines - away, lines)
        return remote(
            spread.at[kind, s, 2 * y + core], spread.at[kind, s, 2 * y + core],
            spread_line_send.at[kind, s, away - 1], spread_line_recv.at[kind, s, away - 1],
            (place, 2 * y + core),
        )

    def send_spread(kind, s, value):
        spread[kind, s, me] = value
        for away in range(1, lines):
            spread_line_copy(kind, s, away).start()
        spread_core_copy(kind, s, 0).start()

    def pass_spread(kind, s):
        for away in range(1, lines):
            spread_line_arrival(kind, s, lines - away).wait_recv()
            spread_core_copy(kind, s, away).start()

    def take_spread(kind, s):
        for away in range(lines):
            spread_core_arrival(kind, s, away).wait_recv()
        return jnp.concatenate([spread[kind, s, j] for j in range(head_parts)], axis=1)

    def attention(s):
        send_part(0, s, raw(gated[s], out_weight[...], NN))

    def rows_in(s):
        total = x_shard[s].astype(F32) + mask[s][:, 0:1] * join_line(0, s)
        residual[s] = total
        leave(s, 0)
        send_stat(0, s, jnp.sum(total * total, axis=1, keepdims=True))

    def norm_second(s):
        inv = lax.rsqrt(join_stat(0, s) / width + NORM_EPSILON)
        inverse[s] = jnp.broadcast_to(inv, (length, LANES))
        send_spread(0, s, (residual[s] * inv * gain[0:1, :]).astype(BF16))

    def swiglu(s):
        normed = take_spread(0, s)
        normed_all[s] = normed
        gate_values = raw(normed, gate_weight[...], NT)
        up_values = raw(normed, up_weight[...], NT)
        out_grad[s] = (cotangent[s].astype(F32) * mask[s][:, 0:1]).astype(BF16)
        act_grad = raw(out_grad[s], down_weight[...], NT)
        sig = sigmoid(gate_values)
        silu = gate_values * sig
        act_all[s] = (silu * up_values).astype(BF16)
        up_grad = (act_grad * silu).astype(BF16)
        gate_grad = (act_grad * up_values * sig * (1.0 + gate_values * (1.0 - sig))).astype(BF16)
        up_grad_all[s] = up_grad
        gate_grad_all[s] = gate_grad
        leave(s, 1)
        send_part(1, s, raw(up_grad, up_weight[...], NN) + raw(gate_grad, gate_weight[...], NN))

    def norm_back(s):
        grad = join_line(1, s)
        inv = inverse[s][:, 0:1]
        gain_grad_out[0:1, :] += jnp.sum(grad * residual[s] * inv, axis=0, keepdims=True)
        weighted = grad * gain[0:1, :]
        grad_shard[s] = weighted
        send_stat(1, s, jnp.sum(weighted * residual[s], axis=1, keepdims=True))

    def residual_back(s):
        stat = join_stat(1, s) / width
        inv = inverse[s][:, 0:1]
        cot = cotangent[s, :, pl.ds(pl.multiple_of(me * shard, shard), shard)].astype(F32)
        grad = cot + inv * (grad_shard[s] - residual[s] * (inv * inv * stat))
        residual_grad_out[s] = grad
        leave(s, 5)
        send_spread(1, s, (mask[s][:, 0:1] * grad).astype(BF16))

    def gate_back(s, gated_grad):
        out_gain = gain_row[0:1, :]
        for h in range(heads):
            here = slice(h * value_dim, (h + 1) * value_dim)
            grad = gated_grad[:, here]
            mixer_h = mixer[s, h]
            gate_h = gate[s, :, here]
            scale = lax.rsqrt(jnp.sum(mixer_h * mixer_h, axis=1, keepdims=True) / value_dim + NORM_EPSILON)
            sig = sigmoid(gate_h)
            unit_rows = mixer_h * scale
            gate_grad_out[s, :, here] = (
                grad * unit_rows * out_gain * (sig * (1.0 + gate_h * (1.0 - sig)))
            ).astype(BF16)
            scaled_grad = grad * (gate_h * sig)
            output_gain_grad[0:1, :] += jnp.sum(scaled_grad * unit_rows, axis=0, keepdims=True)
            unit_grad = scaled_grad * out_gain
            stat = jnp.sum(unit_grad * mixer_h, axis=1, keepdims=True) / value_dim
            mixer_grad_h = scale * (unit_grad - mixer_h * (scale * scale * stat))
            mixer_grad[s, h] = mixer_grad_h
            entering = mm(split(mixer_grad_h), split(eff[s, h]), TN).astype(BF16)
            for i, piece in enumerate(units.pieces(entering)):
                shifts_low[(s * heads + h) * units.share + i] = piece

        for i in range(heads * units.share):
            unit = s * heads * units.share + i

            @pl.when(unit != units.me)
            def _(unit=unit):
                shift_copy(unit).start()

            @pl.when(unit == units.me)
            def _(unit=unit):
                shifts_in[unit] = shifts_low[unit]

    def mixer_rows(s):
        grad = take_spread(1, s)
        mixer_rows_grad[s] = grad
        gate_back(s, raw(grad, out_weight[...], NT))
        leave(s, 6, 7, 8)

    stages = (
        (10, mixer_rows),
        (9, functools.partial(pass_spread, 1)),
        (8, residual_back),
        (7, norm_back),
        (6, functools.partial(join_core, 1)),
        (4, functools.partial(pass_spread, 0)),
        (3, norm_second),
        (2, rows_in),
        (1, functools.partial(join_core, 0)),
        (0, attention),
        (5, swiglu),
    )

    def step(t, carry):
        @pl.when(t == 5)
        def _():
            arrive(0)

        @pl.when(t == 10)
        def _():
            arrive(1)

        for offset, stage in stages:
            s = t - offset

            @pl.when((s >= 0) & (s < slots))
            def _(stage=stage, s=s):
                stage(s)

        for late, left, right, target, index in (
            (5, up_grad_all, normed_all, up_part, 2),
            (6, gate_grad_all, normed_all, gate_part, 3),
            (7, act_all, out_grad, down_part, 4),
        ):

            @pl.when(t == slots + late)
            def _(left=left, right=right, target=target, index=index):
                def store(start, size, block):
                    target[pl.ds(start, size), :] = block

                weight_rows(left, right[...].reshape(-1, width), store)
                if target.shape[0] > hidden:
                    target[hidden:, :] = jnp.zeros((target.shape[0] - hidden, width), BF16)
                leave(None, index)

        return carry

    lax.fori_loop(0, slots + 10, step, 0)

    def drain(s, carry):
        tools.drain(s)
        for kind in range(2):
            for away in range(1, lines):
                spread_line_copy(kind, s, away).wait_send()
            for away in range(lines):
                spread_core_copy(kind, s, away).wait_send()
        return carry

    lax.fori_loop(0, slots, drain, 0)

    def take_units(away, carry):
        unit = lax.rem(units.me + away, parts)
        units.at_owner(shifts_low.at[0], shifts_in, shift_send, shift_recv, unit).wait_recv()
        return carry

    lax.fori_loop(1, parts, take_units, 0)

    def drain_units(away, carry):
        shift_copy(lax.rem(units.me + away, parts)).wait_send()
        return carry

    lax.fori_loop(1, parts, drain_units, 0)


def padded_rows(count, parts):
    return count + -count % (32 * parts)


def middle_call(parts, head_parts, heads, *operands):
    gated, x_shard, gate_weight, mixer, eff = (operands[i] for i in (0, 1, 5, 9, 12))
    slots, length, shard = x_shard.shape
    width = shard * head_parts
    hidden = gate_weight.shape[0]
    lines = head_parts // 2
    value_dim, key_dim = mixer.shape[3], eff.shape[3]
    unit = (parts, value_dim * slots * heads // parts, key_dim)
    sds = jax.ShapeDtypeStruct
    dma = pltpu.SemaphoreType.DMA
    product = sds((padded_rows(hidden, parts), width), BF16)
    outs = (
        sds((slots, length, shard), F32), sds((slots, length, hidden), BF16), product, product, product,
        sds((slots, length, shard), F32), sds((slots, length, width), BF16), sds(mixer.shape, F32),
        sds(gated.shape, BF16), sds((8, shard), F32), sds((8, value_dim), F32), sds(unit, BF16),
    )
    scratch = [
        pltpu.VMEM((slots, length, width), BF16),
        pltpu.VMEM((slots, length, hidden), BF16),
        pltpu.VMEM((slots, length, hidden), BF16),
        pltpu.VMEM((slots, length, width), BF16),
        pltpu.VMEM((slots, length, LANES), F32),
        pltpu.VMEM((2, slots, head_parts, length, shard), BF16),
        pltpu.VMEM((slots, length, shard), F32),
        pltpu.VMEM(unit, BF16), dma((parts - 1,)), dma((parts - 1,)),
        dma((2, slots, lines - 1)), dma((2, slots, lines - 1)),
        dma((2, slots, lines)), dma((2, slots, lines)),
    ] + head_scratch(2, 2, slots, head_parts, length, shard)
    return staged_call(
        functools.partial(middle_kernel, slots, head_parts, parts, heads),
        operands, outs, scratch, 0, late=((5, 6, 7, 2), (9, 10, 12)), leaving=tuple(range(9)), slots=slots,
    )


def ring_scratch(parts, shapes):
    dma = pltpu.SemaphoreType.DMA
    count = len(shapes)
    return [
        pltpu.VMEM((2, parts, rows // (2 * parts), wide), BF16) for rows, wide in shapes
    ] + [dma((count, 2)), dma((count, 2, parts - 1)), dma((count, 2)), dma((count, 2, parts - 1)), dma((count, 2))]


def ring_tools(parts, ins, outs, held, send, recv, spread_send, spread_recv, own):
    count = len(ins)
    index = lax.axis_index("seq")
    other = lax.axis_index("head")
    side = lax.rem(index, 2)
    level = index // 2
    levels = parts // 2
    position = jnp.where(side == 1, level, parts - 1 - level)
    up = jnp.where(side == 1, jnp.where(level == levels - 1, index - 1, index + 2),
                   jnp.where(level == 0, index + 1, index - 2))
    down = jnp.where(side == 1, jnp.where(level == 0, index - 1, index - 2),
                     jnp.where(level == levels - 1, index + 1, index + 2))
    targets = (up, down)
    def greet(barrier):
        for target in targets:
            pl.semaphore_signal(barrier, inc=1, device_id=(target, other), device_id_type=MESH)

    def rows_of(a, way, chunk):
        size = ins[a].shape[0] // (2 * parts)
        return pl.ds(pl.multiple_of((chunk * 2 + way) * size, size), size)

    def chunk_at(way, step):
        if way == 0:
            return lax.rem(position - step + 2 * parts, parts)
        return lax.rem(position + step + 2 * parts, parts)

    def sum_copy(a, way, step):
        return remote(
            held[a].at[way, step], held[a].at[way, step + 1], send.at[a, way], recv.at[a, way, step],
            (targets[way], other),
        )

    def spread_copy(a, way, step):
        block = rows_of(a, way, chunk_at(way, step - 1))
        return remote(
            outs[a].at[block, :], outs[a].at[block, :], spread_send.at[a, way], spread_recv.at[a, way, step],
            (targets[way], other),
        )

    def spread_first(a, way):
        block = rows_of(a, way, chunk_at(way, parts - 1))
        return remote(
            held[a].at[way, parts - 1], outs[a].at[block, :], spread_send.at[a, way],
            spread_recv.at[a, way, 0], (targets[way], other),
        )

    def own_copy(a, way):
        block = rows_of(a, way, chunk_at(way, parts - 1))
        return pltpu.make_async_copy(held[a].at[way, parts - 1], outs[a].at[block, :], own.at[a, way])

    def spread_arrival(a, way, step):
        block = rows_of(a, way, chunk_at(way, step))
        return remote(
            outs[a].at[block, :], outs[a].at[block, :], spread_send.at[a, way], spread_recv.at[a, way, step],
            (targets[way], other),
        )

    lanes = [(a, way) for a in range(count) for way in range(2)]
    last = parts - 2

    def add(step, a, way):
        sum_copy(a, way, step).wait_recv()
        mine = ins[a][rows_of(a, way, chunk_at(way, step + 1)), :].astype(F32)
        return (held[a][way, step + 1].astype(F32) + mine).astype(BF16)

    def begin():
        for a, way in lanes:
            held[a][way, 0] = ins[a][rows_of(a, way, chunk_at(way, 0)), :]
            sum_copy(a, way, 0).start()

    def one(step):
        for a, way in lanes:
            held[a][way, step + 1] = add(step, a, way)
            sum_copy(a, way, step).wait_send()
            sum_copy(a, way, step + 1).start()

    def turn():
        for a, way in lanes:
            held[a][way, parts - 1] = add(last, a, way)
            sum_copy(a, way, last).wait_send()
            spread_first(a, way).start()
            own_copy(a, way).start()

    def pass_first():
        for a, way in lanes:
            spread_arrival(a, way, 0).wait_recv()
            spread_first(a, way).wait_send()
            spread_copy(a, way, 1).start()

    def pass_on(step):
        for a, way in lanes:
            spread_arrival(a, way, step).wait_recv()
            spread_copy(a, way, step).wait_send()
            spread_copy(a, way, step + 1).start()

    def finish():
        for a, way in lanes:
            spread_arrival(a, way, last).wait_recv()
            spread_copy(a, way, last).wait_send()
            own_copy(a, way).wait()

    def tick(k):
        @pl.when(k < last)
        def _():
            one(k)

        @pl.when(k == last)
        def _():
            turn()

        @pl.when(k == last + 1)
        def _():
            pass_first()

        @pl.when(k > last + 1)
        def _():
            pass_on(k - last - 1)

    return types.SimpleNamespace(
        greet=greet, begin=begin, tick=tick, finish=finish, ticks=2 * parts - 3, up=up, down=down
    )


def backward_kernel(
    slots, heads, key_dim, value_dim, parts, head_parts, arrive, leave,
    mixer_grad, shifts_in, gated, mixer_rows_grad, normed, gate_grad, act, down_weight, residual, mask,
    pre, rim, ab, abt, taps_ref, lanes, cols,
    queries, keys, value_rows, inverse_all, delta_rows, states, maps_in, up_part, gate_part, down_part,
    block_out, pre_grad_out, ab_grad_out, taps_grad_out, lane_grad_out,
    up_sum, gate_sum, down_sum, out_sum, first_sum,
    out_part, first_part, ext, conv_grad, tail, rim_own, rim_in, leavings, leaving_send,
    back_send, back_recv, rim_send, rim_recv, *refs,
):
    sides = (refs[:7], refs[7:15])
    length = pre.shape[1]
    taps = 4
    width = normed.shape[2]
    values = gated.shape[2]
    units = Units(parts, slots * heads)
    me = units.me
    tools = head_tools(head_parts, refs[15:], 0)
    rings = (
        ring_tools(parts, (up_part, gate_part), (up_sum, gate_sum), sides[0][:2], *sides[0][2:]),
        ring_tools(
            parts, (down_part, out_part, first_part), (down_sum, out_sum, first_sum), sides[1][:3], *sides[1][3:]
        ),
    )
    barrier = pltpu.get_barrier_semaphore()
    units.greet(barrier)
    tools.greet(barrier)
    row, col = grid_masks(length)
    taps_grad_out[...] = jnp.zeros_like(taps_grad_out)
    lane_grad_out[...] = jnp.zeros_like(lane_grad_out)
    pl.semaphore_wait(barrier, parts - 1 + head_parts - 1)
    rings[0].begin()

    def back_copy(place):
        ahead = units.ahead(place)
        return remote(
            leaving_send.at[place], leavings.at[me], back_send.at[ahead], back_recv.at[ahead],
            (place, units.other),
        )

    def back_arrival(unit):
        behind = units.behind(unit)
        return remote(
            leaving_send.at[unit], leavings.at[unit], back_send.at[behind], back_recv.at[behind],
            (unit, units.other),
        )

    def rim_copy():
        return remote(
            rim_own, rim_in, rim_send.at[0], rim_recv.at[0], (lax.rem(me + parts - 1, parts), units.other)
        )

    def scan(hop, leaving):
        place = parts - 1 - hop
        low = leaving.astype(BF16)

        @pl.when(place != me)
        def _():
            leaving_send[place] = low
            back_copy(place).start()

        @pl.when(place == me)
        def _():
            leavings[place] = low

        return mm(split(leaving), maps_in[place], NT) + shifts_in[place].astype(F32)

    lax.fori_loop(0, parts, scan, jnp.zeros((value_dim // units.share, key_dim), F32))
    arrive(0)

    def store_out(start, size, block):
        out_part[pl.ds(start, size), :] = block

    def store_first(start, size, block):
        first_part[pl.ds(start, size), :] = block

    weight_rows(gated, mixer_rows_grad[...].reshape(-1, width), store_out)
    weight_rows(normed, gate_grad[...].reshape(-1, values), store_first)
    rings[1].begin()
    arrive(1)

    def swiglu_out(s, carry):
        tools.send_part(0, s, raw(act[s], down_weight[...], NN))
        return carry

    lax.fori_loop(0, slots, swiglu_out, 0)
    rings[0].tick(0)

    def swiglu_core(s, carry):
        tools.join_core(0, s)
        return carry

    lax.fori_loop(0, slots, swiglu_core, 0)
    rings[1].tick(0)
    arrive(2)

    def delta_slot(s, carry):
        for i in range(heads * units.share):
            unit = s * heads * units.share + i

            @pl.when(unit != me)
            def _(unit=unit):
                back_arrival(unit).wait_recv()

        ext[0:RIM, :] = rim[s]
        ext[RIM : RIM + length, :] = pre[s].astype(F32)
        lane = lax.broadcasted_iota(jnp.int32, (length, LANES), 1)
        log_cols, strength_cols = gates_of(ab[s], lanes[0:1, :], lanes[1:2, :])
        log_rows, strength_rows = gates_of(abt[s], cols[0:8, 0:1], cols[8:16, 0:1])
        key_start = heads * key_dim
        value_start = 2 * heads * key_dim
        strict = row > col
        grads = jnp.zeros((length, LANES), F32)
        conv_grad[0:RIM, :] = jnp.zeros((RIM, conv_grad.shape[1]), F32)
        conv_grad[RIM + length : 2 * RIM + length, :] = jnp.zeros((RIM, conv_grad.shape[1]), F32)

        def activation(start, width):
            total = taps_ref[0:1, start : start + width] * ext[pl.ds(RIM - taps + 1, length), start : start + width]
            for tap in range(1, taps):
                total = total + (
                    taps_ref[tap : tap + 1, start : start + width]
                    * ext[pl.ds(RIM - taps + 1 + tap, length), start : start + width]
                )
            sig = sigmoid(total)
            return total * sig, sig * (1.0 + total * (1.0 - sig))

        def unit_back(grad, start, scale_by):
            act, slope = activation(start, key_dim)
            scale = lax.rsqrt(jnp.sum(act * act, axis=1, keepdims=True) + UNIT_EPSILON)
            inner = jnp.sum(act * grad, axis=1, keepdims=True)
            back = scale_by * scale * (grad - act * (scale * scale * inner))
            conv_grad[RIM : RIM + length, start : start + key_dim] = back * slope

        for h in range(heads):
            query, key, value = queries[s, h], keys[s, h], value_rows[s, h]
            query_f, key_f = query.astype(F32), key.astype(F32)
            strength = strength_cols[:, heads + h : heads + h + 1]
            cum_col, cum_row, end, decayed = decay_of(
                log_cols[:, h : h + 1], log_rows[h : h + 1, :], row, col
            )
            rise = jnp.exp(cum_col)
            end_weight = jnp.exp(end - cum_col)
            state = units.whole(states, s * heads + h)
            leaving = units.whole(leavings, s * heads + h)
            state_f, leaving_f = state.astype(F32), leaving.astype(F32)
            rows = split(delta_rows[s, h])
            out_grad = split(mixer_grad[s, h])
            products = mm(key, key, NT)
            scores = decayed * mm(query, key, NT)
            rows_grad = mm(split(scores), out_grad, TN) + end_weight * mm(key, leaving, NT)
            scores_grad = mm(out_grad, rows, NT)
            query_grad = rise * mm(out_grad, state)
            right_grad = mm(split(inverse_all[s, h]), split(rows_grad), TN)
            key_state = mm(key, state, NT)
            triangle_grad = -jnp.where(strict, mm(split(right_grad), rows, NT), 0.0)
            value_grad = strength * right_grad
            strength_grad = jnp.sum(right_grad * (value.astype(F32) - rise * key_state), axis=1, keepdims=True)
            read_grad = -rise * value_grad
            cum_grad = jnp.sum(read_grad * key_state, axis=1, keepdims=True)
            key_grad = mm(split(read_grad), state)
            decayed_grad = triangle_grad * decayed
            strength_grad = strength_grad + jnp.sum(decayed_grad * products, axis=1, keepdims=True)
            weighted = strength * decayed_grad
            both = weighted * products + scores_grad * scores
            products_grad = split(weighted)
            overlap_grad = split(scores_grad * decayed)
            cum_grad = cum_grad + jnp.sum(both, axis=1, keepdims=True) + jnp.sum(query_f * query_grad, axis=1, keepdims=True)
            query_grad = query_grad + mm(overlap_grad, key)
            key_grad = (
                key_grad + mm(overlap_grad, query, TN) + mm(products_grad, key) + mm(products_grad, key, TN)
            )
            moved = mm(rows, leaving)
            key_grad = key_grad + end_weight * moved
            end_part = jnp.sum(moved * key_f, axis=1, keepdims=True) * end_weight
            cum_grad = cum_grad - end_part
            last = jnp.sum(end_part, axis=0, keepdims=True) + jnp.exp(end) * jnp.sum(
                jnp.sum(leaving_f * state_f, axis=1, keepdims=True), axis=0, keepdims=True
            )
            turned = jnp.sum(jnp.where(row == col, cum_grad, 0.0), axis=0, keepdims=True)
            turned = turned - jnp.sum(both, axis=0, keepdims=True)
            log_grad = jnp.sum(jnp.where(row <= col, turned, 0.0), axis=1, keepdims=True) + last
            grads = jnp.where(lane == h, log_grad, grads)
            grads = jnp.where(lane == heads + h, strength_grad, grads)
            unit_back(query_grad, h * key_dim, key_dim ** (-0.5))
            unit_back(key_grad, key_start + h * key_dim, 1.0)
            if h == 0:
                rings[0].tick(s + 1)
            _, slope = activation(value_start + h * value_dim, value_dim)
            conv_grad[RIM : RIM + length, value_start + h * value_dim : value_start + (h + 1) * value_dim] = (
                value_grad * slope
            )

        softened = -lanes[0:1, :] * sigmoid(ab[s] + lanes[1:2, :])
        decay_part = grads * softened
        is_log = lane < heads
        ab_grad_out[s] = jnp.where(is_log, decay_part, grads * strength_cols * (1.0 - strength_cols))
        lane_grad_out[0:1, :] += jnp.sum(jnp.where(is_log, grads * log_cols, 0.0), axis=0, keepdims=True)
        lane_grad_out[1:2, :] += jnp.sum(jnp.where(is_log, decay_part, 0.0), axis=0, keepdims=True)
        main = conv_grad[RIM : RIM + length, :]
        pre_grad = jnp.zeros_like(main)
        rim_grad = jnp.zeros((RIM, conv_grad.shape[1]), F32)
        for tap in range(taps):
            weight = taps_ref[tap : tap + 1, :]
            taps_grad_out[tap : tap + 1, :] += jnp.sum(
                main * ext[pl.ds(RIM - taps + 1 + tap, length), :], axis=0, keepdims=True
            )
            pre_grad = pre_grad + weight * conv_grad[pl.ds(RIM + taps - 1 - tap, length), :]
            rim_grad = rim_grad + weight * conv_grad[pl.ds(taps - 1 - tap, RIM), :]
        pre_grad_out[s] = pre_grad.astype(BF16)
        tail[s] = pre_grad[length - 2 * RIM : length, :]
        rim_own[s] = rim_grad


        rings[1].tick(s + 1)
        block_out[s] = (residual[s] + mask[s][:, 0:1] * tools.join_line(0, s)).astype(BF16)
        return carry

    lax.fori_loop(0, slots, delta_slot, 0)
    rim_copy().start()

    def rest(k, carry):
        rings[0].tick(k)
        rings[1].tick(k)
        return carry

    lax.fori_loop(slots + 1, rings[0].ticks, rest, 0)
    rim_copy().wait_recv()
    inside = me < parts - 1
    for s in range(slots):
        late = jnp.where(inside, rim_in[s], 0.0)
        end = tail[s]
        shifted_in = jnp.concatenate([jnp.zeros_like(late), late], axis=0)
        pre_grad_out[s, length - 2 * RIM : length, :] = (end + shifted_in).astype(BF16)
    rim_copy().wait_send()

    def drain(away, carry):
        back_copy(lax.rem(me + away, parts)).wait_send()
        return carry

    lax.fori_loop(1, parts, drain, 0)

    def drain_head(s, carry):
        tools.drain(s)
        return carry

    lax.fori_loop(0, slots, drain_head, 0)
    rings[0].finish()
    rings[1].finish()


def backward_call(parts, head_parts, heads, *operands):
    (
        mixer_grad, shifts_in, gated, mixer_rows_grad, normed, gate_grad, act, down_weight, residual, mask,
        pre, rim, ab, abt, taps, lanes, cols,
        queries, keys, value_rows, inverse, delta_rows, states, maps_in, up_part, gate_part, down_part,
    ) = operands
    slots, length, channels = pre.shape
    value_dim, key_dim = value_rows.shape[3], keys.shape[3]
    width, shard = normed.shape[2], residual.shape[2]
    sds = jax.ShapeDtypeStruct
    dma = pltpu.SemaphoreType.DMA
    out_shape = (padded_rows(gated.shape[2], parts), width)
    first_shape = (width, gate_grad.shape[2])
    outs = (
        sds(residual.shape, BF16), sds(pre.shape, BF16), sds(ab.shape, F32), sds((8, channels), F32),
        sds((8, LANES), F32), sds(up_part.shape, BF16), sds(gate_part.shape, BF16), sds(down_part.shape, BF16),
        sds(out_shape, BF16), sds(first_shape, BF16),
    )
    unit = pltpu.VMEM(states.shape, BF16)
    edge = pltpu.VMEM((slots, RIM, channels), F32)
    scratch = ([
        pltpu.VMEM(out_shape, BF16), pltpu.VMEM(first_shape, BF16),
        pltpu.VMEM((length + RIM, channels), F32), pltpu.VMEM((length + 2 * RIM, channels), F32),
        pltpu.VMEM((slots, 2 * RIM, channels), F32), edge, edge, unit, unit,
        dma((parts - 1,)), dma((parts - 1,)), dma((1,)), dma((1,)),
    ]
    + ring_scratch(parts, [up_part.shape, gate_part.shape])
    + ring_scratch(parts, [down_part.shape, out_shape, first_shape])
    + head_scratch(1, 1, slots, head_parts, length, shard))
    return staged_call(
        functools.partial(backward_kernel, slots, heads, key_dim, value_dim, parts, head_parts),
        operands, outs, scratch, 3,
        late=((2, 3, 4, 5, 26), (6, 7), (0, 8, 9, 10, 11, 12, 13, 17, 18, 19, 20, 21, 22)),
        kept=(5, 6, 7, 8, 9), flops=5 * 10**10,
    )


def last_kernel(
    slots, head_parts, heads, parts, taps, arrive, leave,
    pre_grad, gate_grad, ab_grad, normed, query_weight, key_weight, value_weight, gate_weight, ab_weight, x_shard, inv_first,
    residual_grad, input_gain, gain_part, taps_grad, lane_grad, mixed_part,
    input_grad_out, unit_sum, value_sum, small_sum,
    unit_own, value_own, small_own, small_in, gain_own, gain_in, first_shard,
    small_send, small_recv, gain_send, gain_recv, *refs,
):
    head_refs = refs[12:]
    tools = head_tools(head_parts, head_refs, 1)
    rings = (
        ring_tools(parts, (unit_own,), (unit_sum,), refs[0:1], *refs[1:6]),
        ring_tools(parts, (value_own,), (value_sum,), refs[6:7], *refs[7:12]),
    )
    me, place = tools.me, tools.place
    length, shard = x_shard.shape[1], x_shard.shape[2]
    width = shard * head_parts
    channels = pre_grad.shape[2]
    unit_wide = unit_own.shape[1]
    barrier = pltpu.get_barrier_semaphore()
    tools.greet(barrier)

    def greet(away, carry):
        pl.semaphore_signal(
            barrier, inc=1, device_id=(lax.rem(place + away, parts), me), device_id_type=MESH
        )
        return carry

    lax.fori_loop(1, parts, greet, 0)

    def gain_copy(away):
        return remote(
            gain_own, gain_in.at[away - 1], gain_send.at[away - 1], gain_recv.at[away - 1],
            (place, lax.rem(me + away, head_parts)),
        )

    def small_copy(away):
        return remote(
            small_own, small_in.at[away - 1], small_send.at[away - 1], small_recv.at[away - 1],
            (lax.rem(place + away, parts), me),
        )

    def store_unit(start, size, block):
        unit_own[pl.ds(start, size), :] = block

    def store_value(start, size, block):
        value_own[pl.ds(start, size), :] = block

    weight_rows(normed, pre_grad[:, :, :unit_wide].reshape(-1, unit_wide), store_unit)
    pl.semaphore_wait(barrier, head_parts - 1 + parts - 1)
    rings[0].begin()
    weight_rows(normed, pre_grad[:, :, unit_wide:].reshape(-1, channels - unit_wide), store_value)
    rings[1].begin()
    def products(s, carry):
        low = ab_grad[s].astype(BF16)
        half = unit_wide // 2
        tools.send_part(
            0, s,
            raw(pre_grad[s, :, :half], query_weight[...], NT)
            + raw(pre_grad[s, :, half:unit_wide], key_weight[...], NT)
            + raw(pre_grad[s, :, unit_wide:], value_weight[...], NT)
            + raw(gate_grad[s], gate_weight[...], NT)
            + raw(low, ab_weight[...], NT),
        )
        rings[0].tick(s)
        rings[1].tick(s)
        return carry

    arrive(0)
    lax.fori_loop(0, slots, products, 0)
    arrive(1)

    def first_join(s, carry):
        tools.join_core(0, s)
        return carry

    lax.fori_loop(0, slots, first_join, 0)
    rings[0].tick(slots)
    rings[1].tick(slots)
    small_own[...] = jnp.zeros_like(small_own)
    gain_own[...] = gain_part[...]
    for away in range(1, head_parts):
        gain_copy(away).start()

    def second_join(s, carry):
        grad = tools.join_line(0, s)
        x = x_shard[s].astype(F32)
        inv = inv_first[s][:, 0:1]
        weighted = grad * input_gain[0:1, :]
        first_shard[s] = weighted
        tools.send_stat(0, s, jnp.sum(weighted * x, axis=1, keepdims=True))
        return carry + jnp.sum(grad * x * inv, axis=0, keepdims=True)

    gain_line = lax.fori_loop(0, slots, second_join, jnp.zeros((1, shard), F32))
    rings[0].tick(slots + 1)
    rings[1].tick(slots + 1)

    def input_rows(s, carry):
        stat = tools.join_stat(0, s) / width
        inv = inv_first[s][:, 0:1]
        input_grad_out[s] = residual_grad[s] + inv * (
            first_shard[s] - x_shard[s].astype(F32) * (inv * inv * stat)
        )
        return carry

    lax.fori_loop(0, slots, input_rows, 0)
    gain_total = gain_own[...]
    for away in range(1, head_parts):
        gain_copy(away).wait_recv()
        gain_total = gain_total + gain_in[away - 1]
    low = ab_grad[...].astype(BF16).reshape(-1, LANES)
    ab_lines = raw(low, normed[...].reshape(-1, width), TN)
    at = 0
    for lines in [taps_grad[t : t + 1, :] for t in range(taps)] + [
        ab_lines[t : t + 1, :] for t in range(2 * heads)
    ] + [gain_total[0:1, :], lane_grad[0:1, :], lane_grad[1:2, :], mixed_part[0:1, :], gain_line]:
        for j in range(lines.shape[1] // LANES):
            small_own[at : at + 1, :] = lines[:, j * LANES : (j + 1) * LANES]
            at += 1

    def small_start(away, carry):
        small_copy(away).start()
        return carry

    lax.fori_loop(1, parts, small_start, 0)

    def rest(k, carry):
        rings[0].tick(k)
        rings[1].tick(k)
        return carry

    lax.fori_loop(slots + 2, rings[0].ticks, rest, 0)
    small_sum[...] = small_own[...]

    def small_join(away, carry):
        small_copy(away).wait_recv()
        small_sum[...] += small_in[away - 1]
        small_copy(away).wait_send()
        return carry

    lax.fori_loop(1, parts, small_join, 0)
    for away in range(1, head_parts):
        gain_copy(away).wait_send()

    def drain(s, carry):
        tools.drain(s)
        return carry

    lax.fori_loop(0, slots, drain, 0)
    rings[0].finish()
    rings[1].finish()


def last_call(
    parts, head_parts, heads, taps, unit_wide, pre_grad, gate_grad, ab_grad, normed, query_weight, key_weight, value_weight, gate_weight, ab_weight,
    x_shard, inv_first, residual_grad, input_gain, gain_part, taps_grad, lane_grad, mixed_part,
):
    slots, length, shard = x_shard.shape
    width = shard * head_parts
    channels = pre_grad.shape[2]
    lines = (taps * channels + 2 * heads * width + gain_part.shape[1] + 2 * shard) // LANES + 2
    lines += -lines % 8
    sds = jax.ShapeDtypeStruct
    dma = pltpu.SemaphoreType.DMA
    operands = (
        pre_grad, gate_grad, ab_grad, normed, query_weight, key_weight, value_weight, gate_weight, ab_weight, x_shard, inv_first,
        residual_grad, input_gain, gain_part, taps_grad, lane_grad, mixed_part,
    )
    first, second = (width, unit_wide), (width, channels - unit_wide)
    outs = (sds((slots, length, shard), F32), sds(first, BF16), sds(second, BF16), sds((lines, LANES), F32))
    scratch = ([
        pltpu.VMEM(first, BF16), pltpu.VMEM(second, BF16), pltpu.VMEM((lines, LANES), F32), pltpu.VMEM((parts - 1, lines, LANES), F32),
        pltpu.VMEM(gain_part.shape, F32), pltpu.VMEM((head_parts - 1,) + gain_part.shape, F32),
        pltpu.VMEM((slots, length, shard), F32),
        dma((parts - 1,)), dma((parts - 1,)), dma((head_parts - 1,)), dma((head_parts - 1,)),
    ]
    + ring_scratch(parts, [first])
    + ring_scratch(parts, [second])
    + head_scratch(1, 1, slots, head_parts, length, shard))
    return staged_call(
        functools.partial(last_kernel, slots, head_parts, heads, parts, taps),
        operands, outs, scratch, 4, late=((4, 5, 6, 7, 8, 2, 1), (9, 10, 11, 12, 13, 14, 15, 16)),
        kept=(1, 2), flops=5 * 10**10,
    )


def per_device(
    hidden_in, lengths, input_gain, query_weight, key_weight, value_weight, alpha_weight, beta_weight,
    decay_log, decay_bias, query_kernel, key_kernel, value_kernel, gate_weight, output_gain,
    output_weight, mixed_gain, swiglu_gate, swiglu_up, swiglu_down, cotangent,
):
    slots, segment, width = hidden_in.shape
    heads = decay_log.shape[0]
    key_dim = query_kernel.shape[1] // heads
    value_dim = value_kernel.shape[1] // heads
    taps = query_kernel.shape[0]
    split_key = heads * key_dim
    channels = 2 * split_key + heads * value_dim
    head_parts = lax.axis_size("head")
    seq_parts = lax.axis_size("seq")
    shard = width // head_parts
    head_start = lax.axis_index("head") * shard

    position = lax.axis_index("seq") * segment + jnp.arange(segment)
    mask = (position[None, :] < lengths[:, None]).astype(F32)[:, :, None]
    lane_mask = jnp.broadcast_to(mask, (slots, segment, LANES))
    ab_weight = jnp.concatenate(
        [alpha_weight, beta_weight, jnp.zeros((width, LANES - 2 * heads), BF16)], axis=1
    )
    kernel = jnp.concatenate([query_kernel, key_kernel, value_kernel], axis=1).astype(F32)
    kernel = jnp.pad(kernel, ((0, 8 - taps), (0, 0)))
    rate = jnp.exp(decay_log)
    pad_heads = lambda v: jnp.pad(v, (0, LANES - heads))
    lane_gates = jnp.pad(jnp.stack([pad_heads(rate), pad_heads(decay_bias)]), ((0, 6), (0, 0)))
    pad_rows = lambda v: jnp.broadcast_to(jnp.pad(v, (0, 8 - heads))[:, None], (8, LANES))
    col_gates = jnp.concatenate([pad_rows(rate), pad_rows(decay_bias)], axis=0)
    gain_row = jnp.broadcast_to(output_gain[None, :], (8, value_dim))

    (
        query, key, value, inverse, eff, delta_rows, mixer, gated, normed_first, pre_all, gate_pre, x_low,
        inv_first, rim_pre, ab_pre, ab_rows, states, maps_in,
    ) = forward_call(
        seq_parts, head_parts, heads, hidden_in, jnp.broadcast_to(input_gain[None, :], (8, width)),
        query_weight, key_weight, value_weight, gate_weight, ab_weight, kernel, lane_gates, col_gates, gain_row,
    )
    (
        residual, activation, up_part, gate_part, down_part, residual_grad, mixer_rows_grad, mixer_grad,
        gate_grad, mixed_part, gain_part, shifts_in,
    ) = middle_call(
        seq_parts, head_parts, heads, gated, x_low, cotangent, lane_mask, output_weight, swiglu_gate.T,
        swiglu_up.T, swiglu_down, jnp.broadcast_to(mixed_gain[None, :], (8, shard)), mixer, gate_pre, gain_row, eff,
    )
    (
        block_out, pre_grad, ab_grad, taps_grad, lane_grad, up_sum, gate_sum, down_sum, out_sum, gate_first_sum
    ) = backward_call(
        seq_parts, head_parts, heads, mixer_grad, shifts_in, gated, mixer_rows_grad, normed_first, gate_grad,
        activation, swiglu_down, residual, lane_mask, pre_all, rim_pre, ab_pre, ab_rows, kernel, lane_gates,
        col_gates, query, key, value, inverse, delta_rows, states, maps_in, up_part, gate_part, down_part,
    )
    gain_shard = lax.dynamic_slice_in_dim(input_gain, head_start, shard, 0)
    input_grad, unit_sum, value_sum, small_sum = last_call(
        seq_parts, head_parts, heads, taps, 2 * split_key, pre_grad, gate_grad, ab_grad,
        normed_first, query_weight, key_weight, value_weight, gate_weight, ab_weight, x_low,
        inv_first, residual_grad,
        jnp.broadcast_to(gain_shard[None, :], (8, shard)), gain_part, taps_grad, lane_grad, mixed_part,
    )
    hidden = swiglu_gate.shape[1]
    flat_small = small_sum.reshape(-1)
    pieces, at = [], 0
    for size in (taps * channels, 2 * heads * width, value_dim, LANES, LANES, shard, shard):
        pieces.append(flat_small[at : at + size])
        at += size
    taps_sum = pieces[0].reshape(taps, channels)
    ab_sum = pieces[1].reshape(2 * heads, width).T
    value_share = value_dim // head_parts
    output_gain_grad = lax.dynamic_slice_in_dim(
        pieces[2], lax.axis_index("head") * value_share, value_share, 0
    )
    return (
        block_out,
        input_grad,
        pieces[6],
        unit_sum[:, :split_key].astype(F32),
        unit_sum[:, split_key:].astype(F32),
        value_sum.astype(F32),
        ab_sum[:, :heads],
        ab_sum[:, heads:],
        pieces[3][:heads],
        pieces[4][:heads],
        taps_sum[:, :split_key],
        taps_sum[:, split_key : 2 * split_key],
        taps_sum[:, 2 * split_key :],
        gate_first_sum.astype(F32),
        output_gain_grad,
        out_sum[: heads * value_dim].astype(F32),
        pieces[5],
        gate_sum[:hidden].astype(F32).T,
        up_sum[:hidden].astype(F32).T,
        down_sum[:hidden].astype(F32),
    )


def solution(mesh):
    seq, cols, lines = P(None, "seq", None), P(None, "head"), P("head", None)
    one = P("head")
    placed = (
        seq, P(), P(), cols, cols, cols, cols, cols, one, one, cols, cols, cols, cols, P(), lines, one,
        cols, cols, lines, seq,
    )
    both = P(None, "seq", "head")
    return jax.shard_map(
        per_device,
        mesh=mesh,
        in_specs=placed,
        out_specs=(
            both, both, one, cols, cols, cols, cols, cols, one, one, cols, cols, cols, cols, one, lines,
            one, cols, cols, lines,
        ),
        check_vma=False,
    )
```

time: 591 us -> 412 us (0.70); the launches traced: 581 us -> 412 us
  matrix products: 52.9 us -> 0 us
  Pallas kernels: 336 us -> 380 us
  local copies, waits for them, and re-layouts: 50.4 us -> 14.7 us
  starting transfers between devices: 30.1 us -> 0 us
  other arithmetic: 45.7 us -> 17 us
  blocking collectives: 26.2 us -> 0 us
  waiting for transfers between devices: 24.5 us -> 0 us
  between operations: 15.1 us -> 0.76 us
    dot_general x28 -> x0, matrix products: 52.9 us -> none  [the longest x6 19.4 us: weight_grad(): lax.dot_general(left, right, TN, preferred_element_type=F32).astype(BF16)]
    pallas_call x6 -> x4, Pallas kernels: 336 us -> 380 us  [staged_call(): pl.pallas_call(body, in_specs=[free if i in late_set else vmem for i in r...]
    psum x2 -> x0, blocking collectives: 26.2 us -> none  [the longest x1 20.4 us: per_device(): input_gain_sum = lax.psum(input_gain_grad, 'seq')]
    all_to_all x5 -> x0, waiting for transfers between devices: 23.6 us -> none  [exchange(): return lax.all_to_all(parts, axis, 0, 0, tiled=True)]
    all_to_all x5 -> x0, starting transfers between devices: 23.5 us -> none  [exchange(): return lax.all_to_all(parts, axis, 0, 0, tiled=True)]
    unnamed x85 -> x26, local copies, waits for them, and re-layouts: 17.3 us -> 3.59 us
    slice x11 -> x3, local copies, waits for them, and re-layouts: 14 us -> 1.09 us  [the longest x2 0.57 us: per_device(): pieces.append(flat_small[at:at + size])]
    concatenate x3 -> x1, other arithmetic: 9.29 us -> 0.87 us  [per_device(): jnp.concatenate([alpha_weight, beta_weight, jnp.zeros((width, LANES - 2 *...]
  transfers between devices with their start and end apart: 8 -> 0, of which waited for: 5 -> 0; matrix products, arithmetic and copies ran while one was open for 17% -> 0% of each run, Pallas kernels for 30% -> 0%
where the time goes in v3:
time: 412 us
  Pallas kernels  380 us (92%)
  other arithmetic  17 us (4%)
  local copies, waits for them, and re-layouts  14.7 us (4%)
    pallas_call x4, Pallas kernels, staged_call(): pl.pallas_call(body, in_specs=[free if i in late_set else vmem for i in r...  380 us

profile of v3, /device:TPU:0, one launch (start us, length us, event | category | flops | bytes accessed | tf_op | source)
XLA Modules:
  0.0 412.0 jit_solution(3615329437425629)
XLA Ops:
  0.7 0.7 exp.3
  1.3 0.7 pad_bitcast_fusion
  2.0 0.6 select_maximum_fusion.refs_8_.refs_15_
  2.6 0.7 fusion.6
  3.3 0.7 broadcast.44.refs_9_.refs_16_
  4.0 0.9 copy.41
  4.9 0.9 copy.42
  5.8 0.1 pad.40.clone
  5.9 0.9 maximum_maximum_fusion.refs_6_.refs_8_
  6.7 1.3 fusion.5.refs_7_.refs_14_
  8.1 1.3 broadcast_in_dim.20.refs_10_.refs_11_
  9.3 1.3 broadcast_in_dim.16.refs_1_
  10.6 61.7 %shard_map.356 = (bf16[4,2,256,128]{3,2,1,0:T(8,128)(2,1)}, bf16[4,2,256,128]{3,2,1,0:T(8,128)(2,1)}, bf16[4,2,256,256]{3,2,1,0:T(8,128)(2,1)}, f32[4,2,256,256]...) custom-call(bf16[4,256,1024]{2,1,0:T(8,128)(2,1)} %refs_0_.1, ...), custom_call_target="tpu_custom_call" | custom-call | flops 10000000000 | bytes 60000000 | tf_op jit(solution)/shard_map/pallas_call | solution.py:173
  72.3 0.0 copy-done.10
  72.3 0.1 compare_convert_fusion
  72.4 1.0 broadcast_in_dim.21.refs_3_.refs_9_
  73.4 0.0 copy-done.9
  73.4 0.6 broadcast_in_dim.22.refs_8_
  74.0 86.0 %shard_map.357 = (f32[4,256,256]{2,1,0:T(8,128)}, bf16[4,256,704]{2,1,0:T(8,128)(2,1)}, bf16[768,1024]{1,0:T(8,128)(2,1)}, bf16[768,1024]{1,0:T(8,128)(2,1)}, bf...) custom-call(bf16[4,256,512]{2,1,0:T(8,128)(2,1)} %get-tuple-element., ...), custom_call_target="tpu_custom_call" | custom-call | flops 10000000000 | bytes 60000000 | tf_op jit(solution)/shard_map/pallas_call | solution.py:173
  160.0 156.5 %shard_map.358 = (bf16[4,256,256]{2,1,0:T(8,128)(2,1)}, bf16[4,256,1024]{2,1,0:T(8,128)(2,1)}, f32[4,256,128]{2,1,0:T(8,128)}, f32[8,1024]{1,0:T(8,128)}, f32[8,...) custom-call(f32[4,2,256,256]{3,2,1,0:T(8,128)} %get-tuple-element.69, ...), custom_call_target="tpu_custom_call" | custom-call | flops 49999998976 | bytes 60000000 | tf_op jit(solution)/shard_map/pallas_call | solution.py:173
  316.5 0.8 dynamic_slice.6
  317.3 0.6 broadcast_in_dim.23.refs_12_
  317.9 75.4 %shard_map.359 = (f32[4,256,256]{2,1,0:T(8,128)}, bf16[1024,512]{1,0:T(8,128)(2,1)}, bf16[1024,512]{1,0:T(8,128)(2,1)}, f32[72,128]{1,0:T(8,128)}) custom-call(bf16[4,256,1024]{2,1,0:T(8,128)(2,1)} %get-tuple-element.91.refs_0_, bf16[4,256,512]{2,1,0:T(8,128)(2,1)} %get-tuple-element.73.refs_5_.refs_1_, f32[4,256,128]{2,1,0:T(8,128)} %get-tuple-element.92.refs_2_, ...), custom_call_target="tpu_custom_call" | custom-call | flops 49999998976 | bytes 60000000 | tf_op jit(solution)/shard_map/pallas_call | solution.py:173
  393.3 0.0 copy-start.5
  393.3 2.8 slice_convert_fusion.1
  396.1 0.0 copy-done.5
  396.1 1.6 convert_element_type.41
  397.7 0.0 copy-done.8
  397.7 0.6 fusion.9
  398.3 0.6 fusion.8
  398.9 0.6 slice.100
  399.5 0.6 slice_bitcast_fusion
  400.1 0.6 dynamic_slice.7
  400.7 0.5 slice_bitcast_fusion.3
  401.2 0.0 copy-done.2
  401.2 1.9 convert_bitcast_fusion
  403.1 0.0 copy-done.1
  403.1 1.9 convert_bitcast_fusion.1
  405.1 0.0 copy-done
  405.1 1.9 slice_convert_fusion
  407.0 0.0 copy-done.4
  407.0 1.6 convert_element_type.42
  408.6 0.0 copy-done.3
  408.6 1.6 convert_element_type.43
  410.2 0.0 copy-done.7
  410.2 0.8 copy.45
  411.0 0.0 copy-done.6
  411.0 1.0 copy.46
  (15 shorter events, 0.1 us)
Async XLA Ops:
  10.6 61.7 %copy-start.10 = (s32[4]{0:T(128)S(1)}, s32[4]{0:T(128)}, u32[]{:S(2)}) copy-start(s32[4]{0:T(128)} %param.22) | copy-start | bytes 52
  10.6 62.8 %copy-start.9 = (f32[256]{0:T(256)S(1)}, f32[256]{0:T(256)}, u32[]{:S(2)}) copy-start(f32[256]{0:T(256)} %param.37) | copy-start | bytes 3076
  393.3 2.8 copy-start.5
  396.0 1.6 copy-start.8
  396.0 5.1 %copy-start.2 = (bf16[768,1024]{1,0:T(8,128)(2,1)S(1)}, bf16[768,1024]{1,0:T(8,128)(2,1)}, u32[]{:S(2)}) copy-start(bf16[768,1024]{1,0:T(8,128)(2,1)} %get-tuple-element.106) | copy-start | bytes 4718596
  401.2 1.9 copy-start.1
  403.1 1.9 copy-start
  405.1 1.9 copy-start.4
  407.0 1.6 copy-start.3
  408.6 1.6 copy-start.7
  408.6 2.4 copy-start.6
